TPU v7x, 32 devices: a whole 2x2x4 slice. The times are simulated.
32 devices in a mesh: grp: 16 (over z, y, x), row: 2 (over core).
Axes of the slice: x: 2, y: 2, z: 4, core: 2. Of those that a mesh axis runs over, the one named last changes fastest.
Arguments:
- latents: bfloat16 [16, 4096], P('grp'), may hold values from -6 to 6
- frames: int32 [16], replicated, may hold values from 1 to 4, as said below
- offsets: int32 [16], replicated, may hold values from 0 to 240, as said below
- assign: int32 [16], replicated, may hold values from 0 to 15, each once
- w_in: bfloat16 [16, 27, 384], replicated, may hold values from -0.3125 to 0.3125
- w_mid: bfloat16 [384, 27, 192], P('grp'), may hold values from -0.0625 to 0.0625
- w_out: bfloat16 [192, 27, 96], P('grp'), may hold values from -0.078125 to 0.078125
- gain_in: float32 [384], replicated, may hold values from 0.25 to 1.75
- gain_mid: float32 [192], replicated, may hold values from 0.25 to 1.75
- gain_out: float32 [96], replicated, may hold values from 0.25 to 1.75
Outputs:
- decoded: bfloat16 [16, 4, 16, 6144], P('grp', None, 'row')
Inputs may be any that keep to these rules, and one draw needn't show every extreme that they name: Some request has exactly 4 frames. The blocks of different requests do not intersect, and offsets[r] + 16 <= 256 for every request; some request starts at 240. `assign`: every request is decoded by exactly one group.
All inputs are finite; a program needn't handle non-finite values.
Results may differ from a plain program's by a relative error of at most 0.006.
Values may be sent and summed in bfloat16 or wider, within the bound.
No kernel may reach another device: no remote copies, remote signals or barrier semaphores. Data moves between devices by JAX's collectives and lax.ppermute only.
A program may use at most 128 MiB of HBM per device.

v0:
```python
import jax
import jax.numpy as jnp
from jax import lax
from jax.sharding import PartitionSpec as P

RL = 2
WL = 16
FMAX = 4


def extended_2(cells, sides, width):
    for axis, dim in sides:
        count = lax.axis_size(axis)
        ends = count - 1
        head = lax.slice_in_dim(cells, 0, width, axis=dim)
        tail = lax.slice_in_dim(cells, cells.shape[dim] - width, cells.shape[dim], axis=dim)
        cells = jnp.concatenate(
            [
                lax.ppermute(tail, axis, [(i, (i + 1) % count) for i in range(ends)]),
                cells,
                lax.ppermute(head, axis, [((i + 1) % count, i) for i in range(ends)]),
            ],
            axis=dim,
        )
    return cells


def rms_silu(hidden, gain):
    mean_sq = jnp.mean(hidden * hidden, axis=-1, keepdims=True)
    scaled = hidden * lax.rsqrt(mean_sq + 1e-06) * gain
    return jax.nn.silu(scaled)


def causal_conv(extended, weight):
    count_t = extended.shape[0]
    count_r = extended.shape[1] - 2
    count_c = extended.shape[2]
    width_in = extended.shape[3]
    width_out = weight.shape[2]
    padded = jnp.pad(extended, ((2, 0), (0, 0), (1, 1), (0, 0)))
    total = jnp.zeros((count_t * count_r * count_c, width_out), jnp.float32)
    for time_tap in range(3):
        for row_tap in range(3):
            for col_tap in range(3):
                window = padded[
                    time_tap : time_tap + count_t,
                    row_tap : row_tap + count_r,
                    col_tap : col_tap + count_c,
                ]
                window = window.reshape(count_t * count_r * count_c, width_in)
                tap_index = 9 * time_tap + 3 * row_tap + col_tap
                total = total + jnp.dot(
                    window, weight[:, tap_index, :], preferred_element_type=jnp.float32
                )
    return total.reshape(count_t, count_r, count_c, width_out)


def upsample(values):
    return jnp.repeat(jnp.repeat(values, 2, axis=1), 2, axis=2)


def per_device(latents, frames, offsets, assign, w_in, w_mid, w_out, gain_in, gain_mid, gain_out):
    groups = lax.axis_size("grp")
    row_count = lax.axis_size("row")
    row_index = lax.axis_index("row")
    group_index = lax.axis_index("grp")
    channels = w_in.shape[0]
    cap_vals = latents.shape[1] // groups
    cap_tokens = cap_vals // channels
    span_len = cap_tokens // FMAX
    flat = latents[0]
    slot_ids = jnp.arange(cap_vals, dtype=jnp.int32)

    def select_span(request):
        start = offsets[request] * channels
        block = lax.dynamic_slice_in_dim(flat, start, cap_vals)
        keep = slot_ids < frames[request] * span_len * channels
        return jnp.where(keep, block, jnp.zeros((), block.dtype))

    outgoing = jax.vmap(select_span)(assign)
    incoming = lax.all_to_all(outgoing, "grp", split_axis=0, concat_axis=0, tiled=True)
    table = incoming.reshape(groups * cap_tokens, channels)
    request = assign[group_index]
    count = frames[request]
    fill_len = count * span_len
    image_rows = RL * row_count
    frame_ids = jnp.arange(FMAX, dtype=jnp.int32)[:, None, None]
    row_ids = row_index * RL + jnp.arange(RL, dtype=jnp.int32)[None, :, None]
    col_ids = jnp.arange(WL, dtype=jnp.int32)[None, None, :]
    position = (frame_ids * image_rows + row_ids) * WL + col_ids
    shard = jnp.minimum(position // fill_len, groups - 1)
    within = position % fill_len
    tokens = table[shard * cap_tokens + within]
    valid = (frame_ids < count)[..., None]
    latent_in = jnp.where(valid, tokens, jnp.zeros((), tokens.dtype))
    full_mid, full_out = (
        lax.all_gather(w_mid, "grp", axis=0, tiled=True),
        lax.all_gather(w_out, "grp", axis=0, tiled=True),
    )
    latent_ext = extended_2(latent_in, (("row", 1),), 1)
    act_in = rms_silu(causal_conv(latent_ext, w_in), gain_in).astype(jnp.bfloat16)
    mid_ext = extended_2(upsample(act_in), (("row", 1),), 1)
    act_mid = rms_silu(causal_conv(mid_ext, full_mid), gain_mid).astype(jnp.bfloat16)
    out_ext = extended_2(upsample(act_mid), (("row", 1),), 1)
    final = rms_silu(causal_conv(out_ext, full_out), gain_out)
    final = jnp.where(valid, final, jnp.zeros((), jnp.float32)).astype(jnp.bfloat16)
    return final.reshape(1, FMAX, 4 * RL, 4 * WL * final.shape[3])


def solution(mesh):
    placed = (
        P("grp", None),
        P(),
        P(),
        P(),
        P(),
        P("grp", None, None),
        P("grp", None, None),
        P(),
        P(),
        P(),
    )
    return jax.shard_map(
        per_device,
        mesh=mesh,
        in_specs=placed,
        out_specs=P("grp", None, "row", None),
        check_vma=False,
    )
```

profile of v0, /device:TPU:0, one launch (start us, length us, event | category | flops | bytes accessed | tf_op | source)
XLA Modules:
  0.0 204.2 jit_solution(9359900438937594989)
XLA Ops:
  8.6 1.3 gather_fusion
  9.9 0.8 reduce.3
  10.7 22.6 %while.1 = (s32[]{:T(128)}, bf16[4096]{0:T(1024)(128)(2,1)S(1)}, s32[16,1]{0,1:T(1,128)S(1)}, bf16[16,256]{1,0:T(8,128)(2,1)S(1)}, s32[]{:T(128)}, /*index=5*/s32[]{:T(128)}) while((s32[]{:T(128)}, bf16[4096]{0:T(1024)(128)(2,1)S(1)}, s32[16,1]{0,1:T(1,128)S(1)}, bf16[16,256]{1,0:T(8,128)(2,1)S(1)}, s32[]{:T(128)}, /*index=5*/s32[]{:T(128)}) %tuple.116), condition=%wide.while_cond, body=%wide.while_body.sunk | while | flops 2 | bytes 3169 | solution.py:76
  11.4 0.7 dynamic-slice.7
  12.8 0.7 dynamic-slice.7
  14.2 0.7 dynamic-slice.7
  15.6 0.7 dynamic-slice.7
  17.0 0.7 dynamic-slice.7
  18.4 0.7 dynamic-slice.7
  19.8 0.7 dynamic-slice.7
  21.2 0.7 dynamic-slice.7
  22.7 0.7 dynamic-slice.7
  24.1 0.7 dynamic-slice.7
  25.5 0.7 dynamic-slice.7
  26.9 0.7 dynamic-slice.7
  28.3 0.7 dynamic-slice.7
  29.7 0.7 dynamic-slice.7
  31.1 0.7 dynamic-slice.7
  32.5 0.7 dynamic-slice.7
  35.1 8.3 %all-to-all-start = ((bf16[16,2,128]{2,1,0:T(2,128)(2,1)}), bf16[16,2,128]{2,1,0:T(2,128)(2,1)S(1)}, u32[]{:S(2)}, u32[]{:S(2)}) async-start(bf16[16,2,128]{2,1,0:T(2,128)(2,1)} %reshape.702), calls=%async_computation | async-start | bytes 16384 | tf_op jit(solution)/shard_map/all_to_all | solution.py:81
  43.5 1.3 dynamic_slice.6
  46.7 1.3 dynamic_slice.7
  49.9 0.8 all-to-all-done
  50.9 0.7 gather_fusion.2
  51.7 1.3 collective-permute-start
  53.0 1.3 collective-permute-start.1
  54.3 67.8 %all_gather.7 = bf16[192,27,96]{2,1,0:T(8,128)(2,1)S(1)} all-gather(bf16[12,27,96]{2,1,0:T(8,128)(2,1)} %param.16), channel_id=1, replica_groups=mesh['grp'=16,'row'=2] {'grp'}, dimensions={0}, use_global_device_ids=true | all-gather | bytes 1057536 | tf_op jit(solution)/shard_map/all_gather | solution.py:98
  127.2 1.3 collective-permute-start.2
  128.5 1.5 collective-permute-start.3
  130.0 2.8 %fusion.103 = (bf16[192,1,96]{2,1,0:T(2,128)(2,1)}, bf16[192,1,96]{2,1,0:T(2,128)(2,1)}, bf16[192,1,96]{2,1,0:T(2,128)(2,1)}, bf16[192,1,96]{2,1,0:T(2,128)(2,1)...) fusion(bf16[192,27,96]{2,1,0:T(8,128)(2,1)S(1)} %all_gather.7), kind=kLoop, calls=%fused_computation.271 | loop fusion | bytes 1400832 | tf_op jit(solution)/shard_map/slice | solution.py:53
  133.4 1.4 fusion.106
  134.8 3.4 %fusion.105 = (bf16[4,4,32,384]{3,2,1,0:T(8,128)(2,1)S(1)}, bf16[4,4,32,384]{3,2,1,0:T(8,128)(2,1)}, bf16[4,4,32,384]{3,2,1,0:T(8,128)(2,1)}, bf16[4,4,32,384]{3...) fusion(bf16[6,6,34,384]{3,2,1,0:T(8,128)(2,1)S(1)} %fusion.23), kind=kLoop, calls=%fused_computation.273 | loop fusion | bytes 14942208 | tf_op jit(solution)/shard_map/slice | solution.py:45
  138.2 1.5 fusion.33
  139.7 1.7 fusion.31
  141.5 1.4 fusion.32
  142.9 1.3 convolution_add_fusion.47
  144.2 1.4 convolution_add_fusion.46
  145.7 1.4 convolution_add_fusion.45
  154.5 1.8 broadcast_in_dim.66
  156.3 2.1 %reshape.625 = bf16[4,8,64,192]{3,2,1,0:T(8,128)(2,1)S(1)} reshape(bf16[4,8,32,2,192]{4,3,2,1,0:T(2,128)(2,1)} %broadcast_in_dim.66) | data formatting | bytes 1572864 | tf_op jit(solution)/shard_map/reshape | solution.py:59
  159.1 3.0 %collective-permute-start.4 = (bf16[4,1,64,192]{3,2,1,0:T(8,128)(2,1)}, bf16[4,1,64,192]{3,2,1,0:T(8,128)(2,1)S(1)}, u32[]{:S(2)}, u32[]{:S(2)}) collective-permute-start(bf16[4,1,64,192]{3,2,1,0:T(8,128)(2,1)} %get-tuple-element.98), channel_id=1, source_target_pairs={{0,1},{2,3},{4,5},{6,7},{8,9},{10,11},{12,13},{14,15},{16,17},{18,... | collective-permute-start | bytes 294920 | tf_op jit(solution)/shard_map/ppermute | solution.py:19
  162.1 1.5 collective-permute-start.5
  163.6 1.3 fusion.104
  165.0 2.8 %reshape.648 = bf16[2048,192]{1,0:T(8,128)(2,1)} reshape(bf16[4,8,32,2,192]{4,3,2,1,0:T(2,128)(2,1)} %broadcast_in_dim.66) | data formatting | bytes 1572864 | tf_op jit(solution)/shard_map/reshape | solution.py:50
  167.9 2.0 fusion.9
  169.9 3.1 %fusion.102 = (bf16[4,8,64,192]{3,2,1,0:T(8,128)(2,1)}, bf16[4,8,64,192]{3,2,1,0:T(8,128)(2,1)}, bf16[4,8,64,192]{3,2,1,0:T(8,128)(2,1)}, bf16[4,8,64,192]{3,2,1,0:T(8,128)(2,1)S(1)}, bf16[4,8,64,192]{3,2,1,0:T(8,128)(2,1)S(1)}) fusion(bf16[6,10,66,192]{3,2,1,0:T(8,128)(2,1)S(1)} %fusion.9), kind=kLoop, calls=%fused_computation.270 | loop fusion | bytes 7864320 | tf_op jit(solution)/shard_map/slice | solution.py:45
  173.0 7.7 %fusion.101 = (bf16[4,8,64,192]{3,2,1,0:T(8,128)(2,1)S(1)}, bf16[4,8,64,192]{3,2,1,0:T(8,128)(2,1)S(1)}, bf16[4,8,64,192]{3,2,1,0:T(8,128)(2,1)S(1)}, bf16[4,8,6...) fusion(bf16[6,10,66,192]{3,2,1,0:T(8,128)(2,1)S(1)} %fusion.9), kind=kLoop, calls=%fused_computation.269 | loop fusion | bytes 29884416 | tf_op jit(solution)/shard_map/slice | solution.py:45
  196.4 1.0 select_convert_fusion
  (305 shorter events, 44.6 us)
Async XLA Ops:
  6.5 115.7 %copy-start.36 = (bf16[16,27,384]{2,0,1:T(8,128)(2,1)S(1)}, bf16[16,27,384]{2,0,1:T(8,128)(2,1)}, u32[]{:S(2)}) copy-start(bf16[16,27,384]{2,0,1:T(8,128)(2,1)} %param.14) | copy-start | bytes 995332
  6.5 131.6 %all-gather.2.cloned.1.call-start = ((), (), s32[]{:S(2)}) async-start(), calls=%async_computation.1 | async-start | bytes 5640192 | tf_op jit(solution)/shard_map/all_gather | solution.py:97
  35.1 15.6 %all-to-all-start = ((bf16[16,2,128]{2,1,0:T(2,128)(2,1)}), bf16[16,2,128]{2,1,0:T(2,128)(2,1)S(1)}, u32[]{:S(2)}, u32[]{:S(2)}) async-start(bf16[16,2,128]{2,1,0:T(2,128)(2,1)} %reshape.702), calls=%async_computation | async-start | bytes 16384 | tf_op jit(solution)/shard_map/all_to_all | solution.py:81
  51.7 70.4 %collective-permute-start = (bf16[4,1,16,16]{3,2,1,0:T(8,128)(2,1)S(1)}, bf16[4,1,16,16]{3,2,1,0:T(8,128)(2,1)S(1)}, u32[]{:S(2)}, u32[]{:S(2)}) collective-permute-start(bf16[4,1,16,16]{3,2,1,0:T(8,128)(2,1)S(1)} %get-tuple-element.130), channel_id=1, source_target_pairs={{0,1},{2,3},{4,5},{6,7},{8,9},{10,11},{12,13},{14,15},{16,17},{18,... | collective-permute-start | bytes 6152 | tf_op jit(solution)/shard_map/ppermute | solution.py:19
  53.0 69.1 %collective-permute-start.1 = (bf16[4,1,16,16]{3,2,1,0:T(8,128)(2,1)S(1)}, bf16[4,1,16,16]{3,2,1,0:T(8,128)(2,1)S(1)}, u32[]{:S(2)}, u32[]{:S(2)}) collective-permute-start(bf16[4,1,16,16]{3,2,1,0:T(8,128)(2,1)S(1)} %get-tuple-element.131), channel_id=1, source_target_pairs={{1,0},{3,2},{5,4},{7,6},{9,8},{11,10},{13,12},{15,14},{17,16},{19,... | collective-permute-start | bytes 6152 | tf_op jit(solution)/shard_map/ppermute | solution.py:21
  123.5 3.1 %copy-start.58 = (f32[384]{0:T(512)S(1)}, f32[384]{0:T(512)}, u32[]{:S(2)}) copy-start(f32[384]{0:T(512)} %param.17) | copy-start | bytes 4612
  127.2 5.7 %collective-permute-start.2 = (bf16[4,1,32,384]{3,2,1,0:T(8,128)(2,1)S(1)}, bf16[4,1,32,384]{3,2,1,0:T(8,128)(2,1)S(1)}, u32[]{:S(2)}, u32[]{:S(2)}) collective-permute-start(bf16[4,1,32,384]{3,2,1,0:T(8,128)(2,1)S(1)} %get-tuple-element.102), channel_id=1, source_target_pairs={{0,1},{2,3},{4,5},{6,7},{8,9},{10,11},{12,13},{14,15},{16,17},{18,... | collective-permute-start | bytes 294920 | tf_op jit(solution)/shard_map/ppermute | solution.py:19
  128.5 4.5 %collective-permute-start.3 = (bf16[4,1,32,384]{3,2,1,0:T(8,128)(2,1)S(1)}, bf16[4,1,32,384]{3,2,1,0:T(8,128)(2,1)S(1)}, u32[]{:S(2)}, u32[]{:S(2)}) collective-permute-start(bf16[4,1,32,384]{3,2,1,0:T(8,128)(2,1)S(1)} %get-tuple-element.103), channel_id=1, source_target_pairs={{1,0},{3,2},{5,4},{7,6},{9,8},{11,10},{13,12},{15,14},{17,16},{19,... | collective-permute-start | bytes 294920 | tf_op jit(solution)/shard_map/ppermute | solution.py:21
  138.2 7.5 %copy-start.2 = (bf16[384,27,192]{2,0,1:T(8,128)(2,1)S(1)}, bf16[384,27,192]{2,0,1:T(8,128)(2,1)}, u32[]{:S(2)}) copy-start(bf16[384,27,192]{2,0,1:T(8,128)(2,1)} %all-gather.2.cloned.1.call-done) | copy-start | bytes 11943940
  138.2 8.8 %copy-start.35 = (bf16[4,4,32,384]{3,2,1,0:T(8,128)(2,1)S(1)}, bf16[4,4,32,384]{3,2,1,0:T(8,128)(2,1)}, u32[]{:S(2)}) copy-start(bf16[4,4,32,384]{3,2,1,0:T(8,128)(2,1)} %get-tuple-element.90) | copy-start | bytes 1179652
  138.2 9.2 %copy-start.34 = (bf16[4,4,32,384]{3,2,1,0:T(8,128)(2,1)S(1)}, bf16[4,4,32,384]{3,2,1,0:T(8,128)(2,1)}, u32[]{:S(2)}) copy-start(bf16[4,4,32,384]{3,2,1,0:T(8,128)(2,1)} %get-tuple-element.89) | copy-start | bytes 1179652
  139.7 8.0 %copy-start.33 = (bf16[4,4,32,384]{3,2,1,0:T(8,128)(2,1)S(1)}, bf16[4,4,32,384]{3,2,1,0:T(8,128)(2,1)}, u32[]{:S(2)}) copy-start(bf16[4,4,32,384]{3,2,1,0:T(8,128)(2,1)} %get-tuple-element.88) | copy-start | bytes 1179652
  141.5 6.6 %copy-start.32 = (bf16[4,4,32,384]{3,2,1,0:T(8,128)(2,1)S(1)}, bf16[4,4,32,384]{3,2,1,0:T(8,128)(2,1)}, u32[]{:S(2)}) copy-start(bf16[4,4,32,384]{3,2,1,0:T(8,128)(2,1)} %get-tuple-element.87) | copy-start | bytes 1179652
  144.2 4.1 %copy-start.31 = (bf16[4,4,32,384]{3,2,1,0:T(8,128)(2,1)S(1)}, bf16[4,4,32,384]{3,2,1,0:T(8,128)(2,1)}, u32[]{:S(2)}) copy-start(bf16[4,4,32,384]{3,2,1,0:T(8,128)(2,1)} %get-tuple-element.86) | copy-start | bytes 1179652
  145.6 3.1 %copy-start.30 = (bf16[4,4,32,384]{3,2,1,0:T(8,128)(2,1)S(1)}, bf16[4,4,32,384]{3,2,1,0:T(8,128)(2,1)}, u32[]{:S(2)}) copy-start(bf16[4,4,32,384]{3,2,1,0:T(8,128)(2,1)} %get-tuple-element.85) | copy-start | bytes 1179652
  147.0 2.0 copy-start.29
  147.4 2.0 copy-start.28
  147.7 2.0 copy-start.27
  148.0 2.0 copy-start.26
  148.3 2.0 copy-start.25
  148.7 2.0 copy-start.24
  149.0 2.0 copy-start.23
  149.3 2.0 copy-start.22
  149.7 2.0 copy-start.21
  150.3 2.0 copy-start.20
  151.0 2.0 copy-start.19
  152.3 1.9 copy-start.59
  153.9 11.0 %copy-start.60 = (f32[96]{0:T(128)S(1)}, f32[96]{0:T(128)}, u32[]{:S(2)}) copy-start(f32[96]{0:T(128)} %param.19) | copy-start | bytes 1156
  159.1 8.8 %collective-permute-start.4 = (bf16[4,1,64,192]{3,2,1,0:T(8,128)(2,1)}, bf16[4,1,64,192]{3,2,1,0:T(8,128)(2,1)S(1)}, u32[]{:S(2)}, u32[]{:S(2)}) collective-permute-start(bf16[4,1,64,192]{3,2,1,0:T(8,128)(2,1)} %get-tuple-element.98), channel_id=1, source_target_pairs={{0,1},{2,3},{4,5},{6,7},{8,9},{10,11},{12,13},{14,15},{16,17},{18,... | collective-permute-start | bytes 294920 | tf_op jit(solution)/shard_map/ppermute | solution.py:19
  162.1 5.8 %collective-permute-start.5 = (bf16[4,1,64,192]{3,2,1,0:T(8,128)(2,1)}, bf16[4,1,64,192]{3,2,1,0:T(8,128)(2,1)S(1)}, u32[]{:S(2)}, u32[]{:S(2)}) collective-permute-start(bf16[4,1,64,192]{3,2,1,0:T(8,128)(2,1)} %get-tuple-element.99), channel_id=1, source_target_pairs={{1,0},{3,2},{5,4},{7,6},{9,8},{11,10},{13,12},{15,14},{17,16},{19,... | collective-permute-start | bytes 294920 | tf_op jit(solution)/shard_map/ppermute | solution.py:21
  173.0 8.7 %copy-start.39 = (bf16[192,1,96]{2,1,0:T(2,128)(2,1)S(1)}, bf16[192,1,96]{2,1,0:T(2,128)(2,1)}, u32[]{:S(2)}) copy-start(bf16[192,1,96]{2,1,0:T(2,128)(2,1)} %get-tuple-element.50) | copy-start | bytes 110596
  180.8 1.9 copy-start.16
  180.8 1.9 copy-start.40
  181.3 1.9 copy-start.15
  184.2 1.5 copy-start.10
  184.2 1.5 copy-start.56
  184.6 1.5 copy-start.9
  184.7 1.5 copy-start.55
  185.1 1.5 copy-start.8
  185.2 1.5 copy-start.54
  185.7 1.5 copy-start.7
  185.7 1.5 copy-start.53
  186.2 1.5 copy-start.6
  186.2 1.5 copy-start.52
  186.7 1.5 copy-start.5
  186.7 1.5 copy-start.51
  187.2 1.5 copy-start.4
  193.9 3.5 %copy-start.1 = (s32[16]{0:T(128)S(1)}, s32[16]{0:T(128)}, u32[]{:S(2)}) copy-start(s32[16]{0:T(128)} %param.12) | copy-start | bytes 196
  (21 other events, 30.4 us)
Sparse Core Ops, SparseCore 0:
  10.1 108.1 all-gather.1
where the time goes:
time: 206 us; the launch traced here: 204 us
  blocking collectives  67.8 us (33%)
  local copies, waits for them, and re-layouts  59.6 us (29%)
  matrix products  31.6 us (15%)
  starting transfers between devices  18.2 us (9%)
  between operations  17.7 us (9%)
  other arithmetic  7.68 us (4%)
    all_gather x1, blocking collectives, per_device(): lax.all_gather(w_out, 'grp', axis=0, tiled=True)  67.8 us
    dot_general x81, matrix products, causal_conv(): jnp.dot(window, weight[:, tap_index, :], preferred_element_type=jnp.float32)  31.6 us
    gather x64, local copies, waits for them, and re-layouts  22.5 us
    slice x6, local copies, waits for them, and re-layouts, causal_conv(): padded[time_tap:time_tap + count_t, row_tap:row_tap + count_r, col_tap:co...  15.7 us
    all_to_all x1, starting transfers between devices, per_device(): lax.all_to_all(outgoing, 'grp', split_axis=0, concat_axis=0, tiled=True)  8.31 us
    ppermute x3, starting transfers between devices, extended_2(): lax.ppermute(tail, axis, [(i, (i + 1) % count) for i in range(ends)])  5.62 us
    ppermute x3, starting transfers between devices, extended_2(): lax.ppermute(head, axis, [((i + 1) % count, i) for i in range(ends)])  4.28 us
  transfers between devices with their start and end apart: 8, of which 1 were waited for; matrix products, arithmetic and copies ran while one was open for 24% of the time, Pallas kernels for 0%

commit v1 on v0

--- a/solution.py
+++ b/solution.py
@@ -1,6 +1,10 @@
+import functools
+
 import jax
 import jax.numpy as jnp
 from jax import lax
+from jax.experimental import pallas as pl
+from jax.experimental.pallas import tpu as pltpu
 from jax.sharding import PartitionSpec as P
 
 RL = 2
@@ -59,7 +63,7 @@
     return jnp.repeat(jnp.repeat(values, 2, axis=1), 2, axis=2)
 
 
-def per_device(latents, frames, offsets, assign, w_in, w_mid, w_out, gain_in, gain_mid, gain_out):
+def per_device_general(latents, frames, offsets, assign, w_in, w_mid, w_out, gain_in, gain_mid, gain_out):
     groups = lax.axis_size("grp")
     row_count = lax.axis_size("row")
     row_index = lax.axis_index("row")
@@ -107,7 +111,377 @@
     return final.reshape(1, FMAX, 4 * RL, 4 * WL * final.shape[3])
 
 
+LINE = 4
+PLANE = 4
+ZC, C1, C2, C3 = 16, 384, 192, 96
+TOK = 16
+IN_SH = C1 // 16
+MID_SH = C2 // 16
+OUT_BLK = C2 // (2 * LINE)
+PIECE_ROWS = 96
+W_ROWS = 3 * IN_SH
+B_ROWS = LINE * W_ROWS + LINE * LINE
+WOUT_LANES = 896
+F32, BF16 = jnp.float32, jnp.bfloat16
+VMEM = functools.partial(pl.BlockSpec, memory_space=pltpu.VMEM)
+SMEM = functools.partial(pl.BlockSpec, memory_space=pltpu.SMEM)
+
+
+def iota(shape, dim):
+    return lax.broadcasted_iota(jnp.int32, shape, dim)
+
+
+def place():
+    group = lax.axis_index("grp")
+    return lax.div(group, PLANE), lax.rem(group, PLANE), lax.axis_index("row")
+
+
+def silu(v):
+    return v / (1.0 + jnp.exp(-v))
+
+
+def dot_nt(lhs, rhs):
+    return lax.dot_general(lhs, rhs, (((1,), (1,)), ((), ())), preferred_element_type=F32)
+
+
+def pack_kernel(offsets, assign, w_ref, lat_ref, *refs):
+    outs, (wf, lf, pf) = refs[:LINE], refs[LINE:]
+    z, _, c = place()
+    wf[:, :, :C2] = w_ref[...].astype(F32)
+    lat = lat_ref[...].astype(F32)
+    lf[32:40, :] = jnp.zeros((8, 128), F32)
+    for j in range(32):
+        lf[j : j + 1, :] = lat[:, 128 * j : 128 * j + 128]
+    lane1 = iota((1, 128), 1)
+    pf[PIECE_ROWS - 8 :, :] = jnp.zeros((8, 256), F32)
+    for g in range(16):
+        off = offsets[assign[g]]
+        row, rem = lax.div(off, 8), lax.rem(off, 8)
+        x = pltpu.roll(lf[pl.ds(row, 8), :], lax.rem(128 - ZC * rem, 128), 1)
+        keep = lane1 < 128 - ZC * rem
+        pf[g : g + 1, 0:128] = jnp.where(keep, x[0:1], x[1:2])
+        pf[g : g + 1, 128:256] = jnp.where(keep, x[1:2], x[2:3])
+    lane = iota((IN_SH, 256), 1)
+    for k in range(LINE):
+        first = (lax.rem(z + k, LINE) * 2 + c) * OUT_BLK
+        for b in range(3):
+            acc = jnp.zeros((IN_SH, 256), F32)
+            for j in range(9):
+                tap = 9 * (j // 3) + 3 * b + j % 3
+                at = OUT_BLK * j
+                moved = pltpu.roll(wf[tap], lax.rem(at - first + 256, 256), 1)
+                acc = jnp.where((lane >= at) & (lane < at + OUT_BLK), moved, acc)
+            pf[TOK + IN_SH * b : TOK + IN_SH * (b + 1), :] = acc
+        outs[k][...] = pf[...].astype(BF16)
+
+
+def pack(offsets, assign, w_mid, latents):
+    piece = jax.ShapeDtypeStruct((PIECE_ROWS, 256), BF16)
+    return pl.pallas_call(
+        pack_kernel,
+        out_shape=[piece] * LINE,
+        in_specs=[SMEM(), SMEM(), VMEM(), VMEM()],
+        out_specs=[VMEM()] * LINE,
+        scratch_shapes=[
+            pltpu.VMEM((27, IN_SH, 256), F32),
+            pltpu.VMEM((40, 128), F32),
+            pltpu.VMEM((PIECE_ROWS, 256), F32),
+        ],
+        compiler_params=pltpu.CompilerParams(vmem_limit_bytes=32 << 20),
+        name="pack",
+    )(offsets, assign, w_mid, latents)
+
+
+def join_kernel(*refs):
+    pieces, outs, (pf, bf) = refs[:LINE], refs[LINE : LINE + PLANE], refs[LINE + PLANE :]
+    _, q, _ = place()
+    for k in range(LINE):
+        whole = pieces[k][...].astype(F32)
+        pf[TOK * k : TOK * (k + 1), :] = whole[:TOK]
+        bf[W_ROWS * k : W_ROWS * (k + 1), :] = whole[TOK : TOK + W_ROWS]
+    base = LINE * W_ROWS
+    for d in range(PLANE):
+        for k in range(LINE):
+            for line in range(LINE):
+                at = base + LINE * k + line
+                bf[at : at + 1, :] = pf[pl.ds(TOK * k + PLANE * line + (q ^ d), 1), :]
+        outs[d][...] = bf[...].astype(BF16)
+
+
+def join(pieces):
+    out = jax.ShapeDtypeStruct((B_ROWS, 256), BF16)
+    return pl.pallas_call(
+        join_kernel,
+        out_shape=[out] * PLANE,
+        in_specs=[VMEM()] * LINE,
+        out_specs=[VMEM()] * PLANE,
+        scratch_shapes=[pltpu.VMEM((LINE * TOK, 256), F32), pltpu.VMEM((B_ROWS, 256), F32)],
+        compiler_params=pltpu.CompilerParams(vmem_limit_bytes=32 << 20),
+        name="join",
+    )(*pieces)
+
+
+def mid_kernel(frames, assign, *refs):
+    parts, (win_ref, gain_ref), outs = refs[:PLANE], refs[PLANE : PLANE + 2], refs[PLANE + 2 : PLANE + 2 + LINE]
+    lt, xs, zlo, zhi, w1, act, wf = refs[PLANE + 2 + LINE :]
+    z, q, _ = place()
+    base = LINE * W_ROWS
+    for d in range(PLANE):
+        part = parts[d][...].astype(F32)
+        lt[...] = part[base:]
+        for k in range(LINE):
+            shard = lax.rem(z - k + LINE, LINE) * PLANE + (q ^ d)
+            for b in range(3):
+                at = W_ROWS * k + IN_SH * b
+                wf[b, pl.ds(pl.multiple_of(shard * IN_SH, 8), IN_SH), :] = part[at : at + IN_SH]
+            for i in range(LINE):
+                xs[i, pl.ds(shard, 1), :] = lt[pl.ds(LINE * k + lax.rem(z + i, LINE), 1), :]
+    zero_rows = jnp.zeros((1, 6, WL, 640), BF16)
+    zero_cols = jnp.zeros((4, 1, WL, 640), BF16)
+    for ref in (zlo, zhi):
+        for i in range(LINE):
+            ref[i, 0:1] = zero_rows
+            ref[i, 1:2] = zero_rows
+            ref[i, 2:6, 0:1] = zero_cols
+            ref[i, 2:6, 5:6] = zero_cols
+    w1[...] = jnp.zeros((640, C1), BF16)
+    for n in range(9):
+        w1[64 * n : 64 * n + 48, :] = win_ref[48 * n : 48 * n + 48, :]
+    lane_n, row_l = iota((256, 640), 1), iota((256, 640), 0)
+    spread = ((row_l % ZC == lane_n % ZC) & (lane_n % 64 < 48) & (lane_n < 576)).astype(F32).astype(BF16)
+    tap_e = (lane_n % 64) // ZC
+    col = row_l % WL
+    from_left = (tap_e == 0) & (col > 0)
+    from_right = (tap_e == 2) & (col < WL - 1)
+    is_mid = tap_e == 1
+    low = lane_n % 128 < 64
+    pos16, shard16 = iota((256, 16), 0), iota((256, 16), 1)
+    pos, tok_l = iota((256, 256), 0).astype(F32), (iota((256, 256), 1) // ZC).astype(F32)
+    for i in range(LINE):
+        group = lax.rem(z + i, LINE) * PLANE + q
+        fill = frames[assign[group]] * (TOK // FMAX)
+        hit = (pos16 >= fill * shard16) & (pos16 < fill * (shard16 + 1))
+        first = jnp.sum(jnp.where(hit, (fill * shard16).astype(F32), 0.0), axis=1, keepdims=True)
+        rows = jnp.dot(hit.astype(F32).astype(BF16), xs[i].astype(BF16), preferred_element_type=F32)
+        own = jnp.where(pos - first == tok_l, rows, 0.0).astype(BF16)
+        wide = jnp.dot(own, spread, preferred_element_type=F32)
+        left, right = pltpu.roll(wide, 1, 0), pltpu.roll(wide, 255, 0)
+        cols = jnp.where(is_mid, wide, jnp.where(from_left, left, jnp.where(from_right, right, 0.0)))
+        zlo[i, 2:6, 1:5] = jnp.where(low, cols, 0.0).astype(BF16).reshape(4, 4, WL, 640)
+        zhi[i, 2:6, 1:5] = jnp.where(low, 0.0, cols).astype(BF16).reshape(4, 4, WL, 640)
+        taps = []
+        for j in range(5):
+            a0, b0 = divmod(2 * j, 3)
+            a1, b1 = divmod(min(2 * j + 1, 8), 3)
+            at = slice(128 * j, 128 * j + 128)
+            tile = zlo[i, a0 : a0 + 4, b0 : b0 + 4, :, at] + zhi[i, a1 : a1 + 4, b1 : b1 + 4, :, at]
+            taps.append(tile.reshape(256, 128))
+        h = jnp.dot(jnp.concatenate(taps, axis=1), w1[...], preferred_element_type=F32)
+        scale = lax.rsqrt(jnp.mean(h * h, axis=1, keepdims=True) + 1e-6)
+        act[256 * i : 256 * i + 256, :] = silu(h * scale * gain_ref[...]).astype(BF16)
+    lanes = LINE * 256
+    at = iota((OUT_BLK, lanes), 1)
+    frame, row, column = (at // 64) % FMAX, (at // WL) % 4, at % WL
+    summed = []
+    for b in range(3):
+        prod = dot_nt(wf[b].T.astype(BF16), act[...])
+        for e in range(3):
+            now, before, two = (prod[OUT_BLK * (3 * a + e) : OUT_BLK * (3 * a + e + 1)] for a in (2, 1, 0))
+            summed.append(
+                now
+                + jnp.where(frame >= 1, pltpu.roll(before, 64, 1), 0.0)
+                + jnp.where(frame >= 2, pltpu.roll(two, 128, 1), 0.0)
+            )
+    halves = [[], []]
+    for b in range(3):
+        e0, e1, e2 = summed[3 * b : 3 * b + 3]
+        halves[0].append(jnp.where(column > 0, pltpu.roll(e0, 1, 1), 0.0) + e1 + e2)
+        halves[1].append(e0 + e1 + jnp.where(column < WL - 1, pltpu.roll(e2, lanes - 1, 1), 0.0))
+    phases = [None] * 4
+    for px in range(2):
+        b0, b1, b2 = halves[px]
+        phases[px] = jnp.where(row > 0, pltpu.roll(b0, WL, 1), 0.0) + b1 + b2
+        phases[2 + px] = b0 + b1 + jnp.where(row < 3, pltpu.roll(b2, lanes - WL, 1), 0.0)
+    for i in range(LINE):
+        outs[i][...] = jnp.concatenate([p[:, 256 * i : 256 * i + 256] for p in phases], axis=0).astype(BF16)
+
+
+def mid(frames, assign, parts, w_in, gain_in):
+    out = jax.ShapeDtypeStruct((4 * OUT_BLK, 256), BF16)
+    return pl.pallas_call(
+        mid_kernel,
+        out_shape=[out] * LINE,
+        in_specs=[SMEM(), SMEM()] + [VMEM()] * (PLANE + 2),
+        out_specs=[VMEM()] * LINE,
+        scratch_shapes=[
+            pltpu.VMEM((LINE * LINE, 256), F32),
+            pltpu.VMEM((LINE, 16, 256), F32),
+            pltpu.VMEM((LINE, 6, 6, WL, 640), BF16),
+            pltpu.VMEM((LINE, 6, 6, WL, 640), BF16),
+            pltpu.VMEM((640, C1), BF16),
+            pltpu.VMEM((LINE * 256, C1), BF16),
+            pltpu.VMEM((3, C1, 256), F32),
+        ],
+        compiler_params=pltpu.CompilerParams(vmem_limit_bytes=48 << 20),
+        name="mid",
+    )(frames, assign, *parts, w_in, gain_in)
+
+
+def wide_kernel(*refs):
+    own, other, out, wf = refs[:PLANE], refs[PLANE : 2 * PLANE], refs[2 * PLANE], refs[2 * PLANE + 1]
+    z, q, c = place()
+    wf[...] = jnp.zeros((768, 1152), F32)
+    for side, group in ((c, own), (1 - c, other)):
+        for d in range(PLANE):
+            for k in range(LINE):
+                shard = lax.rem(z - k + LINE, LINE) * PLANE + (q ^ d)
+                part = group[d][k].astype(F32)
+                for r in range(3):
+                    block = side * 3 + r
+                    at = lax.div(block, 2) * 256 + shard * 16 + lax.rem(block, 2) * 8
+                    at = pl.multiple_of(at, 8)
+                    for j in range(9):
+                        wf[pl.ds(at, 8), 128 * j : 128 * j + C3] = part[8 * r : 8 * r + 8, C3 * j : C3 * (j + 1)]
+    out[...] = wf[...].astype(BF16)
+
+
+def wide(own, other):
+    return pl.pallas_call(
+        wide_kernel,
+        out_shape=jax.ShapeDtypeStruct((768, 1152), BF16),
+        in_specs=[VMEM()] * (2 * PLANE),
+        out_specs=VMEM(),
+        scratch_shapes=[pltpu.VMEM((768, 1152), F32)],
+        compiler_params=pltpu.CompilerParams(vmem_limit_bytes=48 << 20),
+        name="wide",
+    )(*own, *other)
+
+
+def out_kernel(frames, assign, *refs):
+    own, other, (w_ref, gmid_ref, gout_ref, out_ref) = refs[:LINE], refs[LINE : 2 * LINE], refs[2 * LINE : 2 * LINE + 4]
+    hid, lhs, prod = refs[2 * LINE + 4 :]
+    z, q, c = place()
+    count = frames[assign[z * PLANE + q]]
+    hid[...] = jnp.zeros((4, 256, 256), F32)
+    for side, group in ((c, own), (1 - c, other)):
+        for k in range(LINE):
+            block = lax.rem(z - k + LINE, LINE) * 2 + side
+            part = group[k][...].astype(F32)
+            for p in range(4):
+                for half in range(2):
+                    at = pl.multiple_of((block * 2 + half) * 16, 16)
+                    first = OUT_BLK * p + MID_SH * half
+                    hid[p, pl.ds(at, MID_SH), :] = part[first : first + MID_SH]
+    acts = []
+    for p in range(4):
+        h = hid[p]
+        scale = lax.rsqrt(jnp.sum(h * h, axis=0, keepdims=True) * (1.0 / C2) + 1e-6)
+        acts.append(silu(h * scale * gmid_ref[...]).astype(BF16))
+    r, l = iota((256, 256), 0), iota((256, 256), 1)
+    same = (r // 8) == ((l // 64) % 2) * WL + l % WL
+    mid_row = 2 * ((l // WL) % 4) + l // 128
+    for b in range(3):
+        wanted = (c * 8 + r % 8 + b - 1) >> 1
+        pick = (same & (mid_row == wanted)).astype(F32).astype(BF16)
+        for tp in range(2):
+            for px in range(2):
+                src = jnp.concatenate([acts[2 * py + px][:, 128 * tp : 128 * tp + 128] for py in range(2)], axis=1)
+                lhs[tp, px, :, 256 * b : 256 * b + 256] = dot_nt(pick, src).astype(BF16)
+    for tp in range(2):
+        for px in range(2):
+            prod[tp, px] = jnp.dot(lhs[tp, px], w_ref[...], preferred_element_type=F32)
+    lane = iota((1, 8, 128), 2)
+    below = [lane < 128 - 32 * i for i in range(4)]
+    for t in range(FMAX):
+        sums = []
+        for px in range(2):
+            row = []
+            for e in range(3):
+                total = None
+                for a in range(3):
+                    s = t + a - 2
+                    if s < 0:
+                        continue
+                    at = 128 * (3 * a + e)
+                    term = prod[s // 2, px, 128 * (s % 2) : 128 * (s % 2) + 128, at : at + 128].reshape(WL, 8, 128)
+                    total = term if total is None else total + term
+                row.append(total)
+            sums.append(row)
+        zero = jnp.zeros((1, 8, 128), F32)
+        after = jnp.concatenate([sums[0][2][1:], zero], axis=0)
+        before = jnp.concatenate([zero, sums[1][0][:-1]], axis=0)
+        outs = [
+            before + sums[0][1] + sums[0][2],
+            sums[0][0] + sums[0][1] + sums[1][2],
+            sums[0][0] + sums[1][1] + sums[1][2],
+            sums[1][0] + sums[1][1] + after,
+        ]
+        vals = []
+        for i, o in enumerate(outs):
+            scale = lax.rsqrt(jnp.sum(o * o, axis=2, keepdims=True) * (1.0 / C3) + 1e-6)
+            v = jnp.where(t < count, silu(o * scale * gout_ref[...]), 0.0)
+            vals.append(pltpu.roll(v, 128 - 32 * i, 2) if i else v)
+        tiles = [
+            jnp.where(lane < 96, vals[0], vals[1]),
+            jnp.where(lane < 64, vals[1], vals[2]),
+            jnp.where(lane < 32, vals[2], vals[3]),
+        ]
+        for x in range(WL):
+            both = jnp.concatenate([tile[x] for tile in tiles], axis=1)
+            out_ref[0, t, :, 384 * x : 384 * x + 384] = both.astype(BF16)
+
+
+def finish(frames, assign, own, other, w_out, gain_mid, gain_out):
+    return pl.pallas_call(
+        out_kernel,
+        out_shape=jax.ShapeDtypeStruct((1, FMAX, 4 * RL, 4 * WL * C3), BF16),
+        in_specs=[SMEM(), SMEM()] + [VMEM()] * (2 * LINE + 3),
+        out_specs=VMEM(),
+        scratch_shapes=[
+            pltpu.VMEM((4, 256, 256), F32),
+            pltpu.VMEM((2, 2, 256, 768), BF16),
+            pltpu.VMEM((2, 2, 256, 1152), F32),
+        ],
+        compiler_params=pltpu.CompilerParams(vmem_limit_bytes=48 << 20),
+        name="finish",
+    )(frames, assign, *own, *other, w_out, gain_mid, gain_out)
+
+
+def along_z(value, step):
+    return lax.ppermute(value, "grp", [(g, (g + PLANE * step) % (LINE * PLANE)) for g in range(LINE * PLANE)])
+
+
+def in_plane(value, flip):
+    return lax.ppermute(value, "grp", [(g, g ^ flip) for g in range(LINE * PLANE)])
+
+
+def other_core(value):
+    return lax.ppermute(value, "row", [(0, 1), (1, 0)])
+
+
+def per_device_fast(latents, frames, offsets, assign, w_in, w_mid, w_out, gain_in, gain_mid, gain_out):
+    core = lax.axis_index("row")
+    pieces = pack(offsets, assign, jnp.transpose(w_mid, (1, 0, 2)), latents)
+    pieces = [pieces[0]] + [along_z(pieces[k], k) for k in range(1, LINE)]
+    parts = join(pieces)
+    parts = [parts[0]] + [in_plane(parts[d], d) for d in range(1, PLANE)]
+    rows = w_out.reshape(MID_SH, 3, 3, 3, C3).transpose(2, 0, 1, 3, 4).reshape(3, MID_SH, 9 * C3)
+    rows = jnp.pad(rows, ((0, 0), (0, 16 - MID_SH), (0, WOUT_LANES - 9 * C3))).reshape(48, WOUT_LANES)
+    half = lax.dynamic_slice_in_dim(rows, core * 24, 24, axis=0)
+    line = jnp.stack([half] + [along_z(half, k) for k in range(1, LINE)])
+    own = [line] + [in_plane(line, d) for d in range(1, PLANE)]
+    other = [other_core(v) for v in own]
+    w_last = wide(own, other)
+    hidden = mid(frames, assign, parts, w_in.transpose(1, 0, 2).reshape(27 * ZC, C1), gain_in[None, :])
+    hidden = [hidden[0]] + [along_z(hidden[k], k) for k in range(1, LINE)]
+    swapped = [other_core(v) for v in hidden]
+    gmid = jnp.pad(gain_mid.reshape(16, MID_SH), ((0, 0), (0, 16 - MID_SH))).reshape(256, 1)
+    gout = jnp.pad(gain_out, (0, 128 - C3)).reshape(1, 128)
+    return finish(frames, assign, hidden, swapped, w_last, gmid, gout)
+
+
 def solution(mesh):
+    fast = mesh.shape["grp"] == LINE * PLANE and mesh.shape["row"] == 2
     placed = (
         P("grp", None),
         P(),
@@ -121,7 +495,7 @@
         P(),
     )
     return jax.shard_map(
-        per_device,
+        per_device_fast if fast else per_device_general,
         mesh=mesh,
         in_specs=placed,
         out_specs=P("grp", None, "row", None),

time: 206 us -> 59.2 us (0.29)
  blocking collectives: 67.8 us -> 0 us
  local copies, waits for them, and re-layouts: 59.6 us -> 4.43 us
  matrix products: 31.6 us -> 0 us
  between operations: 17.7 us -> 0.19 us
  waiting for transfers between devices: 1.51 us -> 17.6 us
  Pallas kernels: 0 us -> 12.5 us
  other arithmetic: 7.68 us -> 0.03 us
  starting transfers between devices: 18.2 us -> 24.1 us
    all_gather x1 -> x0, blocking collectives: 67.8 us -> none  [per_device(): lax.all_gather(w_out, 'grp', axis=0, tiled=True)]
    dot_general x81 -> x0, matrix products: 31.6 us -> none  [causal_conv(): jnp.dot(window, weight[:, tap_index, :], preferred_element_type=jnp.float32)]
    gather x67 -> x0, local copies, waits for them, and re-layouts: 25.1 us -> none
    slice x11 -> x0, local copies, waits for them, and re-layouts: 20.6 us -> none  [the longest x6 15.7 us: causal_conv(): padded[time_tap:time_tap + count_t, row_tap:row_tap + count_r, col_tap:co...]
    ppermute x6 -> x23, waiting for transfers between devices: 0.02 us -> 17.6 us  [the longest x9 10.3 us: along_z(): lax.ppermute(value, 'grp', [(g, (g + PLANE * step) % (LINE * PLANE)) for...]
    ppermute x6 -> x23, starting transfers between devices: 9.9 us -> 24.1 us  [the longest x9 13.9 us: along_z(): lax.ppermute(value, 'grp', [(g, (g + PLANE * step) % (LINE * PLANE)) for...]
    pallas_call x0 -> x5, Pallas kernels: none -> 12.5 us  [the longest x1 5.33 us: mid(): pl.pallas_call(mid_kernel, out_shape=[out] * LINE, in_specs=[SMEM(), SMEM...]
    all_to_all x1 -> x0, starting transfers between devices: 8.31 us -> none  [per_device(): lax.all_to_all(outgoing, 'grp', split_axis=0, concat_axis=0, tiled=True)]
  transfers between devices with their start and end apart: 8 -> 23, of which waited for: 1 -> 6; matrix products, arithmetic and copies ran while one was open for 24% -> 2% of each run, Pallas kernels for 0% -> 11%
where the time goes in v1:
time: 59.2 us; the launch traced here: 58.9 us
  starting transfers between devices  24.1 us (41%)
  waiting for transfers between devices  17.6 us (30%)
  Pallas kernels  12.5 us (21%)
  local copies, waits for them, and re-layouts  4.43 us (7%)
    ppermute x9, starting transfers between devices, along_z(): lax.ppermute(value, 'grp', [(g, (g + PLANE * step) % (LINE * PLANE)) for...  13.9 us
    ppermute x9, waiting for transfers between devices, along_z(): lax.ppermute(value, 'grp', [(g, (g + PLANE * step) % (LINE * PLANE)) for...  10.3 us
    ppermute x6, starting transfers between devices, in_plane(): lax.ppermute(value, 'grp', [(g, g ^ flip) for g in range(LINE * PLANE)])  9.42 us
    ppermute x6, waiting for transfers between devices, in_plane(): lax.ppermute(value, 'grp', [(g, g ^ flip) for g in range(LINE * PLANE)])  7.21 us
    pallas_call x1, Pallas kernels, mid(): pl.pallas_call(mid_kernel, out_shape=[out] * LINE, in_specs=[SMEM(), SMEM...  5.33 us
    pallas_call x1, Pallas kernels, finish(): pl.pallas_call(out_kernel, out_shape=jax.ShapeDtypeStruct((1, FMAX, 4 * R...  4.84 us
    unnamed x20, local copies, waits for them, and re-layouts  3.07 us
    pallas_call x1, Pallas kernels, pack(): pl.pallas_call(pack_kernel, out_shape=[piece] * LINE, in_specs=[SMEM(), S...  1.28 us
  transfers between devices with their start and end apart: 23, of which 6 were waited for; matrix products, arithmetic and copies ran while one was open for 2% of the time, Pallas kernels for 11%

profile of v1, /device:TPU:0, one launch (start us, length us, event | category | flops | bytes accessed | tf_op | source)
XLA Modules:
  0.0 58.9 jit_solution(6504232431980697483)
XLA Ops:
  0.0 1.0 %copy-done.1 = bf16[24,27,192]{2,0,1:T(8,128)(2,1)S(1)} copy-done((bf16[24,27,192]{2,0,1:T(8,128)(2,1)S(1)}, bf16[24,27,192]{2,0,1:T(8,128)(2,1)}, u32[]{:S(2)}) %copy-start.1) | copy-done | bytes 248856
  1.0 0.7 %copy-done.2 = bf16[1,4096]{1,0:T(2,128)(2,1)S(1)} copy-done((bf16[1,4096]{1,0:T(2,128)(2,1)S(1)}, bf16[1,4096]{1,0:T(2,128)(2,1)}, u32[]{:S(2)}) %copy-start.2) | copy-done | bytes 8216
  1.7 0.7 %copy-done.3 = s32[16]{0:T(128)S(1)} copy-done((s32[16]{0:T(128)S(1)}, s32[16]{0:T(128)}, u32[]{:S(2)}) %copy-start.3) | copy-done | bytes 88
  2.4 0.7 %copy-done.6 = s32[16]{0:T(128)S(1)} copy-done((s32[16]{0:T(128)S(1)}, s32[16]{0:T(128)}, u32[]{:S(2)}) %copy-start.6) | copy-done | bytes 88
  3.1 1.3 %pack.1 = (bf16[96,256]{1,0:T(8,128)(2,1)S(1)}, bf16[96,256]{1,0:T(8,128)(2,1)S(1)}, bf16[96,256]{1,0:T(8,128)(2,1)S(1)}, bf16[96,256]{1,0:T(8,128)(2,1)S(1)}) custom-call(s32[16]{0:T(128)S(1)} %copy-done.6, s32[16]{0:T(128)S(1)} %copy-done.3, bf16[27,24,192]{2,1,0:T(8,128)(2,1)S(1)} %bitcast.14, bf16[1,4096]{1,0:T(2,128)(2,1)S(1)} %copy-done.2), custom_call_target="tpu_custom_call" | custom-call | tf_op jit(solution)/shard_map/pack/pallas_call | solution.py:180
  4.4 3.1 %collective-permute-start = (bf16[96,256]{1,0:T(8,128)(2,1)S(1)}, bf16[96,256]{1,0:T(8,128)(2,1)S(1)}, u32[]{:S(2)}, u32[]{:S(2)}) collective-permute-start(bf16[96,256]{1,0:T(8,128)(2,1)S(1)} %get-tuple-element.18), channel_id=1, source_target_pairs={{0,8},{2,10},{4,12},{6,14},{8,16},{10,18},{12,20},{14,22},{16,24},... | collective-permute-start | bytes 147464 | tf_op jit(solution)/shard_map/ppermute | solution.py:451
  7.4 1.0 %reshape.22 = bf16[12,3,3,3,96]{4,3,2,1,0:T(4,128)(2,1)S(1)} reshape(bf16[12,27,96]{2,1,0:T(8,128)(2,1)} %param.16) | data formatting | bytes 124416 | tf_op jit(solution)/shard_map/reshape | solution.py:468
  8.4 0.1 reshape.23
  8.6 1.6 %collective-permute-start.13 = (bf16[24,896]{1,0:T(8,128)(2,1)S(1)}, bf16[24,896]{1,0:T(8,128)(2,1)S(1)}, u32[]{:S(2)}, u32[]{:S(2)}) collective-permute-start(bf16[24,896]{1,0:T(8,128)(2,1)S(1)} %constant_dynamic-slice_fusion), channel_id=1, source_target_pairs={{0,8},{2,10},{4,12},{6,14},{8,16},{10,18},{12,20},{14,22},{16,24},... | collective-permute-start | bytes 129032 | tf_op jit(solution)/shard_map/ppermute | solution.py:451
  10.3 1.1 %collective-permute-start.14 = (bf16[24,896]{1,0:T(8,128)(2,1)S(1)}, bf16[24,896]{1,0:T(8,128)(2,1)S(1)}, u32[]{:S(2)}, u32[]{:S(2)}) collective-permute-start(bf16[24,896]{1,0:T(8,128)(2,1)S(1)} %constant_dynamic-slice_fusion), channel_id=1, source_target_pairs={{0,16},{2,18},{4,20},{6,22},{8,24},{10,26},{12,28},{14,30},{16,0},... | collective-permute-start | bytes 129032 | tf_op jit(solution)/shard_map/ppermute | solution.py:451
  11.3 2.8 %collective-permute-start.15 = (bf16[24,896]{1,0:T(8,128)(2,1)S(1)}, bf16[24,896]{1,0:T(8,128)(2,1)S(1)}, u32[]{:S(2)}, u32[]{:S(2)}) collective-permute-start(bf16[24,896]{1,0:T(8,128)(2,1)S(1)} %constant_dynamic-slice_fusion), channel_id=1, source_target_pairs={{0,24},{2,26},{4,28},{6,30},{8,0},{10,2},{12,4},{14,6},{16,8},{18,... | collective-permute-start | bytes 129032 | tf_op jit(solution)/shard_map/ppermute | solution.py:451
  14.2 0.3 collective-permute-start.1
  14.5 1.2 %collective-permute-start.2 = (bf16[96,256]{1,0:T(8,128)(2,1)S(1)}, bf16[96,256]{1,0:T(8,128)(2,1)S(1)}, u32[]{:S(2)}, u32[]{:S(2)}) collective-permute-start(bf16[96,256]{1,0:T(8,128)(2,1)S(1)} %get-tuple-element.20), channel_id=1, source_target_pairs={{0,24},{2,26},{4,28},{6,30},{8,0},{10,2},{12,4},{14,6},{16,8},{18,... | collective-permute-start | bytes 147464 | tf_op jit(solution)/shard_map/ppermute | solution.py:451
  15.7 3.7 %collective-permute-done.1.refs_2_ = bf16[96,256]{1,0:T(8,128)(2,1)S(1)} collective-permute-done((bf16[96,256]{1,0:T(8,128)(2,1)S(1)}, bf16[96,256]{1,0:T(8,128)(2,1)S(1)}, u32[]{:S(2)}, u32[]{:S(2)}) %collective-permute-start.1) | collective-permute-done | bytes 49184 | tf_op jit(solution)/shard_map/ppermute | solution.py:451
  19.4 0.0 collective-permute-done.2.refs_3_
  19.4 0.1 join.1
  19.6 1.6 %collective-permute-start.3 = (bf16[304,256]{1,0:T(8,128)(2,1)S(1)}, bf16[304,256]{1,0:T(8,128)(2,1)S(1)}, u32[]{:S(2)}, u32[]{:S(2)}) collective-permute-start(bf16[304,256]{1,0:T(8,128)(2,1)S(1)} %get-tuple-element.22), channel_id=1, source_target_pairs={{0,2},{2,0},{4,6},{6,4},{8,10},{10,8},{12,14},{14,12},{16,18},{18,... | collective-permute-start | bytes 466952 | tf_op jit(solution)/shard_map/ppermute | solution.py:455
  21.2 1.5 %collective-permute-start.4 = (bf16[304,256]{1,0:T(8,128)(2,1)S(1)}, bf16[304,256]{1,0:T(8,128)(2,1)S(1)}, u32[]{:S(2)}, u32[]{:S(2)}) collective-permute-start(bf16[304,256]{1,0:T(8,128)(2,1)S(1)} %get-tuple-element.23), channel_id=1, source_target_pairs={{0,4},{2,6},{4,0},{6,2},{8,12},{10,14},{12,8},{14,10},{16,20},{18,... | collective-permute-start | bytes 466952 | tf_op jit(solution)/shard_map/ppermute | solution.py:455
  22.7 0.0 collective-permute-done.13
  22.7 0.0 collective-permute-done.14
  22.7 0.0 collective-permute-done.15
  22.7 0.6 %collective-permute-start.16 = (bf16[4,24,896]{2,1,0:T(8,128)(2,1)S(1)}, bf16[4,24,896]{2,1,0:T(8,128)(2,1)S(1)}, u32[]{:S(2)}, u32[]{:S(2)}) collective-permute-start(bf16[4,24,896]{2,1,0:T(8,128)(2,1)S(1)} %pad_maximum_fusion.refs_0_), channel_id=1, source_target_pairs={{0,2},{2,0},{4,6},{6,4},{8,10},{10,8},{12,14},{14,12},{16,18},{18,... | collective-permute-start | bytes 516104 | tf_op jit(solution)/shard_map/ppermute | solution.py:455
  23.3 0.5 collective-permute-start.17
  23.8 2.4 %collective-permute-start.5 = (bf16[304,256]{1,0:T(8,128)(2,1)S(1)}, bf16[304,256]{1,0:T(8,128)(2,1)S(1)}, u32[]{:S(2)}, u32[]{:S(2)}) collective-permute-start(bf16[304,256]{1,0:T(8,128)(2,1)S(1)} %get-tuple-element.24), channel_id=1, source_target_pairs={{0,6},{2,4},{4,2},{6,0},{8,14},{10,12},{12,10},{14,8},{16,22},{18,... | collective-permute-start | bytes 466952 | tf_op jit(solution)/shard_map/ppermute | solution.py:455
  26.3 2.8 %collective-permute-start.18 = (bf16[4,24,896]{2,1,0:T(8,128)(2,1)S(1)}, bf16[4,24,896]{2,1,0:T(8,128)(2,1)S(1)}, u32[]{:S(2)}, u32[]{:S(2)}) collective-permute-start(bf16[4,24,896]{2,1,0:T(8,128)(2,1)S(1)} %pad_maximum_fusion.refs_0_), channel_id=1, source_target_pairs={{0,6},{2,4},{4,2},{6,0},{8,14},{10,12},{12,10},{14,8},{16,22},{18,... | collective-permute-start | bytes 516104 | tf_op jit(solution)/shard_map/ppermute | solution.py:455
  29.1 0.0 collective-permute-done.4.refs_2_
  29.1 1.0 %collective-permute-done.16.refs_1_ = bf16[4,24,896]{2,1,0:T(8,128)(2,1)S(1)} collective-permute-done((bf16[4,24,896]{2,1,0:T(8,128)(2,1)S(1)}, bf16[4,24,896]{2,1,0:T(8,128)(2,1)S(1)}, u32[]{:S(2)}, u32[]{:S(2)}) %collective-permute-start.16) | collective-permute-done | bytes 172064 | tf_op jit(solution)/shard_map/ppermute | solution.py:455
  30.1 6.2 %collective-permute-done.17.refs_2_ = bf16[4,24,896]{2,1,0:T(8,128)(2,1)S(1)} collective-permute-done((bf16[4,24,896]{2,1,0:T(8,128)(2,1)S(1)}, bf16[4,24,896]{2,1,0:T(8,128)(2,1)S(1)}, u32[]{:S(2)}, u32[]{:S(2)}) %collective-permute-start.17) | collective-permute-done | bytes 172064 | tf_op jit(solution)/shard_map/ppermute | solution.py:455
  36.3 0.0 collective-permute-start.21
  36.3 0.0 collective-permute-done.5.refs_3_
  36.3 5.3 %mid.1 = (bf16[96,256]{1,0:T(8,128)(2,1)S(1)}, bf16[96,256]{1,0:T(8,128)(2,1)S(1)}, bf16[96,256]{1,0:T(8,128)(2,1)S(1)}, bf16[96,256]{1,0:T(8,128)(2,1)S(1)}) custom-call(s32[16]{0:T(128)S(1)} %copy-done.5, s32[16]{0:T(128)S(1)} %copy-done.4, bf16[304,256]{1,0:T(8,128)(2,1)S(1)} %get-tuple-element.21.refs_0_, ...), custom_call_target="tpu_custom_call" | custom-call | tf_op jit(solution)/shard_map/mid/pallas_call | solution.py:311
  41.6 1.3 %collective-permute-start.6 = (bf16[96,256]{1,0:T(8,128)(2,1)S(1)}, bf16[96,256]{1,0:T(8,128)(2,1)S(1)}, u32[]{:S(2)}, u32[]{:S(2)}) collective-permute-start(bf16[96,256]{1,0:T(8,128)(2,1)S(1)} %get-tuple-element.26), channel_id=1, source_target_pairs={{0,8},{2,10},{4,12},{6,14},{8,16},{10,18},{12,20},{14,22},{16,24},... | collective-permute-start | bytes 147464 | tf_op jit(solution)/shard_map/ppermute | solution.py:451
  43.0 0.2 collective-permute-start.22
  43.2 0.0 collective-permute-done.19.refs_4_
  43.2 2.0 %collective-permute-start.7 = (bf16[96,256]{1,0:T(8,128)(2,1)S(1)}, bf16[96,256]{1,0:T(8,128)(2,1)S(1)}, u32[]{:S(2)}, u32[]{:S(2)}) collective-permute-start(bf16[96,256]{1,0:T(8,128)(2,1)S(1)} %get-tuple-element.27), channel_id=1, source_target_pairs={{0,16},{2,18},{4,20},{6,22},{8,24},{10,26},{12,28},{14,30},{16,0},... | collective-permute-start | bytes 147464 | tf_op jit(solution)/shard_map/ppermute | solution.py:451
  45.2 3.0 %collective-permute-done.6.refs_1_ = bf16[96,256]{1,0:T(8,128)(2,1)S(1)} collective-permute-done((bf16[96,256]{1,0:T(8,128)(2,1)S(1)}, bf16[96,256]{1,0:T(8,128)(2,1)S(1)}, u32[]{:S(2)}, u32[]{:S(2)}) %collective-permute-start.6) | collective-permute-done | bytes 49184 | tf_op jit(solution)/shard_map/ppermute | solution.py:451
  48.1 0.4 collective-permute-start.8
  48.5 1.3 %collective-permute-done.7.refs_2_ = bf16[96,256]{1,0:T(8,128)(2,1)S(1)} collective-permute-done((bf16[96,256]{1,0:T(8,128)(2,1)S(1)}, bf16[96,256]{1,0:T(8,128)(2,1)S(1)}, u32[]{:S(2)}, u32[]{:S(2)}) %collective-permute-start.7) | collective-permute-done | bytes 49184 | tf_op jit(solution)/shard_map/ppermute | solution.py:451
  49.8 0.0 collective-permute-start.9
  49.8 2.4 %collective-permute-done.8.refs_3_ = bf16[96,256]{1,0:T(8,128)(2,1)S(1)} collective-permute-done((bf16[96,256]{1,0:T(8,128)(2,1)S(1)}, bf16[96,256]{1,0:T(8,128)(2,1)S(1)}, u32[]{:S(2)}, u32[]{:S(2)}) %collective-permute-start.8) | collective-permute-done | bytes 49184 | tf_op jit(solution)/shard_map/ppermute | solution.py:451
  52.2 0.0 collective-permute-start.10
  52.2 0.0 collective-permute-done.20.refs_5_
  52.2 0.5 collective-permute-start.11
  52.7 0.1 collective-permute-start.12
  52.8 0.1 reshape.25
  52.9 0.1 reshape.28.refs_9_
  53.0 1.0 %wide.1.refs_8_ = bf16[768,1152]{1,0:T(8,128)(2,1)S(1)} custom-call(bf16[4,24,896]{2,1,0:T(8,128)(2,1)S(1)} %pad_maximum_fusion.refs_0_, bf16[4,24,896]{2,1,0:T(8,128)(2,1)S(1)} %collective-permute-done.16.refs_1_, bf16[4,24,896]{2,1,0:T(8,128)(2,1)S(1)} %collective-permute-done.17.refs_2_, bf16[4,24,896]{2,1,0:T(8,128)(2,1)S(1)} %collective-permute-done.18.refs_3_, ...), custom_call_target="tpu_custom_call" | custom-call | tf_op jit(solution)/shard_map/wide/pallas_call | solution.py:349
  54.1 4.8 %finish.1 = bf16[1,4,8,6144]{3,2,1,0:T(8,128)(2,1)} custom-call(s32[16]{0:T(128)S(1)} %copy-done.5, s32[16]{0:T(128)S(1)} %copy-done.4, bf16[96,256]{1,0:T(8,128)(2,1)S(1)} %get-tuple-element.25.refs_0_, bf16[96,256]{1,0:T(8,128)(2,1)S(1)} %collective-permute-done.6.refs_1_, bf16[96,256]{1,0:T(8,128)(2,1)S(1)} %collective-permute-done.7.refs_2_, ...), custom_call_target="tpu_custom_call" | custom-call | tf_op jit(solution)/shard_map/finish/pallas_call | solution.py:435
  (35 shorter events, 0.2 us)
Async XLA Ops:
  0.0 36.3 %copy-start = (bf16[16,27,384]{2,0,1:T(8,128)(2,1)S(1)}, bf16[16,27,384]{2,0,1:T(8,128)(2,1)}, u32[]{:S(2)}) copy-start(bf16[16,27,384]{2,0,1:T(8,128)(2,1)} %param.14) | copy-start | bytes 995332
  0.0 1.0 %copy-start.1 = (bf16[24,27,192]{2,0,1:T(8,128)(2,1)S(1)}, bf16[24,27,192]{2,0,1:T(8,128)(2,1)}, u32[]{:S(2)}) copy-start(bf16[24,27,192]{2,0,1:T(8,128)(2,1)} %param.15) | copy-start | bytes 746500
  1.0 0.7 %copy-start.2 = (bf16[1,4096]{1,0:T(2,128)(2,1)S(1)}, bf16[1,4096]{1,0:T(2,128)(2,1)}, u32[]{:S(2)}) copy-start(bf16[1,4096]{1,0:T(2,128)(2,1)} %lat_ref.1) | copy-start | bytes 24580
  1.7 0.7 %copy-start.3 = (s32[16]{0:T(128)S(1)}, s32[16]{0:T(128)}, u32[]{:S(2)}) copy-start(s32[16]{0:T(128)} %assign.5) | copy-start | bytes 196
  2.4 0.7 %copy-start.6 = (s32[16]{0:T(128)S(1)}, s32[16]{0:T(128)}, u32[]{:S(2)}) copy-start(s32[16]{0:T(128)} %offsets.1) | copy-start | bytes 196
  3.1 33.2 %copy-start.7 = (f32[384]{0:T(512)S(1)}, f32[384]{0:T(512)}, u32[]{:S(2)}) copy-start(f32[384]{0:T(512)} %param.17) | copy-start | bytes 4612
  3.1 33.2 %copy-start.4 = (s32[16]{0:T(128)S(1)}, s32[16]{0:T(128)}, u32[]{:S(2)}) copy-start(s32[16]{0:T(128)} %assign.5) | copy-start | bytes 196
  3.1 33.2 %copy-start.5 = (s32[16]{0:T(128)S(1)}, s32[16]{0:T(128)}, u32[]{:S(2)}) copy-start(s32[16]{0:T(128)} %frames.3) | copy-start | bytes 196
  3.1 49.8 %copy-start.9 = (f32[96]{0:T(128)S(1)}, f32[96]{0:T(128)}, u32[]{:S(2)}) copy-start(f32[96]{0:T(128)} %param.19) | copy-start | bytes 1156
  3.1 49.8 %copy-start.8 = (f32[192]{0:T(256)S(1)}, f32[192]{0:T(256)}, u32[]{:S(2)}) copy-start(f32[192]{0:T(256)} %param.18) | copy-start | bytes 2308
  4.4 10.2 %collective-permute-start = (bf16[96,256]{1,0:T(8,128)(2,1)S(1)}, bf16[96,256]{1,0:T(8,128)(2,1)S(1)}, u32[]{:S(2)}, u32[]{:S(2)}) collective-permute-start(bf16[96,256]{1,0:T(8,128)(2,1)S(1)} %get-tuple-element.18), channel_id=1, source_target_pairs={{0,8},{2,10},{4,12},{6,14},{8,16},{10,18},{12,20},{14,22},{16,24},... | collective-permute-start | bytes 147464 | tf_op jit(solution)/shard_map/ppermute | solution.py:451
  8.6 14.0 %collective-permute-start.13 = (bf16[24,896]{1,0:T(8,128)(2,1)S(1)}, bf16[24,896]{1,0:T(8,128)(2,1)S(1)}, u32[]{:S(2)}, u32[]{:S(2)}) collective-permute-start(bf16[24,896]{1,0:T(8,128)(2,1)S(1)} %constant_dynamic-slice_fusion), channel_id=1, source_target_pairs={{0,8},{2,10},{4,12},{6,14},{8,16},{10,18},{12,20},{14,22},{16,24},... | collective-permute-start | bytes 129032 | tf_op jit(solution)/shard_map/ppermute | solution.py:451
  10.3 12.4 %collective-permute-start.14 = (bf16[24,896]{1,0:T(8,128)(2,1)S(1)}, bf16[24,896]{1,0:T(8,128)(2,1)S(1)}, u32[]{:S(2)}, u32[]{:S(2)}) collective-permute-start(bf16[24,896]{1,0:T(8,128)(2,1)S(1)} %constant_dynamic-slice_fusion), channel_id=1, source_target_pairs={{0,16},{2,18},{4,20},{6,22},{8,24},{10,26},{12,28},{14,30},{16,0},... | collective-permute-start | bytes 129032 | tf_op jit(solution)/shard_map/ppermute | solution.py:451
  11.3 11.3 %collective-permute-start.15 = (bf16[24,896]{1,0:T(8,128)(2,1)S(1)}, bf16[24,896]{1,0:T(8,128)(2,1)S(1)}, u32[]{:S(2)}, u32[]{:S(2)}) collective-permute-start(bf16[24,896]{1,0:T(8,128)(2,1)S(1)} %constant_dynamic-slice_fusion), channel_id=1, source_target_pairs={{0,24},{2,26},{4,28},{6,30},{8,0},{10,2},{12,4},{14,6},{16,8},{18,... | collective-permute-start | bytes 129032 | tf_op jit(solution)/shard_map/ppermute | solution.py:451
  14.2 5.2 %collective-permute-start.1 = (bf16[96,256]{1,0:T(8,128)(2,1)S(1)}, bf16[96,256]{1,0:T(8,128)(2,1)S(1)}, u32[]{:S(2)}, u32[]{:S(2)}) collective-permute-start(bf16[96,256]{1,0:T(8,128)(2,1)S(1)} %get-tuple-element.19), channel_id=1, source_target_pairs={{0,16},{2,18},{4,20},{6,22},{8,24},{10,26},{12,28},{14,30},{16,0},... | collective-permute-start | bytes 147464 | tf_op jit(solution)/shard_map/ppermute | solution.py:451
  14.5 4.9 %collective-permute-start.2 = (bf16[96,256]{1,0:T(8,128)(2,1)S(1)}, bf16[96,256]{1,0:T(8,128)(2,1)S(1)}, u32[]{:S(2)}, u32[]{:S(2)}) collective-permute-start(bf16[96,256]{1,0:T(8,128)(2,1)S(1)} %get-tuple-element.20), channel_id=1, source_target_pairs={{0,24},{2,26},{4,28},{6,30},{8,0},{10,2},{12,4},{14,6},{16,8},{18,... | collective-permute-start | bytes 147464 | tf_op jit(solution)/shard_map/ppermute | solution.py:451
  19.6 6.7 %collective-permute-start.3 = (bf16[304,256]{1,0:T(8,128)(2,1)S(1)}, bf16[304,256]{1,0:T(8,128)(2,1)S(1)}, u32[]{:S(2)}, u32[]{:S(2)}) collective-permute-start(bf16[304,256]{1,0:T(8,128)(2,1)S(1)} %get-tuple-element.22), channel_id=1, source_target_pairs={{0,2},{2,0},{4,6},{6,4},{8,10},{10,8},{12,14},{14,12},{16,18},{18,... | collective-permute-start | bytes 466952 | tf_op jit(solution)/shard_map/ppermute | solution.py:455
  21.2 7.9 %collective-permute-start.4 = (bf16[304,256]{1,0:T(8,128)(2,1)S(1)}, bf16[304,256]{1,0:T(8,128)(2,1)S(1)}, u32[]{:S(2)}, u32[]{:S(2)}) collective-permute-start(bf16[304,256]{1,0:T(8,128)(2,1)S(1)} %get-tuple-element.23), channel_id=1, source_target_pairs={{0,4},{2,6},{4,0},{6,2},{8,12},{10,14},{12,8},{14,10},{16,20},{18,... | collective-permute-start | bytes 466952 | tf_op jit(solution)/shard_map/ppermute | solution.py:455
  22.7 7.4 %collective-permute-start.16 = (bf16[4,24,896]{2,1,0:T(8,128)(2,1)S(1)}, bf16[4,24,896]{2,1,0:T(8,128)(2,1)S(1)}, u32[]{:S(2)}, u32[]{:S(2)}) collective-permute-start(bf16[4,24,896]{2,1,0:T(8,128)(2,1)S(1)} %pad_maximum_fusion.refs_0_), channel_id=1, source_target_pairs={{0,2},{2,0},{4,6},{6,4},{8,10},{10,8},{12,14},{14,12},{16,18},{18,... | collective-permute-start | bytes 516104 | tf_op jit(solution)/shard_map/ppermute | solution.py:455
  23.3 13.0 %collective-permute-start.17 = (bf16[4,24,896]{2,1,0:T(8,128)(2,1)S(1)}, bf16[4,24,896]{2,1,0:T(8,128)(2,1)S(1)}, u32[]{:S(2)}, u32[]{:S(2)}) collective-permute-start(bf16[4,24,896]{2,1,0:T(8,128)(2,1)S(1)} %pad_maximum_fusion.refs_0_), channel_id=1, source_target_pairs={{0,4},{2,6},{4,0},{6,2},{8,12},{10,14},{12,8},{14,10},{16,20},{18,... | collective-permute-start | bytes 516104 | tf_op jit(solution)/shard_map/ppermute | solution.py:455
  23.8 12.5 %collective-permute-start.5 = (bf16[304,256]{1,0:T(8,128)(2,1)S(1)}, bf16[304,256]{1,0:T(8,128)(2,1)S(1)}, u32[]{:S(2)}, u32[]{:S(2)}) collective-permute-start(bf16[304,256]{1,0:T(8,128)(2,1)S(1)} %get-tuple-element.24), channel_id=1, source_target_pairs={{0,6},{2,4},{4,2},{6,0},{8,14},{10,12},{12,10},{14,8},{16,22},{18,... | collective-permute-start | bytes 466952 | tf_op jit(solution)/shard_map/ppermute | solution.py:455
  26.3 16.7 %collective-permute-start.18 = (bf16[4,24,896]{2,1,0:T(8,128)(2,1)S(1)}, bf16[4,24,896]{2,1,0:T(8,128)(2,1)S(1)}, u32[]{:S(2)}, u32[]{:S(2)}) collective-permute-start(bf16[4,24,896]{2,1,0:T(8,128)(2,1)S(1)} %pad_maximum_fusion.refs_0_), channel_id=1, source_target_pairs={{0,6},{2,4},{4,2},{6,0},{8,14},{10,12},{12,10},{14,8},{16,22},{18,... | collective-permute-start | bytes 516104 | tf_op jit(solution)/shard_map/ppermute | solution.py:455
  29.1 14.1 %collective-permute-start.19 = (bf16[4,24,896]{2,1,0:T(8,128)(2,1)S(1)}, bf16[4,24,896]{2,1,0:T(8,128)(2,1)S(1)}, u32[]{:S(2)}, u32[]{:S(2)}) collective-permute-start(bf16[4,24,896]{2,1,0:T(8,128)(2,1)S(1)} %pad_maximum_fusion.refs_0_), channel_id=1, source_target_pairs={{0,1},{1,0},{2,3},{3,2},{4,5},{5,4},{6,7},{7,6},{8,9},{9,8},{10,11... | collective-permute-start | bytes 516104 | tf_op jit(solution)/shard_map/ppermute | solution.py:459
  30.1 22.1 %collective-permute-start.20 = (bf16[4,24,896]{2,1,0:T(8,128)(2,1)S(1)}, bf16[4,24,896]{2,1,0:T(8,128)(2,1)S(1)}, u32[]{:S(2)}, u32[]{:S(2)}) collective-permute-start(bf16[4,24,896]{2,1,0:T(8,128)(2,1)S(1)} %collective-permute-done.16.refs_1_), channel_id=1, source_target_pairs={{0,1},{1,0},{2,3},{3,2},{4,5},{5,4},{6,7},{7,6},{8,9},{9,8},{10,11... | collective-permute-start | bytes 516104 | tf_op jit(solution)/shard_map/ppermute | solution.py:459
  36.3 16.5 %collective-permute-start.21 = (bf16[4,24,896]{2,1,0:T(8,128)(2,1)S(1)}, bf16[4,24,896]{2,1,0:T(8,128)(2,1)S(1)}, u32[]{:S(2)}, u32[]{:S(2)}) collective-permute-start(bf16[4,24,896]{2,1,0:T(8,128)(2,1)S(1)} %collective-permute-done.17.refs_2_), channel_id=1, source_target_pairs={{0,1},{1,0},{2,3},{3,2},{4,5},{5,4},{6,7},{7,6},{8,9},{9,8},{10,11... | collective-permute-start | bytes 516104 | tf_op jit(solution)/shard_map/ppermute | solution.py:459
  41.6 6.5 %collective-permute-start.6 = (bf16[96,256]{1,0:T(8,128)(2,1)S(1)}, bf16[96,256]{1,0:T(8,128)(2,1)S(1)}, u32[]{:S(2)}, u32[]{:S(2)}) collective-permute-start(bf16[96,256]{1,0:T(8,128)(2,1)S(1)} %get-tuple-element.26), channel_id=1, source_target_pairs={{0,8},{2,10},{4,12},{6,14},{8,16},{10,18},{12,20},{14,22},{16,24},... | collective-permute-start | bytes 147464 | tf_op jit(solution)/shard_map/ppermute | solution.py:451
  43.0 10.1 %collective-permute-start.22 = (bf16[4,24,896]{2,1,0:T(8,128)(2,1)S(1)}, bf16[4,24,896]{2,1,0:T(8,128)(2,1)S(1)}, u32[]{:S(2)}, u32[]{:S(2)}) collective-permute-start(bf16[4,24,896]{2,1,0:T(8,128)(2,1)S(1)} %collective-permute-done.18.refs_3_), channel_id=1, source_target_pairs={{0,1},{1,0},{2,3},{3,2},{4,5},{5,4},{6,7},{7,6},{8,9},{9,8},{10,11... | collective-permute-start | bytes 516104 | tf_op jit(solution)/shard_map/ppermute | solution.py:459
  43.2 6.6 %collective-permute-start.7 = (bf16[96,256]{1,0:T(8,128)(2,1)S(1)}, bf16[96,256]{1,0:T(8,128)(2,1)S(1)}, u32[]{:S(2)}, u32[]{:S(2)}) collective-permute-start(bf16[96,256]{1,0:T(8,128)(2,1)S(1)} %get-tuple-element.27), channel_id=1, source_target_pairs={{0,16},{2,18},{4,20},{6,22},{8,24},{10,26},{12,28},{14,30},{16,0},... | collective-permute-start | bytes 147464 | tf_op jit(solution)/shard_map/ppermute | solution.py:451
  48.1 4.1 %collective-permute-start.8 = (bf16[96,256]{1,0:T(8,128)(2,1)S(1)}, bf16[96,256]{1,0:T(8,128)(2,1)S(1)}, u32[]{:S(2)}, u32[]{:S(2)}) collective-permute-start(bf16[96,256]{1,0:T(8,128)(2,1)S(1)} %get-tuple-element.28), channel_id=1, source_target_pairs={{0,24},{2,26},{4,28},{6,30},{8,0},{10,2},{12,4},{14,6},{16,8},{18,... | collective-permute-start | bytes 147464 | tf_op jit(solution)/shard_map/ppermute | solution.py:451
  49.8 4.2 %collective-permute-start.9 = (bf16[96,256]{1,0:T(8,128)(2,1)S(1)}, bf16[96,256]{1,0:T(8,128)(2,1)S(1)}, u32[]{:S(2)}, u32[]{:S(2)}) collective-permute-start(bf16[96,256]{1,0:T(8,128)(2,1)S(1)} %get-tuple-element.25.refs_0_), channel_id=1, source_target_pairs={{0,1},{1,0},{2,3},{3,2},{4,5},{5,4},{6,7},{7,6},{8,9},{9,8},{10,11... | collective-permute-start | bytes 147464 | tf_op jit(solution)/shard_map/ppermute | solution.py:459
  52.2 1.8 %collective-permute-start.10 = (bf16[96,256]{1,0:T(8,128)(2,1)S(1)}, bf16[96,256]{1,0:T(8,128)(2,1)S(1)}, u32[]{:S(2)}, u32[]{:S(2)}) collective-permute-start(bf16[96,256]{1,0:T(8,128)(2,1)S(1)} %collective-permute-done.6.refs_1_), channel_id=1, source_target_pairs={{0,1},{1,0},{2,3},{3,2},{4,5},{5,4},{6,7},{7,6},{8,9},{9,8},{10,11... | collective-permute-start | bytes 147464 | tf_op jit(solution)/shard_map/ppermute | solution.py:459
  52.2 1.8 %collective-permute-start.11 = (bf16[96,256]{1,0:T(8,128)(2,1)S(1)}, bf16[96,256]{1,0:T(8,128)(2,1)S(1)}, u32[]{:S(2)}, u32[]{:S(2)}) collective-permute-start(bf16[96,256]{1,0:T(8,128)(2,1)S(1)} %collective-permute-done.7.refs_2_), channel_id=1, source_target_pairs={{0,1},{1,0},{2,3},{3,2},{4,5},{5,4},{6,7},{7,6},{8,9},{9,8},{10,11... | collective-permute-start | bytes 147464 | tf_op jit(solution)/shard_map/ppermute | solution.py:459
  52.7 1.3 %collective-permute-start.12 = (bf16[96,256]{1,0:T(8,128)(2,1)S(1)}, bf16[96,256]{1,0:T(8,128)(2,1)S(1)}, u32[]{:S(2)}, u32[]{:S(2)}) collective-permute-start(bf16[96,256]{1,0:T(8,128)(2,1)S(1)} %collective-permute-done.8.refs_3_), channel_id=1, source_target_pairs={{0,1},{1,0},{2,3},{3,2},{4,5},{5,4},{6,7},{7,6},{8,9},{9,8},{10,11... | collective-permute-start | bytes 147464 | tf_op jit(solution)/shard_map/ppermute | solution.py:459

commit v2 on v1

--- a/solution.py
+++ b/solution.py
@@ -125,6 +125,11 @@
 F32, BF16 = jnp.float32, jnp.bfloat16
 VMEM = functools.partial(pl.BlockSpec, memory_space=pltpu.VMEM)
 SMEM = functools.partial(pl.BlockSpec, memory_space=pltpu.SMEM)
+HBM = functools.partial(pl.BlockSpec, memory_space=pltpu.HBM)
+
+
+def cost(us):
+    return pl.CostEstimate(flops=int(us * 1.15e9), bytes_accessed=0, transcendentals=0)
 
 
 def iota(shape, dim):
@@ -144,9 +149,15 @@
     return lax.dot_general(lhs, rhs, (((1,), (1,)), ((), ())), preferred_element_type=F32)
 
 
-def pack_kernel(offsets, assign, w_ref, lat_ref, *refs):
-    outs, (wf, lf, pf) = refs[:LINE], refs[LINE:]
+def pack_kernel(offsets_hbm, assign_hbm, w_hbm, lat_hbm, *refs):
+    outs, (wf, lf, pf, w_ref, lat_ref, offsets, assign, sems) = refs[:LINE], refs[LINE:]
+    moves = [(offsets_hbm, offsets), (assign_hbm, assign), (lat_hbm, lat_ref), (w_hbm, w_ref)]
+    copies = [pltpu.make_async_copy(src, dst, sems.at[i]) for i, (src, dst) in enumerate(moves)]
+    for copy in copies:
+        copy.start()
     z, _, c = place()
+    for copy in copies:
+        copy.wait()
     wf[:, :, :C2] = w_ref[...].astype(F32)
     lat = lat_ref[...].astype(F32)
     lf[32:40, :] = jnp.zeros((8, 128), F32)
@@ -180,16 +191,22 @@
     return pl.pallas_call(
         pack_kernel,
         out_shape=[piece] * LINE,
-        in_specs=[SMEM(), SMEM(), VMEM(), VMEM()],
+        in_specs=[HBM()] * 4,
         out_specs=[VMEM()] * LINE,
         scratch_shapes=[
             pltpu.VMEM((27, IN_SH, 256), F32),
             pltpu.VMEM((40, 128), F32),
             pltpu.VMEM((PIECE_ROWS, 256), F32),
+            pltpu.VMEM((27, IN_SH, C2), BF16),
+            pltpu.VMEM(latents.shape, BF16),
+            pltpu.SMEM(offsets.shape, jnp.int32),
+            pltpu.SMEM(assign.shape, jnp.int32),
+            pltpu.SemaphoreType.DMA((4,)),
         ],
+        cost_estimate=cost(2),
         compiler_params=pltpu.CompilerParams(vmem_limit_bytes=32 << 20),
         name="pack",
-    )(offsets, assign, w_mid, latents)
+    )(*(pltpu.with_memory_space_constraint(v, pltpu.HBM) for v in (offsets, assign, w_mid, latents)))
 
 
 def join_kernel(*refs):
@@ -217,6 +234,7 @@
         out_specs=[VMEM()] * PLANE,
         scratch_shapes=[pltpu.VMEM((LINE * TOK, 256), F32), pltpu.VMEM((B_ROWS, 256), F32)],
         compiler_params=pltpu.CompilerParams(vmem_limit_bytes=32 << 20),
+        cost_estimate=cost(5),
         name="join",
     )(*pieces)
 
@@ -323,55 +341,73 @@
             pltpu.VMEM((3, C1, 256), F32),
         ],
         compiler_params=pltpu.CompilerParams(vmem_limit_bytes=48 << 20),
+        cost_estimate=cost(5),
         name="mid",
     )(frames, assign, *parts, w_in, gain_in)
 
 
 def wide_kernel(*refs):
-    own, other, out, wf = refs[:PLANE], refs[PLANE : 2 * PLANE], refs[2 * PLANE], refs[2 * PLANE + 1]
-    z, q, c = place()
-    wf[...] = jnp.zeros((768, 1152), F32)
-    for side, group in ((c, own), (1 - c, other)):
-        for d in range(PLANE):
-            for k in range(LINE):
-                shard = lax.rem(z - k + LINE, LINE) * PLANE + (q ^ d)
-                part = group[d][k].astype(F32)
-                for r in range(3):
-                    block = side * 3 + r
-                    at = lax.div(block, 2) * 256 + shard * 16 + lax.rem(block, 2) * 8
-                    at = pl.multiple_of(at, 8)
-                    for j in range(9):
-                        wf[pl.ds(at, 8), 128 * j : 128 * j + C3] = part[8 * r : 8 * r + 8, C3 * j : C3 * (j + 1)]
+    parts, out, wf = refs[:PLANE], refs[PLANE], refs[PLANE + 1]
+    z, q, _ = place()
+    wf[...] = jnp.zeros((384, 1152), F32)
+    for d in range(PLANE):
+        for k in range(LINE):
+            shard = lax.rem(z - k + LINE, LINE) * PLANE + (q ^ d)
+            at = pl.multiple_of(shard * 8, 8)
+            part = parts[d][k].astype(F32)
+            for r in range(3):
+                for j in range(9):
+                    wf[pl.ds(128 * r + at, 8), 128 * j : 128 * j + C3] = part[8 * r : 8 * r + 8, C3 * j : C3 * (j + 1)]
     out[...] = wf[...].astype(BF16)
 
 
-def wide(own, other):
+def wide(parts):
     return pl.pallas_call(
         wide_kernel,
-        out_shape=jax.ShapeDtypeStruct((768, 1152), BF16),
-        in_specs=[VMEM()] * (2 * PLANE),
+        out_shape=jax.ShapeDtypeStruct((384, 1152), BF16),
+        in_specs=[VMEM()] * PLANE,
         out_specs=VMEM(),
-        scratch_shapes=[pltpu.VMEM((768, 1152), F32)],
+        scratch_shapes=[pltpu.VMEM((384, 1152), F32)],
+        cost_estimate=cost(0.5),
         compiler_params=pltpu.CompilerParams(vmem_limit_bytes=48 << 20),
         name="wide",
-    )(*own, *other)
+    )(*parts)
+
+
+def stack_kernel(*refs):
+    rows = refs[0].shape[0]
+    for i, ref in enumerate(refs[:-1]):
+        refs[-1][rows * i : rows * (i + 1), :] = ref[...]
+
+
+def stack(parts):
+    rows, lanes = parts[0].shape
+    return pl.pallas_call(
+        stack_kernel,
+        out_shape=jax.ShapeDtypeStruct((len(parts) * rows, lanes), BF16),
+        in_specs=[VMEM()] * len(parts),
+        out_specs=VMEM(),
+        cost_estimate=cost(5),
+        compiler_params=pltpu.CompilerParams(vmem_limit_bytes=32 << 20),
+        name="stack",
+    )(*parts)
 
 
 def out_kernel(frames, assign, *refs):
-    own, other, (w_ref, gmid_ref, gout_ref, out_ref) = refs[:LINE], refs[LINE : 2 * LINE], refs[2 * LINE : 2 * LINE + 4]
-    hid, lhs, prod = refs[2 * LINE + 4 :]
+    own, other, w_own, w_other, gmid_ref, gout_ref, out_ref, hid, lhs, prod = refs
     z, q, c = place()
     count = frames[assign[z * PLANE + q]]
     hid[...] = jnp.zeros((4, 256, 256), F32)
     for side, group in ((c, own), (1 - c, other)):
         for k in range(LINE):
             block = lax.rem(z - k + LINE, LINE) * 2 + side
-            part = group[k][...].astype(F32)
+            part = group[96 * k : 96 * k + 96, :].astype(F32)
             for p in range(4):
                 for half in range(2):
-                    at = pl.multiple_of((block * 2 + half) * 16, 16)
+                    at = pl.multiple_of((block * 2 + half) * 8, 8)
                     first = OUT_BLK * p + MID_SH * half
-                    hid[p, pl.ds(at, MID_SH), :] = part[first : first + MID_SH]
+                    hid[p, pl.ds(at, 8), :] = part[first : first + 8]
+                    hid[p, pl.ds(128 + at, 4), :] = part[first + 8 : first + MID_SH]
     acts = []
     for p in range(4):
         h = hid[p]
@@ -389,7 +425,11 @@
                 lhs[tp, px, :, 256 * b : 256 * b + 256] = dot_nt(pick, src).astype(BF16)
     for tp in range(2):
         for px in range(2):
-            prod[tp, px] = jnp.dot(lhs[tp, px], w_ref[...], preferred_element_type=F32)
+            prod[tp, px] = jnp.dot(
+                lhs[tp, px, :, pl.ds(pl.multiple_of(c * 384, 128), 384)], w_own[...], preferred_element_type=F32
+            ) + jnp.dot(
+                lhs[tp, px, :, pl.ds(pl.multiple_of((1 - c) * 384, 128), 384)], w_other[...], preferred_element_type=F32
+            )
     lane = iota((1, 8, 128), 2)
     below = [lane < 128 - 32 * i for i in range(4)]
     for t in range(FMAX):
@@ -431,11 +471,11 @@
             out_ref[0, t, :, 384 * x : 384 * x + 384] = both.astype(BF16)
 
 
-def finish(frames, assign, own, other, w_out, gain_mid, gain_out):
+def finish(frames, assign, *rest):
     return pl.pallas_call(
         out_kernel,
         out_shape=jax.ShapeDtypeStruct((1, FMAX, 4 * RL, 4 * WL * C3), BF16),
-        in_specs=[SMEM(), SMEM()] + [VMEM()] * (2 * LINE + 3),
+        in_specs=[SMEM(), SMEM()] + [VMEM()] * len(rest),
         out_specs=VMEM(),
         scratch_shapes=[
             pltpu.VMEM((4, 256, 256), F32),
@@ -443,8 +483,9 @@
             pltpu.VMEM((2, 2, 256, 1152), F32),
         ],
         compiler_params=pltpu.CompilerParams(vmem_limit_bytes=48 << 20),
+        cost_estimate=cost(4.8),
         name="finish",
-    )(frames, assign, *own, *other, w_out, gain_mid, gain_out)
+    )(frames, assign, *rest)
 
 
 def along_z(value, step):
@@ -468,16 +509,16 @@
     rows = w_out.reshape(MID_SH, 3, 3, 3, C3).transpose(2, 0, 1, 3, 4).reshape(3, MID_SH, 9 * C3)
     rows = jnp.pad(rows, ((0, 0), (0, 16 - MID_SH), (0, WOUT_LANES - 9 * C3))).reshape(48, WOUT_LANES)
     half = lax.dynamic_slice_in_dim(rows, core * 24, 24, axis=0)
-    line = jnp.stack([half] + [along_z(half, k) for k in range(1, LINE)])
+    line = stack([half] + [along_z(half, k) for k in range(1, LINE)]).reshape(LINE, 24, WOUT_LANES)
     own = [line] + [in_plane(line, d) for d in range(1, PLANE)]
-    other = [other_core(v) for v in own]
-    w_last = wide(own, other)
     hidden = mid(frames, assign, parts, w_in.transpose(1, 0, 2).reshape(27 * ZC, C1), gain_in[None, :])
-    hidden = [hidden[0]] + [along_z(hidden[k], k) for k in range(1, LINE)]
-    swapped = [other_core(v) for v in hidden]
-    gmid = jnp.pad(gain_mid.reshape(16, MID_SH), ((0, 0), (0, 16 - MID_SH))).reshape(256, 1)
+    own, _ = lax.optimization_barrier((own, hidden[0]))
+    w_last = wide(own)
+    hidden = stack([hidden[0]] + [along_z(hidden[k], k) for k in range(1, LINE)])
+    gmid = jnp.pad(gain_mid.reshape(16, MID_SH), ((0, 0), (0, 16 - MID_SH)))
+    gmid = jnp.concatenate([gmid[:, :8], gmid[:, 8:]]).reshape(256, 1)
     gout = jnp.pad(gain_out, (0, 128 - C3)).reshape(1, 128)
-    return finish(frames, assign, hidden, swapped, w_last, gmid, gout)
+    return finish(frames, assign, hidden, other_core(hidden), w_last, other_core(w_last), gmid, gout)
 
 
 def solution(mesh):

time: 59.2 us -> 47.4 us (0.80)
  waiting for transfers between devices: 17.6 us -> 9.34 us
  local copies, waits for them, and re-layouts: 4.43 us -> 1.76 us
  starting transfers between devices: 24.1 us -> 22.7 us
  Pallas kernels: 12.5 us -> 13.3 us
    ppermute x9, waiting for transfers between devices: 10.3 us -> 4.99 us  [along_z(): lax.ppermute(value, 'grp', [(g, (g + PLANE * step) % (LINE * PLANE)) for...]
    ppermute x6, waiting for transfers between devices: 7.21 us -> 3.6 us  [in_plane(): lax.ppermute(value, 'grp', [(g, g ^ flip) for g in range(LINE * PLANE)])]
    ppermute x6, starting transfers between devices: 9.42 us -> 7.25 us  [in_plane(): lax.ppermute(value, 'grp', [(g, g ^ flip) for g in range(LINE * PLANE)])]
    unnamed x20 -> x14, local copies, waits for them, and re-layouts: 3.07 us -> 1.24 us
    ppermute x9, starting transfers between devices: 13.9 us -> 15.3 us  [along_z(): lax.ppermute(value, 'grp', [(g, (g + PLANE * step) % (LINE * PLANE)) for...]
    reshape x2, local copies, waits for them, and re-layouts: 1.09 us -> 0.2 us  [per_device_fast(): w_out.reshape(MID_SH, 3, 3, 3, C3).transpose(2, 0, 1, 3, 4)]
    ppermute x8 -> x2, waiting for transfers between devices: 0.02 us -> 0.76 us  [other_core(): return lax.ppermute(value, 'row', [(0, 1), (1, 0)])]
    ppermute x8 -> x2, starting transfers between devices: 0.81 us -> 0.14 us  [other_core(): return lax.ppermute(value, 'row', [(0, 1), (1, 0)])]
  transfers between devices with their start and end apart: 23 -> 17, of which waited for: 6 -> 7; matrix products, arithmetic and copies ran while one was open for 2% -> 1% of each run, Pallas kernels for 11% -> 13%
where the time goes in v2:
time: 47.4 us; the launch traced here: 47.2 us
  starting transfers between devices  22.7 us (48%)
  Pallas kernels  13.3 us (28%)
  waiting for transfers between devices  9.34 us (20%)
  local copies, waits for them, and re-layouts  1.76 us (4%)
    ppermute x9, starting transfers between devices, along_z(): lax.ppermute(value, 'grp', [(g, (g + PLANE * step) % (LINE * PLANE)) for...  15.3 us
    ppermute x6, starting transfers between devices, in_plane(): lax.ppermute(value, 'grp', [(g, g ^ flip) for g in range(LINE * PLANE)])  7.25 us
    pallas_call x1, Pallas kernels, finish(): pl.pallas_call(out_kernel, out_shape=jax.ShapeDtypeStruct((1, FMAX, 4 * R...  5.38 us
    pallas_call x1, Pallas kernels, mid(): pl.pallas_call(mid_kernel, out_shape=[out] * LINE, in_specs=[SMEM(), SMEM...  5.32 us
    ppermute x9, waiting for transfers between devices, along_z(): lax.ppermute(value, 'grp', [(g, (g + PLANE * step) % (LINE * PLANE)) for...  4.99 us
    ppermute x6, waiting for transfers between devices, in_plane(): lax.ppermute(value, 'grp', [(g, g ^ flip) for g in range(LINE * PLANE)])  3.6 us
    pallas_call x1, Pallas kernels, pack(): pl.pallas_call(pack_kernel, out_shape=[piece] * LINE, in_specs=[HBM()] *...  1.93 us
    unnamed x14, local copies, waits for them, and re-layouts  1.24 us
  transfers between devices with their start and end apart: 17, of which 7 were waited for; matrix products, arithmetic and copies ran while one was open for 1% of the time, Pallas kernels for 13%

profile of v2, /device:TPU:0, one launch (start us, length us, event | category | flops | bytes accessed | tf_op | source)
XLA Modules:
  0.0 47.2 jit_solution(16487803146107602090)
XLA Ops:
  0.0 1.9 %pack.1 = (bf16[96,256]{1,0:T(8,128)(2,1)S(1)}, bf16[96,256]{1,0:T(8,128)(2,1)S(1)}, bf16[96,256]{1,0:T(8,128)(2,1)S(1)}, bf16[96,256]{1,0:T(8,128)(2,1)S(1)}) custom-call(s32[16]{0:T(128)} %offsets_hbm.1, s32[16]{0:T(128)} %assign.3, bf16[27,24,192]{2,1,0:T(8,128)(2,1)} %bitcast.16, bf16[1,4096]{1,0:T(2,128)(2,1)} %lat_hbm.1), custom_call_target="tpu_custom_call" | custom-call | flops 2300000000 | tf_op jit(solution)/shard_map/pack/pallas_call | solution.py:191
  1.9 3.1 %collective-permute-start = (bf16[96,256]{1,0:T(8,128)(2,1)S(1)}, bf16[96,256]{1,0:T(8,128)(2,1)S(1)}, u32[]{:S(2)}, u32[]{:S(2)}) collective-permute-start(bf16[96,256]{1,0:T(8,128)(2,1)S(1)} %get-tuple-element.22), channel_id=1, source_target_pairs={{0,8},{2,10},{4,12},{6,14},{8,16},{10,18},{12,20},{14,22},{16,24},... | collective-permute-start | bytes 147464 | tf_op jit(solution)/shard_map/ppermute | solution.py:492
  5.0 2.6 %collective-permute-start.1 = (bf16[96,256]{1,0:T(8,128)(2,1)S(1)}, bf16[96,256]{1,0:T(8,128)(2,1)S(1)}, u32[]{:S(2)}, u32[]{:S(2)}) collective-permute-start(bf16[96,256]{1,0:T(8,128)(2,1)S(1)} %get-tuple-element.23), channel_id=1, source_target_pairs={{0,16},{2,18},{4,20},{6,22},{8,24},{10,26},{12,28},{14,30},{16,0},... | collective-permute-start | bytes 147464 | tf_op jit(solution)/shard_map/ppermute | solution.py:492
  7.6 1.3 %collective-permute-start.2 = (bf16[96,256]{1,0:T(8,128)(2,1)S(1)}, bf16[96,256]{1,0:T(8,128)(2,1)S(1)}, u32[]{:S(2)}, u32[]{:S(2)}) collective-permute-start(bf16[96,256]{1,0:T(8,128)(2,1)S(1)} %get-tuple-element.24), channel_id=1, source_target_pairs={{0,24},{2,26},{4,28},{6,30},{8,0},{10,2},{12,4},{14,6},{16,8},{18,... | collective-permute-start | bytes 147464 | tf_op jit(solution)/shard_map/ppermute | solution.py:492
  9.0 0.1 reshape.25
  9.1 0.1 reshape.26
  9.2 0.0 copy-start.4
  9.3 0.0 copy-start.5
  9.3 0.5 %collective-permute-start.12 = (bf16[24,896]{1,0:T(8,128)(2,1)S(1)}, bf16[24,896]{1,0:T(8,128)(2,1)S(1)}, u32[]{:S(2)}, u32[]{:S(2)}) collective-permute-start(bf16[24,896]{1,0:T(8,128)(2,1)S(1)} %constant_dynamic-slice_fusion.refs_0_), channel_id=1, source_target_pairs={{0,24},{2,26},{4,28},{6,30},{8,0},{10,2},{12,4},{14,6},{16,8},{18,... | collective-permute-start | bytes 129032 | tf_op jit(solution)/shard_map/ppermute | solution.py:492
  9.8 1.7 %collective-permute-start.11 = (bf16[24,896]{1,0:T(8,128)(2,1)S(1)}, bf16[24,896]{1,0:T(8,128)(2,1)S(1)}, u32[]{:S(2)}, u32[]{:S(2)}) collective-permute-start(bf16[24,896]{1,0:T(8,128)(2,1)S(1)} %constant_dynamic-slice_fusion.refs_0_), channel_id=1, source_target_pairs={{0,16},{2,18},{4,20},{6,22},{8,24},{10,26},{12,28},{14,30},{16,0},... | collective-permute-start | bytes 129032 | tf_op jit(solution)/shard_map/ppermute | solution.py:492
  11.5 0.1 reshape.29
  11.6 0.0 collective-permute-done.refs_1_
  11.6 0.1 collective-permute-start.10
  11.7 0.0 collective-permute-done.1.refs_2_
  11.7 0.2 collective-permute-done.2.refs_3_
  12.0 0.1 join.1
  12.1 1.7 %collective-permute-start.3 = (bf16[304,256]{1,0:T(8,128)(2,1)S(1)}, bf16[304,256]{1,0:T(8,128)(2,1)S(1)}, u32[]{:S(2)}, u32[]{:S(2)}) collective-permute-start(bf16[304,256]{1,0:T(8,128)(2,1)S(1)} %get-tuple-element.26), channel_id=1, source_target_pairs={{0,2},{2,0},{4,6},{6,4},{8,10},{10,8},{12,14},{14,12},{16,18},{18,... | collective-permute-start | bytes 466952 | tf_op jit(solution)/shard_map/ppermute | solution.py:496
  13.8 1.5 %collective-permute-start.4 = (bf16[304,256]{1,0:T(8,128)(2,1)S(1)}, bf16[304,256]{1,0:T(8,128)(2,1)S(1)}, u32[]{:S(2)}, u32[]{:S(2)}) collective-permute-start(bf16[304,256]{1,0:T(8,128)(2,1)S(1)} %get-tuple-element.27), channel_id=1, source_target_pairs={{0,4},{2,6},{4,0},{6,2},{8,12},{10,14},{12,8},{14,10},{16,20},{18,... | collective-permute-start | bytes 466952 | tf_op jit(solution)/shard_map/ppermute | solution.py:496
  15.3 0.0 collective-permute-done.12.refs_3_
  15.3 0.5 %collective-permute-start.5 = (bf16[304,256]{1,0:T(8,128)(2,1)S(1)}, bf16[304,256]{1,0:T(8,128)(2,1)S(1)}, u32[]{:S(2)}, u32[]{:S(2)}) collective-permute-start(bf16[304,256]{1,0:T(8,128)(2,1)S(1)} %get-tuple-element.28), channel_id=1, source_target_pairs={{0,6},{2,4},{4,2},{6,0},{8,14},{10,12},{12,10},{14,8},{16,22},{18,... | collective-permute-start | bytes 466952 | tf_op jit(solution)/shard_map/ppermute | solution.py:496
  15.8 0.0 collective-permute-done.11.refs_2_
  15.8 1.6 %collective-permute-done.10.refs_1_ = bf16[24,896]{1,0:T(8,128)(2,1)S(1)} collective-permute-done((bf16[24,896]{1,0:T(8,128)(2,1)S(1)}, bf16[24,896]{1,0:T(8,128)(2,1)S(1)}, u32[]{:S(2)}, u32[]{:S(2)}) %collective-permute-start.10) | collective-permute-done | bytes 43040 | tf_op jit(solution)/shard_map/ppermute | solution.py:492
  17.5 2.5 %collective-permute-start.15 = (bf16[4,24,896]{2,1,0:T(8,128)(2,1)S(1)}, bf16[4,24,896]{2,1,0:T(8,128)(2,1)S(1)}, u32[]{:S(2)}, u32[]{:S(2)}) collective-permute-start(bf16[4,24,896]{2,1,0:T(8,128)(2,1)S(1)} %bitcast.10), channel_id=1, source_target_pairs={{0,6},{2,4},{4,2},{6,0},{8,14},{10,12},{12,10},{14,8},{16,22},{18,... | collective-permute-start | bytes 516104 | tf_op jit(solution)/shard_map/ppermute | solution.py:496
  20.0 0.5 %collective-permute-start.14 = (bf16[4,24,896]{2,1,0:T(8,128)(2,1)S(1)}, bf16[4,24,896]{2,1,0:T(8,128)(2,1)S(1)}, u32[]{:S(2)}, u32[]{:S(2)}) collective-permute-start(bf16[4,24,896]{2,1,0:T(8,128)(2,1)S(1)} %bitcast.11), channel_id=1, source_target_pairs={{0,4},{2,6},{4,0},{6,2},{8,12},{10,14},{12,8},{14,10},{16,20},{18,... | collective-permute-start | bytes 516104 | tf_op jit(solution)/shard_map/ppermute | solution.py:496
  20.5 0.5 %collective-permute-start.13 = (bf16[4,24,896]{2,1,0:T(8,128)(2,1)S(1)}, bf16[4,24,896]{2,1,0:T(8,128)(2,1)S(1)}, u32[]{:S(2)}, u32[]{:S(2)}) collective-permute-start(bf16[4,24,896]{2,1,0:T(8,128)(2,1)S(1)} %bitcast.12), channel_id=1, source_target_pairs={{0,2},{2,0},{4,6},{6,4},{8,10},{10,8},{12,14},{14,12},{16,18},{18,... | collective-permute-start | bytes 516104 | tf_op jit(solution)/shard_map/ppermute | solution.py:496
  21.0 3.6 %collective-permute-done.4.refs_2_ = bf16[304,256]{1,0:T(8,128)(2,1)S(1)} collective-permute-done((bf16[304,256]{1,0:T(8,128)(2,1)S(1)}, bf16[304,256]{1,0:T(8,128)(2,1)S(1)}, u32[]{:S(2)}, u32[]{:S(2)}) %collective-permute-start.4) | collective-permute-done | bytes 155680 | tf_op jit(solution)/shard_map/ppermute | solution.py:496
  24.6 0.6 %copy-done.1 = s32[16]{0:T(128)S(1)} copy-done((s32[16]{0:T(128)S(1)}, s32[16]{0:T(128)}, u32[]{:S(2)}) %copy-start.1) | copy-done | bytes 88
  25.3 0.0 copy-done.2
  25.3 5.3 %mid.1 = (bf16[96,256]{1,0:T(8,128)(2,1)S(1)}, bf16[96,256]{1,0:T(8,128)(2,1)S(1)}, bf16[96,256]{1,0:T(8,128)(2,1)S(1)}, bf16[96,256]{1,0:T(8,128)(2,1)S(1)}) custom-call(s32[16]{0:T(128)S(1)} %copy-done.1, s32[16]{0:T(128)S(1)} %copy-done.2, bf16[304,256]{1,0:T(8,128)(2,1)S(1)} %get-tuple-element.25.refs_0_, ...), custom_call_target="tpu_custom_call" | custom-call | flops 5750000128 | tf_op jit(solution)/shard_map/mid/pallas_call | solution.py:329
  30.6 3.4 %collective-permute-start.6 = (bf16[96,256]{1,0:T(8,128)(2,1)S(1)}, bf16[96,256]{1,0:T(8,128)(2,1)S(1)}, u32[]{:S(2)}, u32[]{:S(2)}) collective-permute-start(bf16[96,256]{1,0:T(8,128)(2,1)S(1)} %get-tuple-element.30), channel_id=1, source_target_pairs={{0,8},{2,10},{4,12},{6,14},{8,16},{10,18},{12,20},{14,22},{16,24},... | collective-permute-start | bytes 147464 | tf_op jit(solution)/shard_map/ppermute | solution.py:492
  34.0 2.3 %collective-permute-start.7 = (bf16[96,256]{1,0:T(8,128)(2,1)S(1)}, bf16[96,256]{1,0:T(8,128)(2,1)S(1)}, u32[]{:S(2)}, u32[]{:S(2)}) collective-permute-start(bf16[96,256]{1,0:T(8,128)(2,1)S(1)} %get-tuple-element.31), channel_id=1, source_target_pairs={{0,16},{2,18},{4,20},{6,22},{8,24},{10,26},{12,28},{14,30},{16,0},... | collective-permute-start | bytes 147464 | tf_op jit(solution)/shard_map/ppermute | solution.py:492
  36.2 0.0 collective-permute-done.15.refs_3_
  36.2 0.3 collective-permute-start.8
  36.6 0.0 collective-permute-done.14.refs_2_
  36.6 0.0 collective-permute-done.13.refs_1_
  36.6 0.5 %wide.1.refs_2_ = bf16[384,1152]{1,0:T(8,128)(2,1)S(1)} custom-call(bf16[4,24,896]{2,1,0:T(8,128)(2,1)S(1)} %bitcast.13, bf16[4,24,896]{2,1,0:T(8,128)(2,1)S(1)} %collective-permute-done.13.refs_1_, bf16[4,24,896]{2,1,0:T(8,128)(2,1)S(1)} %collective-permute-done.14.refs_2_, bf16[4,24,896]{2,1,0:T(8,128)(2,1)S(1)} %collective-permute-done.15.refs_3_), custom_call_target="tpu_custom_call" | custom-call | flops 575000000 | tf_op jit(solution)/shard_map/wide/pallas_call | solution.py:365
  37.1 0.1 collective-permute-start.16
  37.1 0.1 fusion
  37.2 0.5 %collective-permute-done.6.refs_1_ = bf16[96,256]{1,0:T(8,128)(2,1)S(1)} collective-permute-done((bf16[96,256]{1,0:T(8,128)(2,1)S(1)}, bf16[96,256]{1,0:T(8,128)(2,1)S(1)}, u32[]{:S(2)}, u32[]{:S(2)}) %collective-permute-start.6) | collective-permute-done | bytes 49184 | tf_op jit(solution)/shard_map/ppermute | solution.py:492
  37.7 1.4 %collective-permute-done.7.refs_2_ = bf16[96,256]{1,0:T(8,128)(2,1)S(1)} collective-permute-done((bf16[96,256]{1,0:T(8,128)(2,1)S(1)}, bf16[96,256]{1,0:T(8,128)(2,1)S(1)}, u32[]{:S(2)}, u32[]{:S(2)}) %collective-permute-start.7) | collective-permute-done | bytes 49184 | tf_op jit(solution)/shard_map/ppermute | solution.py:492
  39.1 1.2 %collective-permute-done.8.refs_3_ = bf16[96,256]{1,0:T(8,128)(2,1)S(1)} collective-permute-done((bf16[96,256]{1,0:T(8,128)(2,1)S(1)}, bf16[96,256]{1,0:T(8,128)(2,1)S(1)}, u32[]{:S(2)}, u32[]{:S(2)}) %collective-permute-start.8) | collective-permute-done | bytes 49184 | tf_op jit(solution)/shard_map/ppermute | solution.py:492
  40.3 0.1 collective-permute-start.9
  40.4 0.0 copy-start.6
  40.4 0.1 reshape.32.refs_4_
  40.5 0.5 %copy-done.6 = f32[96]{0:T(128)S(1)} copy-done((f32[96]{0:T(128)S(1)}, f32[96]{0:T(128)}, u32[]{:S(2)}) %copy-start.6) | copy-done | bytes 408
  41.1 0.8 %collective-permute-done.9.refs_1_ = bf16[384,256]{1,0:T(8,128)(2,1)S(1)} collective-permute-done((bf16[384,256]{1,0:T(8,128)(2,1)S(1)}, bf16[384,256]{1,0:T(8,128)(2,1)S(1)}, u32[]{:S(2)}, u32[]{:S(2)}) %collective-permute-start.9) | collective-permute-done | bytes 196640 | tf_op jit(solution)/shard_map/ppermute | solution.py:500
  41.8 0.0 collective-permute-done.16.refs_3_
  41.8 5.4 %finish.1 = bf16[1,4,8,6144]{3,2,1,0:T(8,128)(2,1)} custom-call(s32[16]{0:T(128)S(1)} %copy-done.1, s32[16]{0:T(128)S(1)} %copy-done.2, bf16[384,256]{1,0:T(8,128)(2,1)S(1)} %stack.2.refs_0_, bf16[384,256]{1,0:T(8,128)(2,1)S(1)} %collective-permute-done.9.refs_1_, bf16[384,1152]{1,0:T(8,128)(2,1)S(1)} %wide.1.refs_2_, ...), custom_call_target="tpu_custom_call" | custom-call | flops 5520000000 | tf_op jit(solution)/shard_map/finish/pallas_call | solution.py:475
  (18 shorter events, 0.1 us)
Async XLA Ops:
  0.0 9.0 %copy-start.3 = (bf16[12,27,96]{2,1,0:T(8,128)(2,1)S(1)}, bf16[12,27,96]{2,1,0:T(8,128)(2,1)}, u32[]{:S(2)}) copy-start(bf16[12,27,96]{2,1,0:T(8,128)(2,1)} %param.16) | copy-start | bytes 186628
  1.9 9.6 %collective-permute-start = (bf16[96,256]{1,0:T(8,128)(2,1)S(1)}, bf16[96,256]{1,0:T(8,128)(2,1)S(1)}, u32[]{:S(2)}, u32[]{:S(2)}) collective-permute-start(bf16[96,256]{1,0:T(8,128)(2,1)S(1)} %get-tuple-element.22), channel_id=1, source_target_pairs={{0,8},{2,10},{4,12},{6,14},{8,16},{10,18},{12,20},{14,22},{16,24},... | collective-permute-start | bytes 147464 | tf_op jit(solution)/shard_map/ppermute | solution.py:492
  5.0 6.7 %collective-permute-start.1 = (bf16[96,256]{1,0:T(8,128)(2,1)S(1)}, bf16[96,256]{1,0:T(8,128)(2,1)S(1)}, u32[]{:S(2)}, u32[]{:S(2)}) collective-permute-start(bf16[96,256]{1,0:T(8,128)(2,1)S(1)} %get-tuple-element.23), channel_id=1, source_target_pairs={{0,16},{2,18},{4,20},{6,22},{8,24},{10,26},{12,28},{14,30},{16,0},... | collective-permute-start | bytes 147464 | tf_op jit(solution)/shard_map/ppermute | solution.py:492
  7.6 4.3 %collective-permute-start.2 = (bf16[96,256]{1,0:T(8,128)(2,1)S(1)}, bf16[96,256]{1,0:T(8,128)(2,1)S(1)}, u32[]{:S(2)}, u32[]{:S(2)}) collective-permute-start(bf16[96,256]{1,0:T(8,128)(2,1)S(1)} %get-tuple-element.24), channel_id=1, source_target_pairs={{0,24},{2,26},{4,28},{6,30},{8,0},{10,2},{12,4},{14,6},{16,8},{18,... | collective-permute-start | bytes 147464 | tf_op jit(solution)/shard_map/ppermute | solution.py:492
  9.2 2.2 %copy-start.4 = (f32[384]{0:T(512)S(1)}, f32[384]{0:T(512)}, u32[]{:S(2)}) copy-start(f32[384]{0:T(512)} %param.17) | copy-start | bytes 4612
  9.3 2.2 %copy-start.5 = (f32[192]{0:T(256)S(1)}, f32[192]{0:T(256)}, u32[]{:S(2)}) copy-start(f32[192]{0:T(256)} %param.18) | copy-start | bytes 2308
  9.3 6.0 %collective-permute-start.12 = (bf16[24,896]{1,0:T(8,128)(2,1)S(1)}, bf16[24,896]{1,0:T(8,128)(2,1)S(1)}, u32[]{:S(2)}, u32[]{:S(2)}) collective-permute-start(bf16[24,896]{1,0:T(8,128)(2,1)S(1)} %constant_dynamic-slice_fusion.refs_0_), channel_id=1, source_target_pairs={{0,24},{2,26},{4,28},{6,30},{8,0},{10,2},{12,4},{14,6},{16,8},{18,... | collective-permute-start | bytes 129032 | tf_op jit(solution)/shard_map/ppermute | solution.py:492
  9.8 6.0 %collective-permute-start.11 = (bf16[24,896]{1,0:T(8,128)(2,1)S(1)}, bf16[24,896]{1,0:T(8,128)(2,1)S(1)}, u32[]{:S(2)}, u32[]{:S(2)}) collective-permute-start(bf16[24,896]{1,0:T(8,128)(2,1)S(1)} %constant_dynamic-slice_fusion.refs_0_), channel_id=1, source_target_pairs={{0,16},{2,18},{4,20},{6,22},{8,24},{10,26},{12,28},{14,30},{16,0},... | collective-permute-start | bytes 129032 | tf_op jit(solution)/shard_map/ppermute | solution.py:492
  11.6 5.9 %collective-permute-start.10 = (bf16[24,896]{1,0:T(8,128)(2,1)S(1)}, bf16[24,896]{1,0:T(8,128)(2,1)S(1)}, u32[]{:S(2)}, u32[]{:S(2)}) collective-permute-start(bf16[24,896]{1,0:T(8,128)(2,1)S(1)} %constant_dynamic-slice_fusion.refs_0_), channel_id=1, source_target_pairs={{0,8},{2,10},{4,12},{6,14},{8,16},{10,18},{12,20},{14,22},{16,24},... | collective-permute-start | bytes 129032 | tf_op jit(solution)/shard_map/ppermute | solution.py:492
  12.1 8.4 %collective-permute-start.3 = (bf16[304,256]{1,0:T(8,128)(2,1)S(1)}, bf16[304,256]{1,0:T(8,128)(2,1)S(1)}, u32[]{:S(2)}, u32[]{:S(2)}) collective-permute-start(bf16[304,256]{1,0:T(8,128)(2,1)S(1)} %get-tuple-element.26), channel_id=1, source_target_pairs={{0,2},{2,0},{4,6},{6,4},{8,10},{10,8},{12,14},{14,12},{16,18},{18,... | collective-permute-start | bytes 466952 | tf_op jit(solution)/shard_map/ppermute | solution.py:496
  13.8 10.8 %collective-permute-start.4 = (bf16[304,256]{1,0:T(8,128)(2,1)S(1)}, bf16[304,256]{1,0:T(8,128)(2,1)S(1)}, u32[]{:S(2)}, u32[]{:S(2)}) collective-permute-start(bf16[304,256]{1,0:T(8,128)(2,1)S(1)} %get-tuple-element.27), channel_id=1, source_target_pairs={{0,4},{2,6},{4,0},{6,2},{8,12},{10,14},{12,8},{14,10},{16,20},{18,... | collective-permute-start | bytes 466952 | tf_op jit(solution)/shard_map/ppermute | solution.py:496
  15.3 9.3 %copy-start = (bf16[16,27,384]{2,0,1:T(8,128)(2,1)S(1)}, bf16[16,27,384]{2,0,1:T(8,128)(2,1)}, u32[]{:S(2)}) copy-start(bf16[16,27,384]{2,0,1:T(8,128)(2,1)} %param.14) | copy-start | bytes 995332
  15.3 9.3 %collective-permute-start.5 = (bf16[304,256]{1,0:T(8,128)(2,1)S(1)}, bf16[304,256]{1,0:T(8,128)(2,1)S(1)}, u32[]{:S(2)}, u32[]{:S(2)}) collective-permute-start(bf16[304,256]{1,0:T(8,128)(2,1)S(1)} %get-tuple-element.28), channel_id=1, source_target_pairs={{0,6},{2,4},{4,2},{6,0},{8,14},{10,12},{12,10},{14,8},{16,22},{18,... | collective-permute-start | bytes 466952 | tf_op jit(solution)/shard_map/ppermute | solution.py:496
  17.5 18.8 %collective-permute-start.15 = (bf16[4,24,896]{2,1,0:T(8,128)(2,1)S(1)}, bf16[4,24,896]{2,1,0:T(8,128)(2,1)S(1)}, u32[]{:S(2)}, u32[]{:S(2)}) collective-permute-start(bf16[4,24,896]{2,1,0:T(8,128)(2,1)S(1)} %bitcast.10), channel_id=1, source_target_pairs={{0,6},{2,4},{4,2},{6,0},{8,14},{10,12},{12,10},{14,8},{16,22},{18,... | collective-permute-start | bytes 516104 | tf_op jit(solution)/shard_map/ppermute | solution.py:496
  20.0 16.6 %collective-permute-start.14 = (bf16[4,24,896]{2,1,0:T(8,128)(2,1)S(1)}, bf16[4,24,896]{2,1,0:T(8,128)(2,1)S(1)}, u32[]{:S(2)}, u32[]{:S(2)}) collective-permute-start(bf16[4,24,896]{2,1,0:T(8,128)(2,1)S(1)} %bitcast.11), channel_id=1, source_target_pairs={{0,4},{2,6},{4,0},{6,2},{8,12},{10,14},{12,8},{14,10},{16,20},{18,... | collective-permute-start | bytes 516104 | tf_op jit(solution)/shard_map/ppermute | solution.py:496
  20.5 16.1 %collective-permute-start.13 = (bf16[4,24,896]{2,1,0:T(8,128)(2,1)S(1)}, bf16[4,24,896]{2,1,0:T(8,128)(2,1)S(1)}, u32[]{:S(2)}, u32[]{:S(2)}) collective-permute-start(bf16[4,24,896]{2,1,0:T(8,128)(2,1)S(1)} %bitcast.12), channel_id=1, source_target_pairs={{0,2},{2,0},{4,6},{6,4},{8,10},{10,8},{12,14},{14,12},{16,18},{18,... | collective-permute-start | bytes 516104 | tf_op jit(solution)/shard_map/ppermute | solution.py:496
  24.6 0.7 %copy-start.1 = (s32[16]{0:T(128)S(1)}, s32[16]{0:T(128)}, u32[]{:S(2)}) copy-start(s32[16]{0:T(128)} %frames.3) | copy-start | bytes 196
  24.6 0.7 %copy-start.2 = (s32[16]{0:T(128)S(1)}, s32[16]{0:T(128)}, u32[]{:S(2)}) copy-start(s32[16]{0:T(128)} %assign.3) | copy-start | bytes 196
  30.6 7.1 %collective-permute-start.6 = (bf16[96,256]{1,0:T(8,128)(2,1)S(1)}, bf16[96,256]{1,0:T(8,128)(2,1)S(1)}, u32[]{:S(2)}, u32[]{:S(2)}) collective-permute-start(bf16[96,256]{1,0:T(8,128)(2,1)S(1)} %get-tuple-element.30), channel_id=1, source_target_pairs={{0,8},{2,10},{4,12},{6,14},{8,16},{10,18},{12,20},{14,22},{16,24},... | collective-permute-start | bytes 147464 | tf_op jit(solution)/shard_map/ppermute | solution.py:492
  34.0 5.2 %collective-permute-start.7 = (bf16[96,256]{1,0:T(8,128)(2,1)S(1)}, bf16[96,256]{1,0:T(8,128)(2,1)S(1)}, u32[]{:S(2)}, u32[]{:S(2)}) collective-permute-start(bf16[96,256]{1,0:T(8,128)(2,1)S(1)} %get-tuple-element.31), channel_id=1, source_target_pairs={{0,16},{2,18},{4,20},{6,22},{8,24},{10,26},{12,28},{14,30},{16,0},... | collective-permute-start | bytes 147464 | tf_op jit(solution)/shard_map/ppermute | solution.py:492
  36.2 4.1 %collective-permute-start.8 = (bf16[96,256]{1,0:T(8,128)(2,1)S(1)}, bf16[96,256]{1,0:T(8,128)(2,1)S(1)}, u32[]{:S(2)}, u32[]{:S(2)}) collective-permute-start(bf16[96,256]{1,0:T(8,128)(2,1)S(1)} %get-tuple-element.32), channel_id=1, source_target_pairs={{0,24},{2,26},{4,28},{6,30},{8,0},{10,2},{12,4},{14,6},{16,8},{18,... | collective-permute-start | bytes 147464 | tf_op jit(solution)/shard_map/ppermute | solution.py:492
  37.1 4.8 %collective-permute-start.16 = (bf16[384,1152]{1,0:T(8,128)(2,1)S(1)}, bf16[384,1152]{1,0:T(8,128)(2,1)S(1)}, u32[]{:S(2)}, u32[]{:S(2)}) collective-permute-start(bf16[384,1152]{1,0:T(8,128)(2,1)S(1)} %wide.1.refs_2_), channel_id=1, source_target_pairs={{0,1},{1,0},{2,3},{3,2},{4,5},{5,4},{6,7},{7,6},{8,9},{9,8},{10,11... | collective-permute-start | bytes 2654216 | tf_op jit(solution)/shard_map/ppermute | solution.py:500
  40.3 1.5 %collective-permute-start.9 = (bf16[384,256]{1,0:T(8,128)(2,1)S(1)}, bf16[384,256]{1,0:T(8,128)(2,1)S(1)}, u32[]{:S(2)}, u32[]{:S(2)}) collective-permute-start(bf16[384,256]{1,0:T(8,128)(2,1)S(1)} %stack.2.refs_0_), channel_id=1, source_target_pairs={{0,1},{1,0},{2,3},{3,2},{4,5},{5,4},{6,7},{7,6},{8,9},{9,8},{10,11... | collective-permute-start | bytes 589832 | tf_op jit(solution)/shard_map/ppermute | solution.py:500
  40.4 0.7 %copy-start.6 = (f32[96]{0:T(128)S(1)}, f32[96]{0:T(128)}, u32[]{:S(2)}) copy-start(f32[96]{0:T(128)} %param.19) | copy-start | bytes 1156

commit v3 on v2

--- a/solution.py
+++ b/solution.py
@@ -347,14 +347,14 @@
 
 
 def wide_kernel(*refs):
-    parts, out, wf = refs[:PLANE], refs[PLANE], refs[PLANE + 1]
+    parts, out, wf = refs[:LINE], refs[LINE], refs[LINE + 1]
     z, q, _ = place()
     wf[...] = jnp.zeros((384, 1152), F32)
-    for d in range(PLANE):
-        for k in range(LINE):
+    for k in range(LINE):
+        for d in range(PLANE):
             shard = lax.rem(z - k + LINE, LINE) * PLANE + (q ^ d)
             at = pl.multiple_of(shard * 8, 8)
-            part = parts[d][k].astype(F32)
+            part = parts[k][d].astype(F32)
             for r in range(3):
                 for j in range(9):
                     wf[pl.ds(128 * r + at, 8), 128 * j : 128 * j + C3] = part[8 * r : 8 * r + 8, C3 * j : C3 * (j + 1)]
@@ -365,7 +365,7 @@
     return pl.pallas_call(
         wide_kernel,
         out_shape=jax.ShapeDtypeStruct((384, 1152), BF16),
-        in_specs=[VMEM()] * PLANE,
+        in_specs=[VMEM()] * LINE,
         out_specs=VMEM(),
         scratch_shapes=[pltpu.VMEM((384, 1152), F32)],
         cost_estimate=cost(0.5),
@@ -509,8 +509,8 @@
     rows = w_out.reshape(MID_SH, 3, 3, 3, C3).transpose(2, 0, 1, 3, 4).reshape(3, MID_SH, 9 * C3)
     rows = jnp.pad(rows, ((0, 0), (0, 16 - MID_SH), (0, WOUT_LANES - 9 * C3))).reshape(48, WOUT_LANES)
     half = lax.dynamic_slice_in_dim(rows, core * 24, 24, axis=0)
-    line = stack([half] + [along_z(half, k) for k in range(1, LINE)]).reshape(LINE, 24, WOUT_LANES)
-    own = [line] + [in_plane(line, d) for d in range(1, PLANE)]
+    plane = stack([half] + [in_plane(half, d) for d in range(1, PLANE)]).reshape(PLANE, 24, WOUT_LANES)
+    own = [plane] + [along_z(plane, k) for k in range(1, LINE)]
     hidden = mid(frames, assign, parts, w_in.transpose(1, 0, 2).reshape(27 * ZC, C1), gain_in[None, :])
     own, _ = lax.optimization_barrier((own, hidden[0]))
     w_last = wide(own)

time: 47.4 us -> 42.9 us (0.905)
  waiting for transfers between devices: 9.34 us -> 6.13 us
  starting transfers between devices: 22.7 us -> 21.4 us
    ppermute x9, waiting for transfers between devices: 4.99 us -> 2.53 us  [along_z(): lax.ppermute(value, 'grp', [(g, (g + PLANE * step) % (LINE * PLANE)) for...]
    ppermute x9, starting transfers between devices: 15.3 us -> 13.8 us  [along_z(): lax.ppermute(value, 'grp', [(g, (g + PLANE * step) % (LINE * PLANE)) for...]
    ppermute x6, waiting for transfers between devices: 3.6 us -> 2.75 us  [in_plane(): lax.ppermute(value, 'grp', [(g, g ^ flip) for g in range(LINE * PLANE)])]
  transfers between devices with their start and end apart: 17 -> 17, of which waited for: 7 -> 5; matrix products, arithmetic and copies ran while one was open for 1% -> 1% of each run, Pallas kernels for 13% -> 14%
where the time goes in v3:
time: 42.9 us; the launch traced here: 42.8 us
  starting transfers between devices  21.4 us (50%)
  Pallas kernels  13.3 us (31%)
  waiting for transfers between devices  6.13 us (14%)
  local copies, waits for them, and re-layouts  1.76 us (4%)
    ppermute x9, starting transfers between devices, along_z(): lax.ppermute(value, 'grp', [(g, (g + PLANE * step) % (LINE * PLANE)) for...  13.8 us
    ppermute x6, starting transfers between devices, in_plane(): lax.ppermute(value, 'grp', [(g, g ^ flip) for g in range(LINE * PLANE)])  7.54 us
    pallas_call x1, Pallas kernels, finish(): pl.pallas_call(out_kernel, out_shape=jax.ShapeDtypeStruct((1, FMAX, 4 * R...  5.38 us
    pallas_call x1, Pallas kernels, mid(): pl.pallas_call(mid_kernel, out_shape=[out] * LINE, in_specs=[SMEM(), SMEM...  5.32 us
    ppermute x6, waiting for transfers between devices, in_plane(): lax.ppermute(value, 'grp', [(g, g ^ flip) for g in range(LINE * PLANE)])  2.75 us
    ppermute x9, waiting for transfers between devices, along_z(): lax.ppermute(value, 'grp', [(g, (g + PLANE * step) % (LINE * PLANE)) for...  2.53 us
    pallas_call x1, Pallas kernels, pack(): pl.pallas_call(pack_kernel, out_shape=[piece] * LINE, in_specs=[HBM()] *...  1.93 us
    unnamed x14, local copies, waits for them, and re-layouts  1.24 us
  transfers between devices with their start and end apart: 17, of which 5 were waited for; matrix products, arithmetic and copies ran while one was open for 1% of the time, Pallas kernels for 14%

profile of v3, /device:TPU:0, one launch (start us, length us, event | category | flops | bytes accessed | tf_op | source)
XLA Modules:
  0.0 42.8 jit_solution(2200609582574732187)
XLA Ops:
  0.0 1.9 %pack.1 = (bf16[96,256]{1,0:T(8,128)(2,1)S(1)}, bf16[96,256]{1,0:T(8,128)(2,1)S(1)}, bf16[96,256]{1,0:T(8,128)(2,1)S(1)}, bf16[96,256]{1,0:T(8,128)(2,1)S(1)}) custom-call(s32[16]{0:T(128)} %offsets_hbm.1, s32[16]{0:T(128)} %assign.3, bf16[27,24,192]{2,1,0:T(8,128)(2,1)} %bitcast.16, bf16[1,4096]{1,0:T(2,128)(2,1)} %lat_hbm.1), custom_call_target="tpu_custom_call" | custom-call | flops 2300000000 | tf_op jit(solution)/shard_map/pack/pallas_call | solution.py:191
  1.9 3.1 %collective-permute-start = (bf16[96,256]{1,0:T(8,128)(2,1)S(1)}, bf16[96,256]{1,0:T(8,128)(2,1)S(1)}, u32[]{:S(2)}, u32[]{:S(2)}) collective-permute-start(bf16[96,256]{1,0:T(8,128)(2,1)S(1)} %get-tuple-element.22), channel_id=1, source_target_pairs={{0,8},{2,10},{4,12},{6,14},{8,16},{10,18},{12,20},{14,22},{16,24},... | collective-permute-start | bytes 147464 | tf_op jit(solution)/shard_map/ppermute | solution.py:492
  5.0 2.6 %collective-permute-start.1 = (bf16[96,256]{1,0:T(8,128)(2,1)S(1)}, bf16[96,256]{1,0:T(8,128)(2,1)S(1)}, u32[]{:S(2)}, u32[]{:S(2)}) collective-permute-start(bf16[96,256]{1,0:T(8,128)(2,1)S(1)} %get-tuple-element.23), channel_id=1, source_target_pairs={{0,16},{2,18},{4,20},{6,22},{8,24},{10,26},{12,28},{14,30},{16,0},... | collective-permute-start | bytes 147464 | tf_op jit(solution)/shard_map/ppermute | solution.py:492
  7.6 1.3 %collective-permute-start.2 = (bf16[96,256]{1,0:T(8,128)(2,1)S(1)}, bf16[96,256]{1,0:T(8,128)(2,1)S(1)}, u32[]{:S(2)}, u32[]{:S(2)}) collective-permute-start(bf16[96,256]{1,0:T(8,128)(2,1)S(1)} %get-tuple-element.24), channel_id=1, source_target_pairs={{0,24},{2,26},{4,28},{6,30},{8,0},{10,2},{12,4},{14,6},{16,8},{18,... | collective-permute-start | bytes 147464 | tf_op jit(solution)/shard_map/ppermute | solution.py:492
  9.0 0.1 reshape.25
  9.1 0.1 reshape.26
  9.2 0.0 copy-start.4
  9.3 0.0 copy-start.5
  9.3 2.5 %collective-permute-start.12 = (bf16[24,896]{1,0:T(8,128)(2,1)S(1)}, bf16[24,896]{1,0:T(8,128)(2,1)S(1)}, u32[]{:S(2)}, u32[]{:S(2)}) collective-permute-start(bf16[24,896]{1,0:T(8,128)(2,1)S(1)} %constant_dynamic-slice_fusion.refs_0_), channel_id=1, source_target_pairs={{0,6},{2,4},{4,2},{6,0},{8,14},{10,12},{12,10},{14,8},{16,22},{18,... | collective-permute-start | bytes 129032 | tf_op jit(solution)/shard_map/ppermute | solution.py:496
  11.8 0.5 %collective-permute-start.11 = (bf16[24,896]{1,0:T(8,128)(2,1)S(1)}, bf16[24,896]{1,0:T(8,128)(2,1)S(1)}, u32[]{:S(2)}, u32[]{:S(2)}) collective-permute-start(bf16[24,896]{1,0:T(8,128)(2,1)S(1)} %constant_dynamic-slice_fusion.refs_0_), channel_id=1, source_target_pairs={{0,4},{2,6},{4,0},{6,2},{8,12},{10,14},{12,8},{14,10},{16,20},{18,... | collective-permute-start | bytes 129032 | tf_op jit(solution)/shard_map/ppermute | solution.py:496
  12.3 0.1 reshape.29
  12.4 0.0 collective-permute-done.refs_1_
  12.4 0.6 %collective-permute-start.10 = (bf16[24,896]{1,0:T(8,128)(2,1)S(1)}, bf16[24,896]{1,0:T(8,128)(2,1)S(1)}, u32[]{:S(2)}, u32[]{:S(2)}) collective-permute-start(bf16[24,896]{1,0:T(8,128)(2,1)S(1)} %constant_dynamic-slice_fusion.refs_0_), channel_id=1, source_target_pairs={{0,2},{2,0},{4,6},{6,4},{8,10},{10,8},{12,14},{14,12},{16,18},{18,... | collective-permute-start | bytes 129032 | tf_op jit(solution)/shard_map/ppermute | solution.py:496
  13.0 0.0 collective-permute-done.1.refs_2_
  13.0 0.0 collective-permute-done.2.refs_3_
  13.0 0.1 join.1
  13.2 1.6 %collective-permute-start.3 = (bf16[304,256]{1,0:T(8,128)(2,1)S(1)}, bf16[304,256]{1,0:T(8,128)(2,1)S(1)}, u32[]{:S(2)}, u32[]{:S(2)}) collective-permute-start(bf16[304,256]{1,0:T(8,128)(2,1)S(1)} %get-tuple-element.26), channel_id=1, source_target_pairs={{0,2},{2,0},{4,6},{6,4},{8,10},{10,8},{12,14},{14,12},{16,18},{18,... | collective-permute-start | bytes 466952 | tf_op jit(solution)/shard_map/ppermute | solution.py:496
  14.7 1.5 %collective-permute-start.4 = (bf16[304,256]{1,0:T(8,128)(2,1)S(1)}, bf16[304,256]{1,0:T(8,128)(2,1)S(1)}, u32[]{:S(2)}, u32[]{:S(2)}) collective-permute-start(bf16[304,256]{1,0:T(8,128)(2,1)S(1)} %get-tuple-element.27), channel_id=1, source_target_pairs={{0,4},{2,6},{4,0},{6,2},{8,12},{10,14},{12,8},{14,10},{16,20},{18,... | collective-permute-start | bytes 466952 | tf_op jit(solution)/shard_map/ppermute | solution.py:496
  16.2 0.0 collective-permute-done.12.refs_3_
  16.2 0.8 %collective-permute-start.5 = (bf16[304,256]{1,0:T(8,128)(2,1)S(1)}, bf16[304,256]{1,0:T(8,128)(2,1)S(1)}, u32[]{:S(2)}, u32[]{:S(2)}) collective-permute-start(bf16[304,256]{1,0:T(8,128)(2,1)S(1)} %get-tuple-element.28), channel_id=1, source_target_pairs={{0,6},{2,4},{4,2},{6,0},{8,14},{10,12},{12,10},{14,8},{16,22},{18,... | collective-permute-start | bytes 466952 | tf_op jit(solution)/shard_map/ppermute | solution.py:496
  17.1 0.0 collective-permute-done.11.refs_2_
  17.1 0.0 collective-permute-done.10.refs_1_
  17.1 1.5 %collective-permute-start.15 = (bf16[4,24,896]{2,1,0:T(8,128)(2,1)S(1)}, bf16[4,24,896]{2,1,0:T(8,128)(2,1)S(1)}, u32[]{:S(2)}, u32[]{:S(2)}) collective-permute-start(bf16[4,24,896]{2,1,0:T(8,128)(2,1)S(1)} %bitcast.10), channel_id=1, source_target_pairs={{0,24},{2,26},{4,28},{6,30},{8,0},{10,2},{12,4},{14,6},{16,8},{18,... | collective-permute-start | bytes 516104 | tf_op jit(solution)/shard_map/ppermute | solution.py:492
  18.6 0.7 %collective-permute-start.14 = (bf16[4,24,896]{2,1,0:T(8,128)(2,1)S(1)}, bf16[4,24,896]{2,1,0:T(8,128)(2,1)S(1)}, u32[]{:S(2)}, u32[]{:S(2)}) collective-permute-start(bf16[4,24,896]{2,1,0:T(8,128)(2,1)S(1)} %bitcast.11), channel_id=1, source_target_pairs={{0,16},{2,18},{4,20},{6,22},{8,24},{10,26},{12,28},{14,30},{16,0},... | collective-permute-start | bytes 516104 | tf_op jit(solution)/shard_map/ppermute | solution.py:492
  19.3 0.6 %collective-permute-done.3.refs_1_ = bf16[304,256]{1,0:T(8,128)(2,1)S(1)} collective-permute-done((bf16[304,256]{1,0:T(8,128)(2,1)S(1)}, bf16[304,256]{1,0:T(8,128)(2,1)S(1)}, u32[]{:S(2)}, u32[]{:S(2)}) %collective-permute-start.3) | collective-permute-done | bytes 155680 | tf_op jit(solution)/shard_map/ppermute | solution.py:496
  19.9 0.7 %collective-permute-start.13 = (bf16[4,24,896]{2,1,0:T(8,128)(2,1)S(1)}, bf16[4,24,896]{2,1,0:T(8,128)(2,1)S(1)}, u32[]{:S(2)}, u32[]{:S(2)}) collective-permute-start(bf16[4,24,896]{2,1,0:T(8,128)(2,1)S(1)} %bitcast.12), channel_id=1, source_target_pairs={{0,8},{2,10},{4,12},{6,14},{8,16},{10,18},{12,20},{14,22},{16,24},... | collective-permute-start | bytes 516104 | tf_op jit(solution)/shard_map/ppermute | solution.py:492
  20.6 2.2 %collective-permute-done.4.refs_2_ = bf16[304,256]{1,0:T(8,128)(2,1)S(1)} collective-permute-done((bf16[304,256]{1,0:T(8,128)(2,1)S(1)}, bf16[304,256]{1,0:T(8,128)(2,1)S(1)}, u32[]{:S(2)}, u32[]{:S(2)}) %collective-permute-start.4) | collective-permute-done | bytes 155680 | tf_op jit(solution)/shard_map/ppermute | solution.py:496
  22.7 0.0 collective-permute-done.5.refs_3_
  22.7 0.6 %copy-done.1 = s32[16]{0:T(128)S(1)} copy-done((s32[16]{0:T(128)S(1)}, s32[16]{0:T(128)}, u32[]{:S(2)}) %copy-start.1) | copy-done | bytes 88
  23.4 0.0 copy-done.2
  23.4 5.3 %mid.1 = (bf16[96,256]{1,0:T(8,128)(2,1)S(1)}, bf16[96,256]{1,0:T(8,128)(2,1)S(1)}, bf16[96,256]{1,0:T(8,128)(2,1)S(1)}, bf16[96,256]{1,0:T(8,128)(2,1)S(1)}) custom-call(s32[16]{0:T(128)S(1)} %copy-done.1, s32[16]{0:T(128)S(1)} %copy-done.2, bf16[304,256]{1,0:T(8,128)(2,1)S(1)} %get-tuple-element.25.refs_0_, ...), custom_call_target="tpu_custom_call" | custom-call | flops 5750000128 | tf_op jit(solution)/shard_map/mid/pallas_call | solution.py:329
  28.7 0.7 %collective-permute-start.6 = (bf16[96,256]{1,0:T(8,128)(2,1)S(1)}, bf16[96,256]{1,0:T(8,128)(2,1)S(1)}, u32[]{:S(2)}, u32[]{:S(2)}) collective-permute-start(bf16[96,256]{1,0:T(8,128)(2,1)S(1)} %get-tuple-element.30), channel_id=1, source_target_pairs={{0,8},{2,10},{4,12},{6,14},{8,16},{10,18},{12,20},{14,22},{16,24},... | collective-permute-start | bytes 147464 | tf_op jit(solution)/shard_map/ppermute | solution.py:492
  29.4 1.8 %collective-permute-start.7 = (bf16[96,256]{1,0:T(8,128)(2,1)S(1)}, bf16[96,256]{1,0:T(8,128)(2,1)S(1)}, u32[]{:S(2)}, u32[]{:S(2)}) collective-permute-start(bf16[96,256]{1,0:T(8,128)(2,1)S(1)} %get-tuple-element.31), channel_id=1, source_target_pairs={{0,16},{2,18},{4,20},{6,22},{8,24},{10,26},{12,28},{14,30},{16,0},... | collective-permute-start | bytes 147464 | tf_op jit(solution)/shard_map/ppermute | solution.py:492
  31.3 0.0 collective-permute-done.15.refs_3_
  31.3 1.3 %collective-permute-start.8 = (bf16[96,256]{1,0:T(8,128)(2,1)S(1)}, bf16[96,256]{1,0:T(8,128)(2,1)S(1)}, u32[]{:S(2)}, u32[]{:S(2)}) collective-permute-start(bf16[96,256]{1,0:T(8,128)(2,1)S(1)} %get-tuple-element.32), channel_id=1, source_target_pairs={{0,24},{2,26},{4,28},{6,30},{8,0},{10,2},{12,4},{14,6},{16,8},{18,... | collective-permute-start | bytes 147464 | tf_op jit(solution)/shard_map/ppermute | solution.py:492
  32.6 1.5 %collective-permute-done.14.refs_2_ = bf16[4,24,896]{2,1,0:T(8,128)(2,1)S(1)} collective-permute-done((bf16[4,24,896]{2,1,0:T(8,128)(2,1)S(1)}, bf16[4,24,896]{2,1,0:T(8,128)(2,1)S(1)}, u32[]{:S(2)}, u32[]{:S(2)}) %collective-permute-start.14) | collective-permute-done | bytes 172064 | tf_op jit(solution)/shard_map/ppermute | solution.py:492
  34.1 0.0 collective-permute-done.13.refs_1_
  34.1 0.5 %wide.1.refs_2_ = bf16[384,1152]{1,0:T(8,128)(2,1)S(1)} custom-call(bf16[4,24,896]{2,1,0:T(8,128)(2,1)S(1)} %bitcast.13, bf16[4,24,896]{2,1,0:T(8,128)(2,1)S(1)} %collective-permute-done.13.refs_1_, bf16[4,24,896]{2,1,0:T(8,128)(2,1)S(1)} %collective-permute-done.14.refs_2_, bf16[4,24,896]{2,1,0:T(8,128)(2,1)S(1)} %collective-permute-done.15.refs_3_), custom_call_target="tpu_custom_call" | custom-call | flops 575000000 | tf_op jit(solution)/shard_map/wide/pallas_call | solution.py:365
  34.6 0.1 collective-permute-start.16
  34.7 0.1 fusion
  34.8 1.0 %collective-permute-done.7.refs_2_ = bf16[96,256]{1,0:T(8,128)(2,1)S(1)} collective-permute-done((bf16[96,256]{1,0:T(8,128)(2,1)S(1)}, bf16[96,256]{1,0:T(8,128)(2,1)S(1)}, u32[]{:S(2)}, u32[]{:S(2)}) %collective-permute-start.7) | collective-permute-done | bytes 49184 | tf_op jit(solution)/shard_map/ppermute | solution.py:492
  35.8 0.0 collective-permute-done.8.refs_3_
  35.8 0.1 collective-permute-start.9
  35.9 0.0 copy-start.6
  35.9 0.1 reshape.32.refs_4_
  36.0 0.5 %copy-done.6 = f32[96]{0:T(128)S(1)} copy-done((f32[96]{0:T(128)S(1)}, f32[96]{0:T(128)}, u32[]{:S(2)}) %copy-start.6) | copy-done | bytes 408
  36.6 0.8 %collective-permute-done.9.refs_1_ = bf16[384,256]{1,0:T(8,128)(2,1)S(1)} collective-permute-done((bf16[384,256]{1,0:T(8,128)(2,1)S(1)}, bf16[384,256]{1,0:T(8,128)(2,1)S(1)}, u32[]{:S(2)}, u32[]{:S(2)}) %collective-permute-start.9) | collective-permute-done | bytes 196640 | tf_op jit(solution)/shard_map/ppermute | solution.py:500
  37.4 5.4 %finish.1 = bf16[1,4,8,6144]{3,2,1,0:T(8,128)(2,1)} custom-call(s32[16]{0:T(128)S(1)} %copy-done.1, s32[16]{0:T(128)S(1)} %copy-done.2, bf16[384,256]{1,0:T(8,128)(2,1)S(1)} %stack.2.refs_0_, bf16[384,256]{1,0:T(8,128)(2,1)S(1)} %collective-permute-done.9.refs_1_, bf16[384,1152]{1,0:T(8,128)(2,1)S(1)} %wide.1.refs_2_, ...), custom_call_target="tpu_custom_call" | custom-call | flops 5520000000 | tf_op jit(solution)/shard_map/finish/pallas_call | solution.py:475
  (18 shorter events, 0.1 us)
Async XLA Ops:
  0.0 9.0 %copy-start.3 = (bf16[12,27,96]{2,1,0:T(8,128)(2,1)S(1)}, bf16[12,27,96]{2,1,0:T(8,128)(2,1)}, u32[]{:S(2)}) copy-start(bf16[12,27,96]{2,1,0:T(8,128)(2,1)} %param.16) | copy-start | bytes 186628
  1.9 10.4 %collective-permute-start = (bf16[96,256]{1,0:T(8,128)(2,1)S(1)}, bf16[96,256]{1,0:T(8,128)(2,1)S(1)}, u32[]{:S(2)}, u32[]{:S(2)}) collective-permute-start(bf16[96,256]{1,0:T(8,128)(2,1)S(1)} %get-tuple-element.22), channel_id=1, source_target_pairs={{0,8},{2,10},{4,12},{6,14},{8,16},{10,18},{12,20},{14,22},{16,24},... | collective-permute-start | bytes 147464 | tf_op jit(solution)/shard_map/ppermute | solution.py:492
  5.0 8.0 %collective-permute-start.1 = (bf16[96,256]{1,0:T(8,128)(2,1)S(1)}, bf16[96,256]{1,0:T(8,128)(2,1)S(1)}, u32[]{:S(2)}, u32[]{:S(2)}) collective-permute-start(bf16[96,256]{1,0:T(8,128)(2,1)S(1)} %get-tuple-element.23), channel_id=1, source_target_pairs={{0,16},{2,18},{4,20},{6,22},{8,24},{10,26},{12,28},{14,30},{16,0},... | collective-permute-start | bytes 147464 | tf_op jit(solution)/shard_map/ppermute | solution.py:492
  7.6 5.4 %collective-permute-start.2 = (bf16[96,256]{1,0:T(8,128)(2,1)S(1)}, bf16[96,256]{1,0:T(8,128)(2,1)S(1)}, u32[]{:S(2)}, u32[]{:S(2)}) collective-permute-start(bf16[96,256]{1,0:T(8,128)(2,1)S(1)} %get-tuple-element.24), channel_id=1, source_target_pairs={{0,24},{2,26},{4,28},{6,30},{8,0},{10,2},{12,4},{14,6},{16,8},{18,... | collective-permute-start | bytes 147464 | tf_op jit(solution)/shard_map/ppermute | solution.py:492
  9.2 3.1 %copy-start.4 = (f32[384]{0:T(512)S(1)}, f32[384]{0:T(512)}, u32[]{:S(2)}) copy-start(f32[384]{0:T(512)} %param.17) | copy-start | bytes 4612
  9.3 3.0 %copy-start.5 = (f32[192]{0:T(256)S(1)}, f32[192]{0:T(256)}, u32[]{:S(2)}) copy-start(f32[192]{0:T(256)} %param.18) | copy-start | bytes 2308
  9.3 6.9 %collective-permute-start.12 = (bf16[24,896]{1,0:T(8,128)(2,1)S(1)}, bf16[24,896]{1,0:T(8,128)(2,1)S(1)}, u32[]{:S(2)}, u32[]{:S(2)}) collective-permute-start(bf16[24,896]{1,0:T(8,128)(2,1)S(1)} %constant_dynamic-slice_fusion.refs_0_), channel_id=1, source_target_pairs={{0,6},{2,4},{4,2},{6,0},{8,14},{10,12},{12,10},{14,8},{16,22},{18,... | collective-permute-start | bytes 129032 | tf_op jit(solution)/shard_map/ppermute | solution.py:496
  11.8 5.3 %collective-permute-start.11 = (bf16[24,896]{1,0:T(8,128)(2,1)S(1)}, bf16[24,896]{1,0:T(8,128)(2,1)S(1)}, u32[]{:S(2)}, u32[]{:S(2)}) collective-permute-start(bf16[24,896]{1,0:T(8,128)(2,1)S(1)} %constant_dynamic-slice_fusion.refs_0_), channel_id=1, source_target_pairs={{0,4},{2,6},{4,0},{6,2},{8,12},{10,14},{12,8},{14,10},{16,20},{18,... | collective-permute-start | bytes 129032 | tf_op jit(solution)/shard_map/ppermute | solution.py:496
  12.4 4.7 %collective-permute-start.10 = (bf16[24,896]{1,0:T(8,128)(2,1)S(1)}, bf16[24,896]{1,0:T(8,128)(2,1)S(1)}, u32[]{:S(2)}, u32[]{:S(2)}) collective-permute-start(bf16[24,896]{1,0:T(8,128)(2,1)S(1)} %constant_dynamic-slice_fusion.refs_0_), channel_id=1, source_target_pairs={{0,2},{2,0},{4,6},{6,4},{8,10},{10,8},{12,14},{14,12},{16,18},{18,... | collective-permute-start | bytes 129032 | tf_op jit(solution)/shard_map/ppermute | solution.py:496
  13.2 6.7 %collective-permute-start.3 = (bf16[304,256]{1,0:T(8,128)(2,1)S(1)}, bf16[304,256]{1,0:T(8,128)(2,1)S(1)}, u32[]{:S(2)}, u32[]{:S(2)}) collective-permute-start(bf16[304,256]{1,0:T(8,128)(2,1)S(1)} %get-tuple-element.26), channel_id=1, source_target_pairs={{0,2},{2,0},{4,6},{6,4},{8,10},{10,8},{12,14},{14,12},{16,18},{18,... | collective-permute-start | bytes 466952 | tf_op jit(solution)/shard_map/ppermute | solution.py:496
  14.7 8.0 %collective-permute-start.4 = (bf16[304,256]{1,0:T(8,128)(2,1)S(1)}, bf16[304,256]{1,0:T(8,128)(2,1)S(1)}, u32[]{:S(2)}, u32[]{:S(2)}) collective-permute-start(bf16[304,256]{1,0:T(8,128)(2,1)S(1)} %get-tuple-element.27), channel_id=1, source_target_pairs={{0,4},{2,6},{4,0},{6,2},{8,12},{10,14},{12,8},{14,10},{16,20},{18,... | collective-permute-start | bytes 466952 | tf_op jit(solution)/shard_map/ppermute | solution.py:496
  16.2 6.5 %copy-start = (bf16[16,27,384]{2,0,1:T(8,128)(2,1)S(1)}, bf16[16,27,384]{2,0,1:T(8,128)(2,1)}, u32[]{:S(2)}) copy-start(bf16[16,27,384]{2,0,1:T(8,128)(2,1)} %param.14) | copy-start | bytes 995332
  16.2 6.5 %collective-permute-start.5 = (bf16[304,256]{1,0:T(8,128)(2,1)S(1)}, bf16[304,256]{1,0:T(8,128)(2,1)S(1)}, u32[]{:S(2)}, u32[]{:S(2)}) collective-permute-start(bf16[304,256]{1,0:T(8,128)(2,1)S(1)} %get-tuple-element.28), channel_id=1, source_target_pairs={{0,6},{2,4},{4,2},{6,0},{8,14},{10,12},{12,10},{14,8},{16,22},{18,... | collective-permute-start | bytes 466952 | tf_op jit(solution)/shard_map/ppermute | solution.py:496
  17.1 14.2 %collective-permute-start.15 = (bf16[4,24,896]{2,1,0:T(8,128)(2,1)S(1)}, bf16[4,24,896]{2,1,0:T(8,128)(2,1)S(1)}, u32[]{:S(2)}, u32[]{:S(2)}) collective-permute-start(bf16[4,24,896]{2,1,0:T(8,128)(2,1)S(1)} %bitcast.10), channel_id=1, source_target_pairs={{0,24},{2,26},{4,28},{6,30},{8,0},{10,2},{12,4},{14,6},{16,8},{18,... | collective-permute-start | bytes 516104 | tf_op jit(solution)/shard_map/ppermute | solution.py:492
  18.6 15.5 %collective-permute-start.14 = (bf16[4,24,896]{2,1,0:T(8,128)(2,1)S(1)}, bf16[4,24,896]{2,1,0:T(8,128)(2,1)S(1)}, u32[]{:S(2)}, u32[]{:S(2)}) collective-permute-start(bf16[4,24,896]{2,1,0:T(8,128)(2,1)S(1)} %bitcast.11), channel_id=1, source_target_pairs={{0,16},{2,18},{4,20},{6,22},{8,24},{10,26},{12,28},{14,30},{16,0},... | collective-permute-start | bytes 516104 | tf_op jit(solution)/shard_map/ppermute | solution.py:492
  19.9 14.2 %collective-permute-start.13 = (bf16[4,24,896]{2,1,0:T(8,128)(2,1)S(1)}, bf16[4,24,896]{2,1,0:T(8,128)(2,1)S(1)}, u32[]{:S(2)}, u32[]{:S(2)}) collective-permute-start(bf16[4,24,896]{2,1,0:T(8,128)(2,1)S(1)} %bitcast.12), channel_id=1, source_target_pairs={{0,8},{2,10},{4,12},{6,14},{8,16},{10,18},{12,20},{14,22},{16,24},... | collective-permute-start | bytes 516104 | tf_op jit(solution)/shard_map/ppermute | solution.py:492
  22.7 0.7 %copy-start.1 = (s32[16]{0:T(128)S(1)}, s32[16]{0:T(128)}, u32[]{:S(2)}) copy-start(s32[16]{0:T(128)} %frames.3) | copy-start | bytes 196
  22.7 0.7 %copy-start.2 = (s32[16]{0:T(128)S(1)}, s32[16]{0:T(128)}, u32[]{:S(2)}) copy-start(s32[16]{0:T(128)} %assign.3) | copy-start | bytes 196
  28.7 6.1 %collective-permute-start.6 = (bf16[96,256]{1,0:T(8,128)(2,1)S(1)}, bf16[96,256]{1,0:T(8,128)(2,1)S(1)}, u32[]{:S(2)}, u32[]{:S(2)}) collective-permute-start(bf16[96,256]{1,0:T(8,128)(2,1)S(1)} %get-tuple-element.30), channel_id=1, source_target_pairs={{0,8},{2,10},{4,12},{6,14},{8,16},{10,18},{12,20},{14,22},{16,24},... | collective-permute-start | bytes 147464 | tf_op jit(solution)/shard_map/ppermute | solution.py:492
  29.4 6.3 %collective-permute-start.7 = (bf16[96,256]{1,0:T(8,128)(2,1)S(1)}, bf16[96,256]{1,0:T(8,128)(2,1)S(1)}, u32[]{:S(2)}, u32[]{:S(2)}) collective-permute-start(bf16[96,256]{1,0:T(8,128)(2,1)S(1)} %get-tuple-element.31), channel_id=1, source_target_pairs={{0,16},{2,18},{4,20},{6,22},{8,24},{10,26},{12,28},{14,30},{16,0},... | collective-permute-start | bytes 147464 | tf_op jit(solution)/shard_map/ppermute | solution.py:492
  31.3 4.5 %collective-permute-start.8 = (bf16[96,256]{1,0:T(8,128)(2,1)S(1)}, bf16[96,256]{1,0:T(8,128)(2,1)S(1)}, u32[]{:S(2)}, u32[]{:S(2)}) collective-permute-start(bf16[96,256]{1,0:T(8,128)(2,1)S(1)} %get-tuple-element.32), channel_id=1, source_target_pairs={{0,24},{2,26},{4,28},{6,30},{8,0},{10,2},{12,4},{14,6},{16,8},{18,... | collective-permute-start | bytes 147464 | tf_op jit(solution)/shard_map/ppermute | solution.py:492
  34.6 2.8 %collective-permute-start.16 = (bf16[384,1152]{1,0:T(8,128)(2,1)S(1)}, bf16[384,1152]{1,0:T(8,128)(2,1)S(1)}, u32[]{:S(2)}, u32[]{:S(2)}) collective-permute-start(bf16[384,1152]{1,0:T(8,128)(2,1)S(1)} %wide.1.refs_2_), channel_id=1, source_target_pairs={{0,1},{1,0},{2,3},{3,2},{4,5},{5,4},{6,7},{7,6},{8,9},{9,8},{10,11... | collective-permute-start | bytes 2654216 | tf_op jit(solution)/shard_map/ppermute | solution.py:500
  35.8 1.6 %collective-permute-start.9 = (bf16[384,256]{1,0:T(8,128)(2,1)S(1)}, bf16[384,256]{1,0:T(8,128)(2,1)S(1)}, u32[]{:S(2)}, u32[]{:S(2)}) collective-permute-start(bf16[384,256]{1,0:T(8,128)(2,1)S(1)} %stack.2.refs_0_), channel_id=1, source_target_pairs={{0,1},{1,0},{2,3},{3,2},{4,5},{5,4},{6,7},{7,6},{8,9},{9,8},{10,11... | collective-permute-start | bytes 589832 | tf_op jit(solution)/shard_map/ppermute | solution.py:500
  35.9 0.7 %copy-start.6 = (f32[96]{0:T(128)S(1)}, f32[96]{0:T(128)}, u32[]{:S(2)}) copy-start(f32[96]{0:T(128)} %param.19) | copy-start | bytes 1156

commit v4 on v3

--- a/solution.py
+++ b/solution.py
@@ -122,10 +122,16 @@
 W_ROWS = 3 * IN_SH
 B_ROWS = LINE * W_ROWS + LINE * LINE
 WOUT_LANES = 896
+HALF_CH = C2 // 2
+FOLD = 9 * C3 // 8
 F32, BF16 = jnp.float32, jnp.bfloat16
 VMEM = functools.partial(pl.BlockSpec, memory_space=pltpu.VMEM)
 SMEM = functools.partial(pl.BlockSpec, memory_space=pltpu.SMEM)
 HBM = functools.partial(pl.BlockSpec, memory_space=pltpu.HBM)
+
+
+def in_hbm(*values):
+    return [pltpu.with_memory_space_constraint(v, pltpu.HBM) for v in values]
 
 
 def cost(us):
@@ -206,7 +212,7 @@
         cost_estimate=cost(2),
         compiler_params=pltpu.CompilerParams(vmem_limit_bytes=32 << 20),
         name="pack",
-    )(*(pltpu.with_memory_space_constraint(v, pltpu.HBM) for v in (offsets, assign, w_mid, latents)))
+    )(*in_hbm(offsets, assign, w_mid, latents))
 
 
 def join_kernel(*refs):
@@ -239,11 +245,16 @@
     )(*pieces)
 
 
-def mid_kernel(frames, assign, *refs):
-    parts, (win_ref, gain_ref), outs = refs[:PLANE], refs[PLANE : PLANE + 2], refs[PLANE + 2 : PLANE + 2 + LINE]
-    lt, xs, zlo, zhi, w1, act, wf = refs[PLANE + 2 + LINE :]
+def mid_kernel(frames_hbm, assign_hbm, win_hbm, gain_ref, *refs):
+    parts, outs = refs[:PLANE], refs[PLANE : PLANE + LINE]
+    lt, xs, tokens, shifted, w1, act, wf, frames, assign, sems = refs[PLANE + LINE :]
     z, q, _ = place()
     base = LINE * W_ROWS
+    moves = [(frames_hbm, frames), (assign_hbm, assign), (win_hbm, w1.at[0 : 27 * ZC])]
+    loads = [pltpu.make_async_copy(src, dst, sems.at[i]) for i, (src, dst) in enumerate(moves)]
+    for load in loads:
+        load.start()
+    w1[27 * ZC :, :] = jnp.zeros((512 - 27 * ZC, C1), BF16)
     for d in range(PLANE):
         part = parts[d][...].astype(F32)
         lt[...] = part[base:]
@@ -254,47 +265,48 @@
                 wf[b, pl.ds(pl.multiple_of(shard * IN_SH, 8), IN_SH), :] = part[at : at + IN_SH]
             for i in range(LINE):
                 xs[i, pl.ds(shard, 1), :] = lt[pl.ds(LINE * k + lax.rem(z + i, LINE), 1), :]
-    zero_rows = jnp.zeros((1, 6, WL, 640), BF16)
-    zero_cols = jnp.zeros((4, 1, WL, 640), BF16)
-    for ref in (zlo, zhi):
-        for i in range(LINE):
-            ref[i, 0:1] = zero_rows
-            ref[i, 1:2] = zero_rows
-            ref[i, 2:6, 0:1] = zero_cols
-            ref[i, 2:6, 5:6] = zero_cols
-    w1[...] = jnp.zeros((640, C1), BF16)
-    for n in range(9):
-        w1[64 * n : 64 * n + 48, :] = win_ref[48 * n : 48 * n + 48, :]
-    lane_n, row_l = iota((256, 640), 1), iota((256, 640), 0)
-    spread = ((row_l % ZC == lane_n % ZC) & (lane_n % 64 < 48) & (lane_n < 576)).astype(F32).astype(BF16)
-    tap_e = (lane_n % 64) // ZC
-    col = row_l % WL
-    from_left = (tap_e == 0) & (col > 0)
-    from_right = (tap_e == 2) & (col < WL - 1)
-    is_mid = tap_e == 1
-    low = lane_n % 128 < 64
-    pos16, shard16 = iota((256, 16), 0), iota((256, 16), 1)
-    pos, tok_l = iota((256, 256), 0).astype(F32), (iota((256, 256), 1) // ZC).astype(F32)
+    own_lane = iota((16, 16, 256), 1) == iota((16, 16, 256), 2) // ZC
+    repeat = (iota((256, 128), 0) % ZC == iota((256, 128), 1) % ZC).astype(F32).astype(BF16)
+    lane, col = iota((256, 128), 1), iota((256, 128), 0) % WL
+    inner_l, inner_r = col > 0, col < WL - 1
+    block = lane // ZC
+    tap_col = [(block + r) % 3 for r in range(3)]
+    lane1 = iota((1, 128), 1)
+    zero_rows = jnp.zeros((2, 6, WL, 128), BF16)
+    zero_cols = jnp.zeros((4, 1, WL, 128), BF16)
+    for load in loads[:2]:
+        load.wait()
     for i in range(LINE):
-        group = lax.rem(z + i, LINE) * PLANE + q
-        fill = frames[assign[group]] * (TOK // FMAX)
-        hit = (pos16 >= fill * shard16) & (pos16 < fill * (shard16 + 1))
-        first = jnp.sum(jnp.where(hit, (fill * shard16).astype(F32), 0.0), axis=1, keepdims=True)
-        rows = jnp.dot(hit.astype(F32).astype(BF16), xs[i].astype(BF16), preferred_element_type=F32)
-        own = jnp.where(pos - first == tok_l, rows, 0.0).astype(BF16)
-        wide = jnp.dot(own, spread, preferred_element_type=F32)
-        left, right = pltpu.roll(wide, 1, 0), pltpu.roll(wide, 255, 0)
-        cols = jnp.where(is_mid, wide, jnp.where(from_left, left, jnp.where(from_right, right, 0.0)))
-        zlo[i, 2:6, 1:5] = jnp.where(low, cols, 0.0).astype(BF16).reshape(4, 4, WL, 640)
-        zhi[i, 2:6, 1:5] = jnp.where(low, 0.0, cols).astype(BF16).reshape(4, 4, WL, 640)
-        taps = []
-        for j in range(5):
-            a0, b0 = divmod(2 * j, 3)
-            a1, b1 = divmod(min(2 * j + 1, 8), 3)
-            at = slice(128 * j, 128 * j + 128)
-            tile = zlo[i, a0 : a0 + 4, b0 : b0 + 4, :, at] + zhi[i, a1 : a1 + 4, b1 : b1 + 4, :, at]
-            taps.append(tile.reshape(256, 128))
-        h = jnp.dot(jnp.concatenate(taps, axis=1), w1[...], preferred_element_type=F32)
+        fill = frames[assign[lax.rem(z + i, LINE) * PLANE + q]] * (TOK // FMAX)
+        spread = jnp.where(own_lane, jnp.broadcast_to(xs[i][:, None, :], (16, 16, 256)), 0.0)
+        rows = jnp.dot(spread.reshape(256, 256).astype(BF16), repeat, preferred_element_type=F32)
+        tokens[i] = jnp.zeros((288, 128), F32)
+        for shard in range(16):
+            tokens[i, pl.ds(8 + shard * fill, TOK), :] = rows[TOK * shard : TOK * (shard + 1)]
+        tokens[i, pl.ds(8 + 16 * fill, TOK), :] = jnp.zeros((TOK, 128), F32)
+        here = tokens[i, 8:264, :]
+        left = jnp.where(inner_l, tokens[i, 7:263, :], 0.0)
+        right = jnp.where(inner_r, tokens[i, 9:265, :], 0.0)
+        for r in range(3):
+            v = jnp.where(tap_col[r] == 0, left, jnp.where(tap_col[r] == 1, here, right)).astype(BF16)
+            shifted[i, r, 0:2] = zero_rows
+            shifted[i, r, 2:6, 0:1] = zero_cols
+            shifted[i, r, 2:6, 5:6] = zero_cols
+            shifted[i, r, 2:6, 1:5] = v.reshape(4, 4, WL, 128)
+    for load in loads[2:]:
+        load.wait()
+    for i in range(LINE):
+        tiles = []
+        for j in range(4):
+            tile = None
+            for tap in range(8 * j // 3, min(8 * j + 7, 26) // 3 + 1):
+                a, b = divmod(tap, 3)
+                lo, hi = max(3 * tap - 8 * j, 0) * ZC, min(3 * tap + 3 - 8 * j, 8) * ZC
+                keep = ((lane1 >= lo) & (lane1 < hi)).astype(F32).astype(BF16)
+                term = shifted[i, 8 * j % 3, a : a + 4, b : b + 4].reshape(256, 128) * keep
+                tile = term if tile is None else tile + term
+            tiles.append(tile)
+        h = jnp.dot(jnp.concatenate(tiles, axis=1), w1[...], preferred_element_type=F32)
         scale = lax.rsqrt(jnp.mean(h * h, axis=1, keepdims=True) + 1e-6)
         act[256 * i : 256 * i + 256, :] = silu(h * scale * gain_ref[...]).astype(BF16)
     lanes = LINE * 256
@@ -329,49 +341,83 @@
     return pl.pallas_call(
         mid_kernel,
         out_shape=[out] * LINE,
-        in_specs=[SMEM(), SMEM()] + [VMEM()] * (PLANE + 2),
+        in_specs=[HBM()] * 3 + [VMEM()] * (PLANE + 1),
         out_specs=[VMEM()] * LINE,
         scratch_shapes=[
             pltpu.VMEM((LINE * LINE, 256), F32),
             pltpu.VMEM((LINE, 16, 256), F32),
-            pltpu.VMEM((LINE, 6, 6, WL, 640), BF16),
-            pltpu.VMEM((LINE, 6, 6, WL, 640), BF16),
-            pltpu.VMEM((640, C1), BF16),
+            pltpu.VMEM((LINE, 288, 128), F32),
+            pltpu.VMEM((LINE, 3, 6, 6, WL, 128), BF16),
+            pltpu.VMEM((512, C1), BF16),
             pltpu.VMEM((LINE * 256, C1), BF16),
             pltpu.VMEM((3, C1, 256), F32),
+            pltpu.SMEM(frames.shape, jnp.int32),
+            pltpu.SMEM(assign.shape, jnp.int32),
+            pltpu.SemaphoreType.DMA((3,)),
         ],
         compiler_params=pltpu.CompilerParams(vmem_limit_bytes=48 << 20),
         cost_estimate=cost(5),
         name="mid",
-    )(frames, assign, *parts, w_in, gain_in)
-
-
-def wide_kernel(*refs):
-    parts, out, wf = refs[:LINE], refs[LINE], refs[LINE + 1]
+    )(*in_hbm(frames, assign, w_in), gain_in, *parts)
+
+
+def wide_kernel(frames_hbm, assign_hbm, gmid_hbm, gout_hbm, *refs):
+    parts, (out, gmid_out, gout_out, limit_out) = refs[:LINE], refs[LINE : LINE + 4]
+    rows, wf, gmid_ref, gout_ref, frames, assign, sems = refs[LINE + 4 :]
+    moves = [(gmid_hbm, gmid_ref), (gout_hbm, gout_ref), (frames_hbm, frames), (assign_hbm, assign)]
+    loads = [pltpu.make_async_copy(src, dst, sems.at[i]) for i, (src, dst) in enumerate(moves)]
+    for load in loads:
+        load.start()
     z, q, _ = place()
-    wf[...] = jnp.zeros((384, 1152), F32)
+    wf[...] = jnp.zeros((9, 3 * HALF_CH, 128), F32)
     for k in range(LINE):
         for d in range(PLANE):
             shard = lax.rem(z - k + LINE, LINE) * PLANE + (q ^ d)
-            at = pl.multiple_of(shard * 8, 8)
-            part = parts[k][d].astype(F32)
-            for r in range(3):
-                for j in range(9):
-                    wf[pl.ds(128 * r + at, 8), 128 * j : 128 * j + C3] = part[8 * r : 8 * r + 8, C3 * j : C3 * (j + 1)]
-    out[...] = wf[...].astype(BF16)
-
-
-def wide(parts):
+            part = parts[k][16 * d : 16 * d + 16, :].astype(F32)
+            rows[0:16, : 9 * C3] = part[:, : 9 * C3]
+            for g in range(8):
+                rows[16:18, FOLD * g : FOLD * (g + 1)] = part[2 * g : 2 * g + 2, 9 * C3 : 9 * C3 + FOLD]
+            for j in range(9):
+                tap = rows[:, C3 * j : C3 * (j + 1)]
+                for b in range(3):
+                    wf[j, pl.ds(HALF_CH * b + 6 * shard, 6), :C3] = tap[6 * b : 6 * b + 6]
+    for j in range(9):
+        out[:, 128 * j : 128 * (j + 1)] = wf[j].astype(BF16)
+    for load in loads:
+        load.wait()
+    row, channel = iota((C2, C2), 0), iota((C2, C2), 1)
+    wanted = (row % HALF_CH) // 6 * MID_SH + row // HALF_CH * 6 + row % 6
+    column = jnp.sum(jnp.where(channel == wanted, gmid_ref[...], 0.0), axis=1, keepdims=True)
+    gmid_out[...] = jnp.broadcast_to(column, (C2, 128))
+    gout_out[...] = jnp.zeros((1, 128), F32)
+    gout_out[:, :C3] = gout_ref[...]
+    limit_out[...] = jnp.full((1, 128), frames[assign[z * PLANE + q]], jnp.int32).astype(F32)
+
+
+def wide(frames, assign, gain_mid, gain_out, parts):
     return pl.pallas_call(
         wide_kernel,
-        out_shape=jax.ShapeDtypeStruct((384, 1152), BF16),
-        in_specs=[VMEM()] * LINE,
-        out_specs=VMEM(),
-        scratch_shapes=[pltpu.VMEM((384, 1152), F32)],
-        cost_estimate=cost(0.5),
+        out_shape=[
+            jax.ShapeDtypeStruct((3 * HALF_CH, 1152), BF16),
+            jax.ShapeDtypeStruct((C2, 128), F32),
+            jax.ShapeDtypeStruct((1, 128), F32),
+            jax.ShapeDtypeStruct((1, 128), F32),
+        ],
+        in_specs=[HBM()] * 4 + [VMEM()] * LINE,
+        out_specs=[VMEM()] * 4,
+        scratch_shapes=[
+            pltpu.VMEM((24, WOUT_LANES), F32),
+            pltpu.VMEM((9, 3 * HALF_CH, 128), F32),
+            pltpu.VMEM(gain_mid.shape, F32),
+            pltpu.VMEM(gain_out.shape, F32),
+            pltpu.SMEM(frames.shape, jnp.int32),
+            pltpu.SMEM(assign.shape, jnp.int32),
+            pltpu.SemaphoreType.DMA((4,)),
+        ],
+        cost_estimate=cost(0.01),
         compiler_params=pltpu.CompilerParams(vmem_limit_bytes=48 << 20),
         name="wide",
-    )(*parts)
+    )(*in_hbm(frames, assign, gain_mid, gain_out), *parts)
 
 
 def stack_kernel(*refs):
@@ -380,39 +426,46 @@
         refs[-1][rows * i : rows * (i + 1), :] = ref[...]
 
 
-def stack(parts):
+def stack(parts, us=5):
     rows, lanes = parts[0].shape
     return pl.pallas_call(
         stack_kernel,
         out_shape=jax.ShapeDtypeStruct((len(parts) * rows, lanes), BF16),
         in_specs=[VMEM()] * len(parts),
         out_specs=VMEM(),
-        cost_estimate=cost(5),
+        cost_estimate=cost(us),
         compiler_params=pltpu.CompilerParams(vmem_limit_bytes=32 << 20),
         name="stack",
     )(*parts)
 
 
-def out_kernel(frames, assign, *refs):
-    own, other, w_own, w_other, gmid_ref, gout_ref, out_ref, hid, lhs, prod = refs
+def out_kernel(own, other, w_own, w_other, gmid_ref, gout_ref, limit_ref, out_ref, hid, lhs, prod, w_all):
     z, q, c = place()
-    count = frames[assign[z * PLANE + q]]
-    hid[...] = jnp.zeros((4, 256, 256), F32)
+    for b in range(3):
+        for side, half in ((c, w_own), (1 - c, w_other)):
+            at = pl.multiple_of(256 * b + HALF_CH * side, 32)
+            w_all[pl.ds(at, HALF_CH), :] = half[HALF_CH * b : HALF_CH * (b + 1), :]
+        w_all[256 * b + C2 : 256 * (b + 1), :] = jnp.zeros((64, 1152), BF16)
+    lhs[:, :, :, :] = jnp.zeros(lhs.shape, BF16)
     for side, group in ((c, own), (1 - c, other)):
         for k in range(LINE):
             block = lax.rem(z - k + LINE, LINE) * 2 + side
             part = group[96 * k : 96 * k + 96, :].astype(F32)
             for p in range(4):
                 for half in range(2):
-                    at = pl.multiple_of((block * 2 + half) * 8, 8)
-                    first = OUT_BLK * p + MID_SH * half
-                    hid[p, pl.ds(at, 8), :] = part[first : first + 8]
-                    hid[p, pl.ds(128 + at, 4), :] = part[first + 8 : first + MID_SH]
+                    for shard in range(2):
+                        first = OUT_BLK * p + MID_SH * shard + 6 * half
+                        at = HALF_CH * half + 12 * block + 6 * shard
+                        for tp in range(2):
+                            hid[p, tp, pl.ds(at, 6), :] = part[first : first + 6, 128 * tp : 128 * tp + 128]
     acts = []
     for p in range(4):
-        h = hid[p]
-        scale = lax.rsqrt(jnp.sum(h * h, axis=0, keepdims=True) * (1.0 / C2) + 1e-6)
-        acts.append(silu(h * scale * gmid_ref[...]).astype(BF16))
+        halves = []
+        for tp in range(2):
+            h = hid[p, tp]
+            scale = lax.rsqrt(jnp.sum(h * h, axis=0, keepdims=True) * (1.0 / C2) + 1e-6)
+            halves.append(silu(h * scale * gmid_ref[...]).astype(BF16))
+        acts.append(halves)
     r, l = iota((256, 256), 0), iota((256, 256), 1)
     same = (r // 8) == ((l // 64) % 2) * WL + l % WL
     mid_row = 2 * ((l // WL) % 4) + l // 128
@@ -421,16 +474,18 @@
         pick = (same & (mid_row == wanted)).astype(F32).astype(BF16)
         for tp in range(2):
             for px in range(2):
-                src = jnp.concatenate([acts[2 * py + px][:, 128 * tp : 128 * tp + 128] for py in range(2)], axis=1)
-                lhs[tp, px, :, 256 * b : 256 * b + 256] = dot_nt(pick, src).astype(BF16)
-    for tp in range(2):
-        for px in range(2):
-            prod[tp, px] = jnp.dot(
-                lhs[tp, px, :, pl.ds(pl.multiple_of(c * 384, 128), 384)], w_own[...], preferred_element_type=F32
-            ) + jnp.dot(
-                lhs[tp, px, :, pl.ds(pl.multiple_of((1 - c) * 384, 128), 384)], w_other[...], preferred_element_type=F32
-            )
+                src = jnp.concatenate([acts[2 * py + px][tp] for py in range(2)], axis=1)
+                rows = dot_nt(pick, src).astype(BF16)
+                for half in range(2):
+                    lhs[2 * tp + half, px, :, 256 * b : 256 * b + C2] = rows[128 * half : 128 * half + 128]
+    prod[0:2] = jnp.dot(lhs[0:2].reshape(512, 768), w_all[...], preferred_element_type=F32).reshape(2, 2, 128, 1152)
+    for t in (2, 3):
+        at = 384 * (t - 1)
+        prod[t, :, :, at:] = jnp.dot(
+            lhs[t].reshape(256, 768), w_all[:, at:], preferred_element_type=F32
+        ).reshape(2, 128, 1152 - at)
     lane = iota((1, 8, 128), 2)
+    limit = limit_ref[...]
     below = [lane < 128 - 32 * i for i in range(4)]
     for t in range(FMAX):
         sums = []
@@ -443,7 +498,7 @@
                     if s < 0:
                         continue
                     at = 128 * (3 * a + e)
-                    term = prod[s // 2, px, 128 * (s % 2) : 128 * (s % 2) + 128, at : at + 128].reshape(WL, 8, 128)
+                    term = prod[s, px, :, at : at + 128].reshape(WL, 8, 128)
                     total = term if total is None else total + term
                 row.append(total)
             sums.append(row)
@@ -459,7 +514,7 @@
         vals = []
         for i, o in enumerate(outs):
             scale = lax.rsqrt(jnp.sum(o * o, axis=2, keepdims=True) * (1.0 / C3) + 1e-6)
-            v = jnp.where(t < count, silu(o * scale * gout_ref[...]), 0.0)
+            v = jnp.where(t < limit, silu(o * scale * gout_ref[...]), 0.0)
             vals.append(pltpu.roll(v, 128 - 32 * i, 2) if i else v)
         tiles = [
             jnp.where(lane < 96, vals[0], vals[1]),
@@ -471,21 +526,22 @@
             out_ref[0, t, :, 384 * x : 384 * x + 384] = both.astype(BF16)
 
 
-def finish(frames, assign, *rest):
+def finish(*rest):
     return pl.pallas_call(
         out_kernel,
         out_shape=jax.ShapeDtypeStruct((1, FMAX, 4 * RL, 4 * WL * C3), BF16),
-        in_specs=[SMEM(), SMEM()] + [VMEM()] * len(rest),
+        in_specs=[VMEM()] * len(rest),
         out_specs=VMEM(),
         scratch_shapes=[
-            pltpu.VMEM((4, 256, 256), F32),
-            pltpu.VMEM((2, 2, 256, 768), BF16),
-            pltpu.VMEM((2, 2, 256, 1152), F32),
+            pltpu.VMEM((4, 2, C2, 128), F32),
+            pltpu.VMEM((4, 2, 128, 768), BF16),
+            pltpu.VMEM((4, 2, 128, 1152), F32),
+            pltpu.VMEM((768, 1152), BF16),
         ],
         compiler_params=pltpu.CompilerParams(vmem_limit_bytes=48 << 20),
         cost_estimate=cost(4.8),
         name="finish",
-    )(frames, assign, *rest)
+    )(*rest)
 
 
 def along_z(value, step):
@@ -506,19 +562,17 @@
     pieces = [pieces[0]] + [along_z(pieces[k], k) for k in range(1, LINE)]
     parts = join(pieces)
     parts = [parts[0]] + [in_plane(parts[d], d) for d in range(1, PLANE)]
-    rows = w_out.reshape(MID_SH, 3, 3, 3, C3).transpose(2, 0, 1, 3, 4).reshape(3, MID_SH, 9 * C3)
-    rows = jnp.pad(rows, ((0, 0), (0, 16 - MID_SH), (0, WOUT_LANES - 9 * C3))).reshape(48, WOUT_LANES)
-    half = lax.dynamic_slice_in_dim(rows, core * 24, 24, axis=0)
-    plane = stack([half] + [in_plane(half, d) for d in range(1, PLANE)]).reshape(PLANE, 24, WOUT_LANES)
+    rows = lax.dynamic_slice_in_dim(w_out, core * 6, 6, axis=0)
+    rows = rows.reshape(6, 3, 3, 3, C3).transpose(2, 0, 1, 3, 4).reshape(18, 9 * C3)
+    fold = rows[16:].reshape(2, 8, FOLD).transpose(1, 0, 2).reshape(16, FOLD)
+    half = jnp.pad(jnp.concatenate([rows[:16], fold], axis=1), ((0, 0), (0, 1024 - 9 * C3 - FOLD)))
+    plane = stack([half] + [in_plane(half, d) for d in range(1, PLANE)])
     own = [plane] + [along_z(plane, k) for k in range(1, LINE)]
     hidden = mid(frames, assign, parts, w_in.transpose(1, 0, 2).reshape(27 * ZC, C1), gain_in[None, :])
     own, _ = lax.optimization_barrier((own, hidden[0]))
-    w_last = wide(own)
-    hidden = stack([hidden[0]] + [along_z(hidden[k], k) for k in range(1, LINE)])
-    gmid = jnp.pad(gain_mid.reshape(16, MID_SH), ((0, 0), (0, 16 - MID_SH)))
-    gmid = jnp.concatenate([gmid[:, :8], gmid[:, 8:]]).reshape(256, 1)
-    gout = jnp.pad(gain_out, (0, 128 - C3)).reshape(1, 128)
-    return finish(frames, assign, hidden, other_core(hidden), w_last, other_core(w_last), gmid, gout)
+    w_last, gmid, gout, limit = wide(frames, assign, gain_mid[None, :], gain_out[None, :], own)
+    hidden = stack([hidden[0]] + [along_z(hidden[k], k) for k in range(1, LINE)], 30)
+    return finish(hidden, other_core(hidden), w_last, other_core(w_last), gmid, gout, limit)
 
 
 def solution(mesh):

time: 42.9 us -> 39.7 us (0.925)
  local copies, waits for them, and re-layouts: 1.76 us -> 0.27 us
  Pallas kernels: 13.3 us -> 12.1 us
  waiting for transfers between devices: 6.13 us -> 5.01 us
  starting transfers between devices: 21.4 us -> 21.9 us
    ppermute x9, waiting for transfers between devices: 2.53 us -> 0.59 us  [along_z(): lax.ppermute(value, 'grp', [(g, (g + PLANE * step) % (LINE * PLANE)) for...]
    pallas_call x1, Pallas kernels: 5.38 us -> 3.77 us  [finish(): pl.pallas_call(out_kernel, out_shape=jax.ShapeDtypeStruct((1, FMAX, 4 * R...]
    unnamed x14 -> x5, local copies, waits for them, and re-layouts: 1.24 us -> 0.03 us
    ppermute x2, waiting for transfers between devices: 0.85 us -> 1.78 us  [other_core(): return lax.ppermute(value, 'row', [(0, 1), (1, 0)])]
    ppermute x2, starting transfers between devices: 0.14 us -> 0.61 us  [other_core(): return lax.ppermute(value, 'row', [(0, 1), (1, 0)])]
  transfers between devices with their start and end apart: 17 -> 17, of which waited for: 5 -> 4; matrix products, arithmetic and copies ran while one was open for 1% -> 1% of each run, Pallas kernels for 14% -> 16%
where the time goes in v4:
time: 39.7 us; the launch traced here: 39.5 us
  starting transfers between devices  21.9 us (55%)
  Pallas kernels  12.1 us (30%)
  waiting for transfers between devices  5.01 us (13%)
    ppermute x9, starting transfers between devices, along_z(): lax.ppermute(value, 'grp', [(g, (g + PLANE * step) % (LINE * PLANE)) for...  13.9 us
    ppermute x6, starting transfers between devices, in_plane(): lax.ppermute(value, 'grp', [(g, g ^ flip) for g in range(LINE * PLANE)])  7.44 us
    pallas_call x1, Pallas kernels, finish(): pl.pallas_call(out_kernel, out_shape=jax.ShapeDtypeStruct((1, FMAX, 4 * R...  3.77 us
    pallas_call x1, Pallas kernels, mid(): pl.pallas_call(mid_kernel, out_shape=[out] * LINE, in_specs=[HBM()] * 3 +...  3.68 us
    ppermute x6, waiting for transfers between devices, in_plane(): lax.ppermute(value, 'grp', [(g, g ^ flip) for g in range(LINE * PLANE)])  2.64 us
    pallas_call x1, Pallas kernels, wide(): pl.pallas_call(wide_kernel, out_shape=[jax.ShapeDtypeStruct((3 * HALF_CH,...  2.54 us
    pallas_call x1, Pallas kernels, pack(): pl.pallas_call(pack_kernel, out_shape=[piece] * LINE, in_specs=[HBM()] *...  1.93 us
    ppermute x2, waiting for transfers between devices, other_core(): return lax.ppermute(value, 'row', [(0, 1), (1, 0)])  1.78 us
  transfers between devices with their start and end apart: 17, of which 4 were waited for; matrix products, arithmetic and copies ran while one was open for 1% of the time, Pallas kernels for 16%

profile of v4, /device:TPU:0, one launch (start us, length us, event | category | flops | bytes accessed | tf_op | source)
XLA Modules:
  0.0 39.5 jit_solution(17008599151107916033)
XLA Ops:
  0.0 0.0 copy-start
  0.0 1.9 %pack.1 = (bf16[96,256]{1,0:T(8,128)(2,1)S(1)}, bf16[96,256]{1,0:T(8,128)(2,1)S(1)}, bf16[96,256]{1,0:T(8,128)(2,1)S(1)}, bf16[96,256]{1,0:T(8,128)(2,1)S(1)}) custom-call(s32[16]{0:T(128)} %offsets_hbm.1, s32[16]{0:T(128)} %assign_hbm.5, bf16[27,24,192]{2,1,0:T(8,128)(2,1)} %bitcast.16, bf16[1,4096]{1,0:T(2,128)(2,1)} %lat_hbm.1), custom_call_target="tpu_custom_call" | custom-call | flops 2300000000 | tf_op jit(solution)/shard_map/pack/pallas_call | solution.py:197
  1.9 3.1 %collective-permute-start = (bf16[96,256]{1,0:T(8,128)(2,1)S(1)}, bf16[96,256]{1,0:T(8,128)(2,1)S(1)}, u32[]{:S(2)}, u32[]{:S(2)}) collective-permute-start(bf16[96,256]{1,0:T(8,128)(2,1)S(1)} %get-tuple-element.26), channel_id=1, source_target_pairs={{0,8},{2,10},{4,12},{6,14},{8,16},{10,18},{12,20},{14,22},{16,24},... | collective-permute-start | bytes 147464 | tf_op jit(solution)/shard_map/ppermute | solution.py:548
  5.0 2.6 %collective-permute-start.1 = (bf16[96,256]{1,0:T(8,128)(2,1)S(1)}, bf16[96,256]{1,0:T(8,128)(2,1)S(1)}, u32[]{:S(2)}, u32[]{:S(2)}) collective-permute-start(bf16[96,256]{1,0:T(8,128)(2,1)S(1)} %get-tuple-element.27), channel_id=1, source_target_pairs={{0,16},{2,18},{4,20},{6,22},{8,24},{10,26},{12,28},{14,30},{16,0},... | collective-permute-start | bytes 147464 | tf_op jit(solution)/shard_map/ppermute | solution.py:548
  7.6 1.3 %collective-permute-start.2 = (bf16[96,256]{1,0:T(8,128)(2,1)S(1)}, bf16[96,256]{1,0:T(8,128)(2,1)S(1)}, u32[]{:S(2)}, u32[]{:S(2)}) collective-permute-start(bf16[96,256]{1,0:T(8,128)(2,1)S(1)} %get-tuple-element.28), channel_id=1, source_target_pairs={{0,24},{2,26},{4,28},{6,30},{8,0},{10,2},{12,4},{14,6},{16,8},{18,... | collective-permute-start | bytes 147464 | tf_op jit(solution)/shard_map/ppermute | solution.py:548
  9.0 0.0 copy-done
  9.0 0.1 reshape.17
  9.2 0.1 reshape.18
  9.3 0.0 copy-start.1
  9.3 0.1 fusion.2.refs_0_
  9.3 2.5 %collective-permute-start.12 = (bf16[16,1024]{1,0:T(8,128)(2,1)S(1)}, bf16[16,1024]{1,0:T(8,128)(2,1)S(1)}, u32[]{:S(2)}, u32[]{:S(2)}) collective-permute-start(bf16[16,1024]{1,0:T(8,128)(2,1)S(1)} %fusion.2.refs_0_), channel_id=1, source_target_pairs={{0,6},{2,4},{4,2},{6,0},{8,14},{10,12},{12,10},{14,8},{16,22},{18,... | collective-permute-start | bytes 98312 | tf_op jit(solution)/shard_map/ppermute | solution.py:552
  11.8 0.5 %collective-permute-start.11 = (bf16[16,1024]{1,0:T(8,128)(2,1)S(1)}, bf16[16,1024]{1,0:T(8,128)(2,1)S(1)}, u32[]{:S(2)}, u32[]{:S(2)}) collective-permute-start(bf16[16,1024]{1,0:T(8,128)(2,1)S(1)} %fusion.2.refs_0_), channel_id=1, source_target_pairs={{0,4},{2,6},{4,0},{6,2},{8,12},{10,14},{12,8},{14,10},{16,20},{18,... | collective-permute-start | bytes 98312 | tf_op jit(solution)/shard_map/ppermute | solution.py:552
  12.3 0.0 copy-done.1
  12.3 0.0 collective-permute-done.refs_1_
  12.3 0.6 %collective-permute-start.10 = (bf16[16,1024]{1,0:T(8,128)(2,1)S(1)}, bf16[16,1024]{1,0:T(8,128)(2,1)S(1)}, u32[]{:S(2)}, u32[]{:S(2)}) collective-permute-start(bf16[16,1024]{1,0:T(8,128)(2,1)S(1)} %fusion.2.refs_0_), channel_id=1, source_target_pairs={{0,2},{2,0},{4,6},{6,4},{8,10},{10,8},{12,14},{14,12},{16,18},{18,... | collective-permute-start | bytes 98312 | tf_op jit(solution)/shard_map/ppermute | solution.py:552
  12.9 0.0 collective-permute-done.1.refs_2_
  12.9 0.0 collective-permute-done.2.refs_3_
  12.9 0.1 join.1
  13.1 1.6 %collective-permute-start.3 = (bf16[304,256]{1,0:T(8,128)(2,1)S(1)}, bf16[304,256]{1,0:T(8,128)(2,1)S(1)}, u32[]{:S(2)}, u32[]{:S(2)}) collective-permute-start(bf16[304,256]{1,0:T(8,128)(2,1)S(1)} %get-tuple-element.30), channel_id=1, source_target_pairs={{0,2},{2,0},{4,6},{6,4},{8,10},{10,8},{12,14},{14,12},{16,18},{18,... | collective-permute-start | bytes 466952 | tf_op jit(solution)/shard_map/ppermute | solution.py:552
  14.6 1.5 %collective-permute-start.4 = (bf16[304,256]{1,0:T(8,128)(2,1)S(1)}, bf16[304,256]{1,0:T(8,128)(2,1)S(1)}, u32[]{:S(2)}, u32[]{:S(2)}) collective-permute-start(bf16[304,256]{1,0:T(8,128)(2,1)S(1)} %get-tuple-element.31), channel_id=1, source_target_pairs={{0,4},{2,6},{4,0},{6,2},{8,12},{10,14},{12,8},{14,10},{16,20},{18,... | collective-permute-start | bytes 466952 | tf_op jit(solution)/shard_map/ppermute | solution.py:552
  16.1 0.0 collective-permute-done.12.refs_3_
  16.1 0.8 %collective-permute-start.5 = (bf16[304,256]{1,0:T(8,128)(2,1)S(1)}, bf16[304,256]{1,0:T(8,128)(2,1)S(1)}, u32[]{:S(2)}, u32[]{:S(2)}) collective-permute-start(bf16[304,256]{1,0:T(8,128)(2,1)S(1)} %get-tuple-element.32), channel_id=1, source_target_pairs={{0,6},{2,4},{4,2},{6,0},{8,14},{10,12},{12,10},{14,8},{16,22},{18,... | collective-permute-start | bytes 466952 | tf_op jit(solution)/shard_map/ppermute | solution.py:552
  17.0 0.0 collective-permute-done.11.refs_2_
  17.0 0.0 collective-permute-done.10.refs_1_
  17.0 1.6 %collective-permute-start.15 = (bf16[64,1024]{1,0:T(8,128)(2,1)S(1)}, bf16[64,1024]{1,0:T(8,128)(2,1)S(1)}, u32[]{:S(2)}, u32[]{:S(2)}) collective-permute-start(bf16[64,1024]{1,0:T(8,128)(2,1)S(1)} %stack.3.refs_0_), channel_id=1, source_target_pairs={{0,24},{2,26},{4,28},{6,30},{8,0},{10,2},{12,4},{14,6},{16,8},{18,... | collective-permute-start | bytes 393224 | tf_op jit(solution)/shard_map/ppermute | solution.py:548
  18.6 0.5 %collective-permute-start.14 = (bf16[64,1024]{1,0:T(8,128)(2,1)S(1)}, bf16[64,1024]{1,0:T(8,128)(2,1)S(1)}, u32[]{:S(2)}, u32[]{:S(2)}) collective-permute-start(bf16[64,1024]{1,0:T(8,128)(2,1)S(1)} %stack.3.refs_0_), channel_id=1, source_target_pairs={{0,16},{2,18},{4,20},{6,22},{8,24},{10,26},{12,28},{14,30},{16,0},... | collective-permute-start | bytes 393224 | tf_op jit(solution)/shard_map/ppermute | solution.py:548
  19.1 0.5 %collective-permute-done.3.refs_1_ = bf16[304,256]{1,0:T(8,128)(2,1)S(1)} collective-permute-done((bf16[304,256]{1,0:T(8,128)(2,1)S(1)}, bf16[304,256]{1,0:T(8,128)(2,1)S(1)}, u32[]{:S(2)}, u32[]{:S(2)}) %collective-permute-start.3) | collective-permute-done | bytes 155680 | tf_op jit(solution)/shard_map/ppermute | solution.py:552
  19.6 0.8 %collective-permute-start.13 = (bf16[64,1024]{1,0:T(8,128)(2,1)S(1)}, bf16[64,1024]{1,0:T(8,128)(2,1)S(1)}, u32[]{:S(2)}, u32[]{:S(2)}) collective-permute-start(bf16[64,1024]{1,0:T(8,128)(2,1)S(1)} %stack.3.refs_0_), channel_id=1, source_target_pairs={{0,8},{2,10},{4,12},{6,14},{8,16},{10,18},{12,20},{14,22},{16,24},... | collective-permute-start | bytes 393224 | tf_op jit(solution)/shard_map/ppermute | solution.py:548
  20.5 2.1 %collective-permute-done.4.refs_2_ = bf16[304,256]{1,0:T(8,128)(2,1)S(1)} collective-permute-done((bf16[304,256]{1,0:T(8,128)(2,1)S(1)}, bf16[304,256]{1,0:T(8,128)(2,1)S(1)}, u32[]{:S(2)}, u32[]{:S(2)}) %collective-permute-start.4) | collective-permute-done | bytes 155680 | tf_op jit(solution)/shard_map/ppermute | solution.py:552
  22.6 0.0 collective-permute-done.5.refs_3_
  22.6 3.7 %mid.1 = (bf16[96,256]{1,0:T(8,128)(2,1)S(1)}, bf16[96,256]{1,0:T(8,128)(2,1)S(1)}, bf16[96,256]{1,0:T(8,128)(2,1)S(1)}, bf16[96,256]{1,0:T(8,128)(2,1)S(1)}) custom-call(s32[16]{0:T(128)} %frames_hbm.3, s32[16]{0:T(128)} %assign_hbm.5, bf16[432,384]{1,0:T(8,128)(2,1)} %bitcast.17, f32[1,384]{1,0:T(1,128)S(1)} %broadcast_in_dim.9.gain_ref, ...), custom_call_target="tpu_custom_call" | custom-call | flops 5750000128 | tf_op jit(solution)/shard_map/mid/pallas_call | solution.py:341
  26.2 0.8 %collective-permute-start.6 = (bf16[96,256]{1,0:T(8,128)(2,1)S(1)}, bf16[96,256]{1,0:T(8,128)(2,1)S(1)}, u32[]{:S(2)}, u32[]{:S(2)}) collective-permute-start(bf16[96,256]{1,0:T(8,128)(2,1)S(1)} %get-tuple-element.34), channel_id=1, source_target_pairs={{0,8},{2,10},{4,12},{6,14},{8,16},{10,18},{12,20},{14,22},{16,24},... | collective-permute-start | bytes 147464 | tf_op jit(solution)/shard_map/ppermute | solution.py:548
  27.0 2.0 %collective-permute-start.7 = (bf16[96,256]{1,0:T(8,128)(2,1)S(1)}, bf16[96,256]{1,0:T(8,128)(2,1)S(1)}, u32[]{:S(2)}, u32[]{:S(2)}) collective-permute-start(bf16[96,256]{1,0:T(8,128)(2,1)S(1)} %get-tuple-element.35), channel_id=1, source_target_pairs={{0,16},{2,18},{4,20},{6,22},{8,24},{10,26},{12,28},{14,30},{16,0},... | collective-permute-start | bytes 147464 | tf_op jit(solution)/shard_map/ppermute | solution.py:548
  29.0 0.0 collective-permute-done.15.refs_3_
  29.0 1.2 %collective-permute-start.8 = (bf16[96,256]{1,0:T(8,128)(2,1)S(1)}, bf16[96,256]{1,0:T(8,128)(2,1)S(1)}, u32[]{:S(2)}, u32[]{:S(2)}) collective-permute-start(bf16[96,256]{1,0:T(8,128)(2,1)S(1)} %get-tuple-element.36), channel_id=1, source_target_pairs={{0,24},{2,26},{4,28},{6,30},{8,0},{10,2},{12,4},{14,6},{16,8},{18,... | collective-permute-start | bytes 147464 | tf_op jit(solution)/shard_map/ppermute | solution.py:548
  30.1 0.6 %collective-permute-done.14.refs_2_ = bf16[64,1024]{1,0:T(8,128)(2,1)S(1)} collective-permute-done((bf16[64,1024]{1,0:T(8,128)(2,1)S(1)}, bf16[64,1024]{1,0:T(8,128)(2,1)S(1)}, u32[]{:S(2)}, u32[]{:S(2)}) %collective-permute-start.14) | collective-permute-done | bytes 131104 | tf_op jit(solution)/shard_map/ppermute | solution.py:548
  30.7 0.0 collective-permute-done.13.refs_1_
  30.7 2.5 %wide.1 = (bf16[288,1152]{1,0:T(8,128)(2,1)S(1)}, f32[192,128]{1,0:T(8,128)S(1)}, f32[1,128]{1,0:T(1,128)S(1)}, f32[1,128]{1,0:T(1,128)S(1)}) custom-call(s32[16]{0:T(128)} %frames_hbm.3, s32[16]{0:T(128)} %assign_hbm.5, f32[1,192]{1,0:T(1,128)} %bitcast.14, f32[1,96]{1,0:T(1,128)} %bitcast.15, bf16[64,1024]{1,0:T(8,128)(2,1)S(1)} %stack.3.refs_0_, ...), custom_call_target="tpu_custom_call" | custom-call | flops 11500000 | tf_op jit(solution)/shard_map/wide/pallas_call | solution.py:398
  33.3 0.1 collective-permute-start.16
  33.3 0.0 collective-permute-done.6.refs_1_
  33.3 0.0 collective-permute-done.7.refs_2_
  33.4 0.0 collective-permute-done.8.refs_3_
  33.4 0.5 %collective-permute-start.9 = (bf16[384,256]{1,0:T(8,128)(2,1)S(1)}, bf16[384,256]{1,0:T(8,128)(2,1)S(1)}, u32[]{:S(2)}, u32[]{:S(2)}) collective-permute-start(bf16[384,256]{1,0:T(8,128)(2,1)S(1)} %stack.2.own), channel_id=1, source_target_pairs={{0,1},{1,0},{2,3},{3,2},{4,5},{5,4},{6,7},{7,6},{8,9},{9,8},{10,11... | collective-permute-start | bytes 589832 | tf_op jit(solution)/shard_map/ppermute | solution.py:556
  33.9 1.8 %collective-permute-done.9.other = bf16[384,256]{1,0:T(8,128)(2,1)S(1)} collective-permute-done((bf16[384,256]{1,0:T(8,128)(2,1)S(1)}, bf16[384,256]{1,0:T(8,128)(2,1)S(1)}, u32[]{:S(2)}, u32[]{:S(2)}) %collective-permute-start.9) | collective-permute-done | bytes 196640 | tf_op jit(solution)/shard_map/ppermute | solution.py:556
  35.7 0.0 collective-permute-done.16.w_other
  35.7 3.8 %finish.1 = bf16[1,4,8,6144]{3,2,1,0:T(8,128)(2,1)} custom-call(bf16[384,256]{1,0:T(8,128)(2,1)S(1)} %stack.2.own, bf16[384,256]{1,0:T(8,128)(2,1)S(1)} %collective-permute-done.9.other, bf16[288,1152]{1,0:T(8,128)(2,1)S(1)} %get-tuple-element.41.w_own, bf16[288,1152]{1,0:T(8,128)(2,1)S(1)} %collective-permute-done.16.w_other, ...), custom_call_target="tpu_custom_call" | custom-call | flops 5520000000 | tf_op jit(solution)/shard_map/finish/pallas_call | solution.py:530
  (9 shorter events, 0.1 us)
Async XLA Ops:
  0.0 9.0 %copy-start = (bf16[12,27,96]{2,1,0:T(8,128)(2,1)S(1)}, bf16[12,27,96]{2,1,0:T(8,128)(2,1)}, u32[]{:S(2)}) copy-start(bf16[12,27,96]{2,1,0:T(8,128)(2,1)} %param.16) | copy-start | bytes 186628
  1.9 10.4 %collective-permute-start = (bf16[96,256]{1,0:T(8,128)(2,1)S(1)}, bf16[96,256]{1,0:T(8,128)(2,1)S(1)}, u32[]{:S(2)}, u32[]{:S(2)}) collective-permute-start(bf16[96,256]{1,0:T(8,128)(2,1)S(1)} %get-tuple-element.26), channel_id=1, source_target_pairs={{0,8},{2,10},{4,12},{6,14},{8,16},{10,18},{12,20},{14,22},{16,24},... | collective-permute-start | bytes 147464 | tf_op jit(solution)/shard_map/ppermute | solution.py:548
  5.0 7.9 %collective-permute-start.1 = (bf16[96,256]{1,0:T(8,128)(2,1)S(1)}, bf16[96,256]{1,0:T(8,128)(2,1)S(1)}, u32[]{:S(2)}, u32[]{:S(2)}) collective-permute-start(bf16[96,256]{1,0:T(8,128)(2,1)S(1)} %get-tuple-element.27), channel_id=1, source_target_pairs={{0,16},{2,18},{4,20},{6,22},{8,24},{10,26},{12,28},{14,30},{16,0},... | collective-permute-start | bytes 147464 | tf_op jit(solution)/shard_map/ppermute | solution.py:548
  7.6 5.3 %collective-permute-start.2 = (bf16[96,256]{1,0:T(8,128)(2,1)S(1)}, bf16[96,256]{1,0:T(8,128)(2,1)S(1)}, u32[]{:S(2)}, u32[]{:S(2)}) collective-permute-start(bf16[96,256]{1,0:T(8,128)(2,1)S(1)} %get-tuple-element.28), channel_id=1, source_target_pairs={{0,24},{2,26},{4,28},{6,30},{8,0},{10,2},{12,4},{14,6},{16,8},{18,... | collective-permute-start | bytes 147464 | tf_op jit(solution)/shard_map/ppermute | solution.py:548
  9.3 3.1 %copy-start.1 = (f32[384]{0:T(512)S(1)}, f32[384]{0:T(512)}, u32[]{:S(2)}) copy-start(f32[384]{0:T(512)} %param.17) | copy-start | bytes 4612
  9.3 6.8 %collective-permute-start.12 = (bf16[16,1024]{1,0:T(8,128)(2,1)S(1)}, bf16[16,1024]{1,0:T(8,128)(2,1)S(1)}, u32[]{:S(2)}, u32[]{:S(2)}) collective-permute-start(bf16[16,1024]{1,0:T(8,128)(2,1)S(1)} %fusion.2.refs_0_), channel_id=1, source_target_pairs={{0,6},{2,4},{4,2},{6,0},{8,14},{10,12},{12,10},{14,8},{16,22},{18,... | collective-permute-start | bytes 98312 | tf_op jit(solution)/shard_map/ppermute | solution.py:552
  11.8 5.2 %collective-permute-start.11 = (bf16[16,1024]{1,0:T(8,128)(2,1)S(1)}, bf16[16,1024]{1,0:T(8,128)(2,1)S(1)}, u32[]{:S(2)}, u32[]{:S(2)}) collective-permute-start(bf16[16,1024]{1,0:T(8,128)(2,1)S(1)} %fusion.2.refs_0_), channel_id=1, source_target_pairs={{0,4},{2,6},{4,0},{6,2},{8,12},{10,14},{12,8},{14,10},{16,20},{18,... | collective-permute-start | bytes 98312 | tf_op jit(solution)/shard_map/ppermute | solution.py:552
  12.3 4.6 %collective-permute-start.10 = (bf16[16,1024]{1,0:T(8,128)(2,1)S(1)}, bf16[16,1024]{1,0:T(8,128)(2,1)S(1)}, u32[]{:S(2)}, u32[]{:S(2)}) collective-permute-start(bf16[16,1024]{1,0:T(8,128)(2,1)S(1)} %fusion.2.refs_0_), channel_id=1, source_target_pairs={{0,2},{2,0},{4,6},{6,4},{8,10},{10,8},{12,14},{14,12},{16,18},{18,... | collective-permute-start | bytes 98312 | tf_op jit(solution)/shard_map/ppermute | solution.py:552
  13.1 6.6 %collective-permute-start.3 = (bf16[304,256]{1,0:T(8,128)(2,1)S(1)}, bf16[304,256]{1,0:T(8,128)(2,1)S(1)}, u32[]{:S(2)}, u32[]{:S(2)}) collective-permute-start(bf16[304,256]{1,0:T(8,128)(2,1)S(1)} %get-tuple-element.30), channel_id=1, source_target_pairs={{0,2},{2,0},{4,6},{6,4},{8,10},{10,8},{12,14},{14,12},{16,18},{18,... | collective-permute-start | bytes 466952 | tf_op jit(solution)/shard_map/ppermute | solution.py:552
  14.6 7.9 %collective-permute-start.4 = (bf16[304,256]{1,0:T(8,128)(2,1)S(1)}, bf16[304,256]{1,0:T(8,128)(2,1)S(1)}, u32[]{:S(2)}, u32[]{:S(2)}) collective-permute-start(bf16[304,256]{1,0:T(8,128)(2,1)S(1)} %get-tuple-element.31), channel_id=1, source_target_pairs={{0,4},{2,6},{4,0},{6,2},{8,12},{10,14},{12,8},{14,10},{16,20},{18,... | collective-permute-start | bytes 466952 | tf_op jit(solution)/shard_map/ppermute | solution.py:552
  16.1 6.4 %collective-permute-start.5 = (bf16[304,256]{1,0:T(8,128)(2,1)S(1)}, bf16[304,256]{1,0:T(8,128)(2,1)S(1)}, u32[]{:S(2)}, u32[]{:S(2)}) collective-permute-start(bf16[304,256]{1,0:T(8,128)(2,1)S(1)} %get-tuple-element.32), channel_id=1, source_target_pairs={{0,6},{2,4},{4,2},{6,0},{8,14},{10,12},{12,10},{14,8},{16,22},{18,... | collective-permute-start | bytes 466952 | tf_op jit(solution)/shard_map/ppermute | solution.py:552
  17.0 12.0 %collective-permute-start.15 = (bf16[64,1024]{1,0:T(8,128)(2,1)S(1)}, bf16[64,1024]{1,0:T(8,128)(2,1)S(1)}, u32[]{:S(2)}, u32[]{:S(2)}) collective-permute-start(bf16[64,1024]{1,0:T(8,128)(2,1)S(1)} %stack.3.refs_0_), channel_id=1, source_target_pairs={{0,24},{2,26},{4,28},{6,30},{8,0},{10,2},{12,4},{14,6},{16,8},{18,... | collective-permute-start | bytes 393224 | tf_op jit(solution)/shard_map/ppermute | solution.py:548
  18.6 12.1 %collective-permute-start.14 = (bf16[64,1024]{1,0:T(8,128)(2,1)S(1)}, bf16[64,1024]{1,0:T(8,128)(2,1)S(1)}, u32[]{:S(2)}, u32[]{:S(2)}) collective-permute-start(bf16[64,1024]{1,0:T(8,128)(2,1)S(1)} %stack.3.refs_0_), channel_id=1, source_target_pairs={{0,16},{2,18},{4,20},{6,22},{8,24},{10,26},{12,28},{14,30},{16,0},... | collective-permute-start | bytes 393224 | tf_op jit(solution)/shard_map/ppermute | solution.py:548
  19.6 11.1 %collective-permute-start.13 = (bf16[64,1024]{1,0:T(8,128)(2,1)S(1)}, bf16[64,1024]{1,0:T(8,128)(2,1)S(1)}, u32[]{:S(2)}, u32[]{:S(2)}) collective-permute-start(bf16[64,1024]{1,0:T(8,128)(2,1)S(1)} %stack.3.refs_0_), channel_id=1, source_target_pairs={{0,8},{2,10},{4,12},{6,14},{8,16},{10,18},{12,20},{14,22},{16,24},... | collective-permute-start | bytes 393224 | tf_op jit(solution)/shard_map/ppermute | solution.py:548
  26.2 7.1 %collective-permute-start.6 = (bf16[96,256]{1,0:T(8,128)(2,1)S(1)}, bf16[96,256]{1,0:T(8,128)(2,1)S(1)}, u32[]{:S(2)}, u32[]{:S(2)}) collective-permute-start(bf16[96,256]{1,0:T(8,128)(2,1)S(1)} %get-tuple-element.34), channel_id=1, source_target_pairs={{0,8},{2,10},{4,12},{6,14},{8,16},{10,18},{12,20},{14,22},{16,24},... | collective-permute-start | bytes 147464 | tf_op jit(solution)/shard_map/ppermute | solution.py:548
  27.0 6.3 %collective-permute-start.7 = (bf16[96,256]{1,0:T(8,128)(2,1)S(1)}, bf16[96,256]{1,0:T(8,128)(2,1)S(1)}, u32[]{:S(2)}, u32[]{:S(2)}) collective-permute-start(bf16[96,256]{1,0:T(8,128)(2,1)S(1)} %get-tuple-element.35), channel_id=1, source_target_pairs={{0,16},{2,18},{4,20},{6,22},{8,24},{10,26},{12,28},{14,30},{16,0},... | collective-permute-start | bytes 147464 | tf_op jit(solution)/shard_map/ppermute | solution.py:548
  29.0 4.4 %collective-permute-start.8 = (bf16[96,256]{1,0:T(8,128)(2,1)S(1)}, bf16[96,256]{1,0:T(8,128)(2,1)S(1)}, u32[]{:S(2)}, u32[]{:S(2)}) collective-permute-start(bf16[96,256]{1,0:T(8,128)(2,1)S(1)} %get-tuple-element.36), channel_id=1, source_target_pairs={{0,24},{2,26},{4,28},{6,30},{8,0},{10,2},{12,4},{14,6},{16,8},{18,... | collective-permute-start | bytes 147464 | tf_op jit(solution)/shard_map/ppermute | solution.py:548
  33.3 2.5 %collective-permute-start.16 = (bf16[288,1152]{1,0:T(8,128)(2,1)S(1)}, bf16[288,1152]{1,0:T(8,128)(2,1)S(1)}, u32[]{:S(2)}, u32[]{:S(2)}) collective-permute-start(bf16[288,1152]{1,0:T(8,128)(2,1)S(1)} %get-tuple-element.41.w_own), channel_id=1, source_target_pairs={{0,1},{1,0},{2,3},{3,2},{4,5},{5,4},{6,7},{7,6},{8,9},{9,8},{10,11... | collective-permute-start | bytes 1990664 | tf_op jit(solution)/shard_map/ppermute | solution.py:556
  33.4 2.3 %collective-permute-start.9 = (bf16[384,256]{1,0:T(8,128)(2,1)S(1)}, bf16[384,256]{1,0:T(8,128)(2,1)S(1)}, u32[]{:S(2)}, u32[]{:S(2)}) collective-permute-start(bf16[384,256]{1,0:T(8,128)(2,1)S(1)} %stack.2.own), channel_id=1, source_target_pairs={{0,1},{1,0},{2,3},{3,2},{4,5},{5,4},{6,7},{7,6},{8,9},{9,8},{10,11... | collective-permute-start | bytes 589832 | tf_op jit(solution)/shard_map/ppermute | solution.py:556

commit v5 on v4

--- a/solution.py
+++ b/solution.py
@@ -123,7 +123,6 @@
 B_ROWS = LINE * W_ROWS + LINE * LINE
 WOUT_LANES = 896
 HALF_CH = C2 // 2
-FOLD = 9 * C3 // 8
 F32, BF16 = jnp.float32, jnp.bfloat16
 VMEM = functools.partial(pl.BlockSpec, memory_space=pltpu.VMEM)
 SMEM = functools.partial(pl.BlockSpec, memory_space=pltpu.SMEM)
@@ -157,39 +156,47 @@
 
 def pack_kernel(offsets_hbm, assign_hbm, w_hbm, lat_hbm, *refs):
     outs, (wf, lf, pf, w_ref, lat_ref, offsets, assign, sems) = refs[:LINE], refs[LINE:]
-    moves = [(offsets_hbm, offsets), (assign_hbm, assign), (lat_hbm, lat_ref), (w_hbm, w_ref)]
+    parts = [pl.ds(9 * a, 9) for a in range(3)]
+    moves = [(w_hbm.at[p], w_ref.at[p]) for p in parts]
+    moves = [(offsets_hbm, offsets), (assign_hbm, assign), (lat_hbm, lat_ref)] + moves
     copies = [pltpu.make_async_copy(src, dst, sems.at[i]) for i, (src, dst) in enumerate(moves)]
     for copy in copies:
         copy.start()
     z, _, c = place()
-    for copy in copies:
+    lf[32:40, :] = jnp.zeros((8, 128), F32)
+    for k in range(LINE):
+        pf[k, TOK:, :] = jnp.zeros((PIECE_ROWS - TOK, 256), F32)
+    lane1 = iota((1, 128), 1)
+    lane = iota((IN_SH, 256), 1)
+    for copy in copies[:3]:
         copy.wait()
-    wf[:, :, :C2] = w_ref[...].astype(F32)
     lat = lat_ref[...].astype(F32)
-    lf[32:40, :] = jnp.zeros((8, 128), F32)
     for j in range(32):
         lf[j : j + 1, :] = lat[:, 128 * j : 128 * j + 128]
-    lane1 = iota((1, 128), 1)
-    pf[PIECE_ROWS - 8 :, :] = jnp.zeros((8, 256), F32)
     for g in range(16):
         off = offsets[assign[g]]
         row, rem = lax.div(off, 8), lax.rem(off, 8)
         x = pltpu.roll(lf[pl.ds(row, 8), :], lax.rem(128 - ZC * rem, 128), 1)
         keep = lane1 < 128 - ZC * rem
-        pf[g : g + 1, 0:128] = jnp.where(keep, x[0:1], x[1:2])
-        pf[g : g + 1, 128:256] = jnp.where(keep, x[1:2], x[2:3])
-    lane = iota((IN_SH, 256), 1)
+        pf[0, g : g + 1, 0:128] = jnp.where(keep, x[0:1], x[1:2])
+        pf[0, g : g + 1, 128:256] = jnp.where(keep, x[1:2], x[2:3])
+    for k in range(1, LINE):
+        pf[k, 0:TOK, :] = pf[0, 0:TOK, :]
+    for a in range(3):
+        copies[3 + a].wait()
+        wf[9 * a : 9 * a + 9, :, :C2] = w_ref[9 * a : 9 * a + 9].astype(F32)
+        for k in range(LINE):
+            first = (lax.rem(z + k, LINE) * 2 + c) * OUT_BLK
+            for b in range(3):
+                rows = slice(TOK + IN_SH * b, TOK + IN_SH * (b + 1))
+                acc = pf[k, rows, :]
+                for e in range(3):
+                    at = OUT_BLK * (3 * a + e)
+                    moved = pltpu.roll(wf[9 * a + 3 * b + e], lax.rem(at - first + 256, 256), 1)
+                    acc = jnp.where((lane >= at) & (lane < at + OUT_BLK), moved, acc)
+                pf[k, rows, :] = acc
     for k in range(LINE):
-        first = (lax.rem(z + k, LINE) * 2 + c) * OUT_BLK
-        for b in range(3):
-            acc = jnp.zeros((IN_SH, 256), F32)
-            for j in range(9):
-                tap = 9 * (j // 3) + 3 * b + j % 3
-                at = OUT_BLK * j
-                moved = pltpu.roll(wf[tap], lax.rem(at - first + 256, 256), 1)
-                acc = jnp.where((lane >= at) & (lane < at + OUT_BLK), moved, acc)
-            pf[TOK + IN_SH * b : TOK + IN_SH * (b + 1), :] = acc
-        outs[k][...] = pf[...].astype(BF16)
+        outs[k][...] = pf[k].astype(BF16)
 
 
 def pack(offsets, assign, w_mid, latents):
@@ -202,12 +209,12 @@
         scratch_shapes=[
             pltpu.VMEM((27, IN_SH, 256), F32),
             pltpu.VMEM((40, 128), F32),
-            pltpu.VMEM((PIECE_ROWS, 256), F32),
+            pltpu.VMEM((LINE, PIECE_ROWS, 256), F32),
             pltpu.VMEM((27, IN_SH, C2), BF16),
             pltpu.VMEM(latents.shape, BF16),
             pltpu.SMEM(offsets.shape, jnp.int32),
             pltpu.SMEM(assign.shape, jnp.int32),
-            pltpu.SemaphoreType.DMA((4,)),
+            pltpu.SemaphoreType.DMA((6,)),
         ],
         cost_estimate=cost(2),
         compiler_params=pltpu.CompilerParams(vmem_limit_bytes=32 << 20),
@@ -361,32 +368,52 @@
     )(*in_hbm(frames, assign, w_in), gain_in, *parts)
 
 
-def wide_kernel(frames_hbm, assign_hbm, gmid_hbm, gout_hbm, *refs):
-    parts, (out, gmid_out, gout_out, limit_out) = refs[:LINE], refs[LINE : LINE + 4]
-    rows, wf, gmid_ref, gout_ref, frames, assign, sems = refs[LINE + 4 :]
+def regroup_kernel(*refs):
+    parts, out, rows = refs[:PLANE], refs[PLANE], refs[PLANE + 1]
+    for d in range(PLANE):
+        part = parts[d][...].astype(F32)
+        for b in range(3):
+            at = OUT_BLK * b + 6 * d
+            rows[at : at + 6, :] = part[8 * b : 8 * b + 6]
+    out[...] = rows[...].astype(BF16)
+
+
+def regroup(parts):
+    return pl.pallas_call(
+        regroup_kernel,
+        out_shape=jax.ShapeDtypeStruct((3 * OUT_BLK, WOUT_LANES), BF16),
+        in_specs=[VMEM()] * PLANE,
+        out_specs=VMEM(),
+        scratch_shapes=[pltpu.VMEM((3 * OUT_BLK, WOUT_LANES), F32)],
+        cost_estimate=cost(5),
+        compiler_params=pltpu.CompilerParams(vmem_limit_bytes=32 << 20),
+        name="regroup",
+    )(*parts)
+
+
+def prep_kernel(frames_hbm, assign_hbm, gmid_hbm, gout_hbm, *refs):
+    parts, (raw, order_out, pick_out, gmid_out, gout_out, limit_out) = refs[:LINE], refs[LINE : LINE + 6]
+    gmid_ref, gout_ref, frames, assign, sems = refs[LINE + 6 :]
     moves = [(gmid_hbm, gmid_ref), (gout_hbm, gout_ref), (frames_hbm, frames), (assign_hbm, assign)]
     loads = [pltpu.make_async_copy(src, dst, sems.at[i]) for i, (src, dst) in enumerate(moves)]
     for load in loads:
         load.start()
-    z, q, _ = place()
-    wf[...] = jnp.zeros((9, 3 * HALF_CH, 128), F32)
+    z, q, c = place()
     for k in range(LINE):
-        for d in range(PLANE):
-            shard = lax.rem(z - k + LINE, LINE) * PLANE + (q ^ d)
-            part = parts[k][16 * d : 16 * d + 16, :].astype(F32)
-            rows[0:16, : 9 * C3] = part[:, : 9 * C3]
-            for g in range(8):
-                rows[16:18, FOLD * g : FOLD * (g + 1)] = part[2 * g : 2 * g + 2, 9 * C3 : 9 * C3 + FOLD]
-            for j in range(9):
-                tap = rows[:, C3 * j : C3 * (j + 1)]
-                for b in range(3):
-                    wf[j, pl.ds(HALF_CH * b + 6 * shard, 6), :C3] = tap[6 * b : 6 * b + 6]
-    for j in range(9):
-        out[:, 128 * j : 128 * (j + 1)] = wf[j].astype(BF16)
+        raw[3 * OUT_BLK * k : 3 * OUT_BLK * (k + 1), :] = parts[k][...]
+    row, channel = iota((C2, C2), 0), iota((C2, C2), 1)
+    side, step = row // HALF_CH, row % HALF_CH // OUT_BLK
+    flip = q ^ (2 * (c ^ side) + row % OUT_BLK // MID_SH)
+    held = (c ^ (row % MID_SH // 6)) * HALF_CH + step * OUT_BLK + 6 * flip + row % 6
+    order_out[...] = (channel == held).astype(F32).astype(BF16)
+    r, l = iota((256, 256), 0), iota((256, 256), 1)
+    same = (r // 8) == ((l // 64) % 2) * WL + l % WL
+    mid_row = 2 * ((l // WL) % 4) + l // 128
+    for b in range(3):
+        pick_out[b] = (same & (mid_row == (c * 8 + r % 8 + b - 1) >> 1)).astype(F32).astype(BF16)
     for load in loads:
         load.wait()
-    row, channel = iota((C2, C2), 0), iota((C2, C2), 1)
-    wanted = (row % HALF_CH) // 6 * MID_SH + row // HALF_CH * 6 + row % 6
+    wanted = (2 * ((z - step) & (LINE - 1)) + (c ^ side)) * OUT_BLK + row % OUT_BLK
     column = jnp.sum(jnp.where(channel == wanted, gmid_ref[...], 0.0), axis=1, keepdims=True)
     gmid_out[...] = jnp.broadcast_to(column, (C2, 128))
     gout_out[...] = jnp.zeros((1, 128), F32)
@@ -394,20 +421,20 @@
     limit_out[...] = jnp.full((1, 128), frames[assign[z * PLANE + q]], jnp.int32).astype(F32)
 
 
-def wide(frames, assign, gain_mid, gain_out, parts):
-    return pl.pallas_call(
-        wide_kernel,
+def prep(frames, assign, gain_mid, gain_out, parts):
+    return pl.pallas_call(
+        prep_kernel,
         out_shape=[
-            jax.ShapeDtypeStruct((3 * HALF_CH, 1152), BF16),
+            jax.ShapeDtypeStruct((LINE * 3 * OUT_BLK, WOUT_LANES), BF16),
+            jax.ShapeDtypeStruct((C2, C2), BF16),
+            jax.ShapeDtypeStruct((3, 256, 256), BF16),
             jax.ShapeDtypeStruct((C2, 128), F32),
             jax.ShapeDtypeStruct((1, 128), F32),
             jax.ShapeDtypeStruct((1, 128), F32),
         ],
         in_specs=[HBM()] * 4 + [VMEM()] * LINE,
-        out_specs=[VMEM()] * 4,
+        out_specs=[VMEM()] * 6,
         scratch_shapes=[
-            pltpu.VMEM((24, WOUT_LANES), F32),
-            pltpu.VMEM((9, 3 * HALF_CH, 128), F32),
             pltpu.VMEM(gain_mid.shape, F32),
             pltpu.VMEM(gain_out.shape, F32),
             pltpu.SMEM(frames.shape, jnp.int32),
@@ -415,9 +442,38 @@
             pltpu.SemaphoreType.DMA((4,)),
         ],
         cost_estimate=cost(0.01),
+        compiler_params=pltpu.CompilerParams(vmem_limit_bytes=32 << 20),
+        name="prep",
+    )(*in_hbm(frames, assign, gain_mid, gain_out), *parts)
+
+
+def wide_kernel(own, other, order, out, wf):
+    wf[:, :, :, C3:] = jnp.zeros((3, 9, C2, 128 - C3), F32)
+    for source, raw in enumerate((own, other)):
+        for k in range(LINE):
+            part = raw[72 * k : 72 * k + 72, :].astype(F32)
+            at = (source * LINE + k) * OUT_BLK
+            for j in range(9):
+                tap = part[:, C3 * j : C3 * (j + 1)]
+                for b in range(3):
+                    wf[b, j, at : at + OUT_BLK, :C3] = tap[OUT_BLK * b : OUT_BLK * (b + 1)]
+    for b in range(3):
+        for j in range(9):
+            moved = jnp.dot(order[...], wf[b, j].astype(BF16), preferred_element_type=F32)
+            out[C2 * b : C2 * (b + 1), 128 * j : 128 * (j + 1)] = moved.astype(BF16)
+
+
+def wide(own, other, order):
+    return pl.pallas_call(
+        wide_kernel,
+        out_shape=jax.ShapeDtypeStruct((3 * C2, 1152), BF16),
+        in_specs=[VMEM()] * 3,
+        out_specs=VMEM(),
+        scratch_shapes=[pltpu.VMEM((3, 9, C2, 128), F32)],
+        cost_estimate=cost(0.01),
         compiler_params=pltpu.CompilerParams(vmem_limit_bytes=48 << 20),
         name="wide",
-    )(*in_hbm(frames, assign, gain_mid, gain_out), *parts)
+    )(own, other, order)
 
 
 def stack_kernel(*refs):
@@ -439,25 +495,14 @@
     )(*parts)
 
 
-def out_kernel(own, other, w_own, w_other, gmid_ref, gout_ref, limit_ref, out_ref, hid, lhs, prod, w_all):
-    z, q, c = place()
-    for b in range(3):
-        for side, half in ((c, w_own), (1 - c, w_other)):
-            at = pl.multiple_of(256 * b + HALF_CH * side, 32)
-            w_all[pl.ds(at, HALF_CH), :] = half[HALF_CH * b : HALF_CH * (b + 1), :]
-        w_all[256 * b + C2 : 256 * (b + 1), :] = jnp.zeros((64, 1152), BF16)
-    lhs[:, :, :, :] = jnp.zeros(lhs.shape, BF16)
-    for side, group in ((c, own), (1 - c, other)):
+def out_kernel(own, other, w_all, pick, gmid_ref, gout_ref, limit_ref, out_ref, hid, lhs, prod):
+    for side, group in enumerate((own, other)):
         for k in range(LINE):
-            block = lax.rem(z - k + LINE, LINE) * 2 + side
             part = group[96 * k : 96 * k + 96, :].astype(F32)
+            at = (side * LINE + k) * OUT_BLK
             for p in range(4):
-                for half in range(2):
-                    for shard in range(2):
-                        first = OUT_BLK * p + MID_SH * shard + 6 * half
-                        at = HALF_CH * half + 12 * block + 6 * shard
-                        for tp in range(2):
-                            hid[p, tp, pl.ds(at, 6), :] = part[first : first + 6, 128 * tp : 128 * tp + 128]
+                for tp in range(2):
+                    hid[p, tp, at : at + OUT_BLK, :] = part[OUT_BLK * p : OUT_BLK * (p + 1), 128 * tp : 128 * tp + 128]
     acts = []
     for p in range(4):
         halves = []
@@ -466,23 +511,18 @@
             scale = lax.rsqrt(jnp.sum(h * h, axis=0, keepdims=True) * (1.0 / C2) + 1e-6)
             halves.append(silu(h * scale * gmid_ref[...]).astype(BF16))
         acts.append(halves)
-    r, l = iota((256, 256), 0), iota((256, 256), 1)
-    same = (r // 8) == ((l // 64) % 2) * WL + l % WL
-    mid_row = 2 * ((l // WL) % 4) + l // 128
     for b in range(3):
-        wanted = (c * 8 + r % 8 + b - 1) >> 1
-        pick = (same & (mid_row == wanted)).astype(F32).astype(BF16)
         for tp in range(2):
             for px in range(2):
                 src = jnp.concatenate([acts[2 * py + px][tp] for py in range(2)], axis=1)
-                rows = dot_nt(pick, src).astype(BF16)
+                rows = dot_nt(pick[b], src).astype(BF16)
                 for half in range(2):
-                    lhs[2 * tp + half, px, :, 256 * b : 256 * b + C2] = rows[128 * half : 128 * half + 128]
-    prod[0:2] = jnp.dot(lhs[0:2].reshape(512, 768), w_all[...], preferred_element_type=F32).reshape(2, 2, 128, 1152)
+                    lhs[2 * tp + half, px, :, C2 * b : C2 * b + C2] = rows[128 * half : 128 * half + 128]
+    prod[0:2] = jnp.dot(lhs[0:2].reshape(512, 3 * C2), w_all[...], preferred_element_type=F32).reshape(2, 2, 128, 1152)
     for t in (2, 3):
         at = 384 * (t - 1)
         prod[t, :, :, at:] = jnp.dot(
-            lhs[t].reshape(256, 768), w_all[:, at:], preferred_element_type=F32
+            lhs[t].reshape(256, 3 * C2), w_all[:, at:], preferred_element_type=F32
         ).reshape(2, 128, 1152 - at)
     lane = iota((1, 8, 128), 2)
     limit = limit_ref[...]
@@ -534,9 +574,8 @@
         out_specs=VMEM(),
         scratch_shapes=[
             pltpu.VMEM((4, 2, C2, 128), F32),
-            pltpu.VMEM((4, 2, 128, 768), BF16),
+            pltpu.VMEM((4, 2, 128, 3 * C2), BF16),
             pltpu.VMEM((4, 2, 128, 1152), F32),
-            pltpu.VMEM((768, 1152), BF16),
         ],
         compiler_params=pltpu.CompilerParams(vmem_limit_bytes=48 << 20),
         cost_estimate=cost(4.8),
@@ -563,16 +602,16 @@
     parts = join(pieces)
     parts = [parts[0]] + [in_plane(parts[d], d) for d in range(1, PLANE)]
     rows = lax.dynamic_slice_in_dim(w_out, core * 6, 6, axis=0)
-    rows = rows.reshape(6, 3, 3, 3, C3).transpose(2, 0, 1, 3, 4).reshape(18, 9 * C3)
-    fold = rows[16:].reshape(2, 8, FOLD).transpose(1, 0, 2).reshape(16, FOLD)
-    half = jnp.pad(jnp.concatenate([rows[:16], fold], axis=1), ((0, 0), (0, 1024 - 9 * C3 - FOLD)))
-    plane = stack([half] + [in_plane(half, d) for d in range(1, PLANE)])
+    rows = rows.reshape(6, 3, 3, 3, C3).transpose(2, 0, 1, 3, 4).reshape(3, 6, 9 * C3)
+    half = jnp.pad(rows, ((0, 0), (0, 2), (0, WOUT_LANES - 9 * C3))).reshape(24, WOUT_LANES)
+    plane = regroup([half] + [in_plane(half, d) for d in range(1, PLANE)])
     own = [plane] + [along_z(plane, k) for k in range(1, LINE)]
     hidden = mid(frames, assign, parts, w_in.transpose(1, 0, 2).reshape(27 * ZC, C1), gain_in[None, :])
     own, _ = lax.optimization_barrier((own, hidden[0]))
-    w_last, gmid, gout, limit = wide(frames, assign, gain_mid[None, :], gain_out[None, :], own)
+    raw, order, pick, gmid, gout, limit = prep(frames, assign, gain_mid[None, :], gain_out[None, :], own)
+    w_last = wide(raw, other_core(raw), order)
     hidden = stack([hidden[0]] + [along_z(hidden[k], k) for k in range(1, LINE)], 30)
-    return finish(hidden, other_core(hidden), w_last, other_core(w_last), gmid, gout, limit)
+    return finish(hidden, other_core(hidden), w_last, pick, gmid, gout, limit)
 
 
 def solution(mesh):

time: 39.7 us -> 38.7 us (0.975)
  Pallas kernels: 12.1 us -> 11.4 us
    ppermute x9, waiting for transfers between devices: 0.59 us -> 2.48 us  [along_z(): lax.ppermute(value, 'grp', [(g, (g + PLANE * step) % (LINE * PLANE)) for...]
    ppermute x2, waiting for transfers between devices: 1.78 us -> 0.25 us  [other_core(): return lax.ppermute(value, 'row', [(0, 1), (1, 0)])]
    ppermute x9, starting transfers between devices: 13.9 us -> 14.8 us  [along_z(): lax.ppermute(value, 'grp', [(g, (g + PLANE * step) % (LINE * PLANE)) for...]
    ppermute x6, waiting for transfers between devices: 2.64 us -> 2.04 us  [in_plane(): lax.ppermute(value, 'grp', [(g, g ^ flip) for g in range(LINE * PLANE)])]
    ppermute x2, starting transfers between devices: 0.61 us -> 0.14 us  [other_core(): return lax.ppermute(value, 'row', [(0, 1), (1, 0)])]
    pallas_call x1 -> x3, Pallas kernels: 2.54 us -> 2.17 us  [the longest x1 1.16 us: wide(): pl.pallas_call(wide_kernel, out_shape=jax.ShapeDtypeStruct((3 * C2, 1152)...]
  transfers between devices with their start and end apart: 17 -> 17, of which waited for: 4 -> 7; matrix products, arithmetic and copies ran while one was open for 1% -> 0% of each run, Pallas kernels for 16% -> 16%
where the time goes in v5:
time: 38.7 us; the launch traced here: 38.6 us
  starting transfers between devices  22.1 us (57%)
  Pallas kernels  11.4 us (29%)
  waiting for transfers between devices  4.77 us (12%)
    ppermute x9, starting transfers between devices, along_z(): lax.ppermute(value, 'grp', [(g, (g + PLANE * step) % (LINE * PLANE)) for...  14.8 us
    ppermute x6, starting transfers between devices, in_plane(): lax.ppermute(value, 'grp', [(g, g ^ flip) for g in range(LINE * PLANE)])  7.17 us
    pallas_call x1, Pallas kernels, mid(): pl.pallas_call(mid_kernel, out_shape=[out] * LINE, in_specs=[HBM()] * 3 +...  3.68 us
    pallas_call x1, Pallas kernels, finish(): pl.pallas_call(out_kernel, out_shape=jax.ShapeDtypeStruct((1, FMAX, 4 * R...  3.43 us
    ppermute x9, waiting for transfers between devices, along_z(): lax.ppermute(value, 'grp', [(g, (g + PLANE * step) % (LINE * PLANE)) for...  2.48 us
    ppermute x6, waiting for transfers between devices, in_plane(): lax.ppermute(value, 'grp', [(g, g ^ flip) for g in range(LINE * PLANE)])  2.04 us
    pallas_call x1, Pallas kernels, pack(): pl.pallas_call(pack_kernel, out_shape=[piece] * LINE, in_specs=[HBM()] *...  1.97 us
    pallas_call x1, Pallas kernels, wide(): pl.pallas_call(wide_kernel, out_shape=jax.ShapeDtypeStruct((3 * C2, 1152)...  1.16 us
  transfers between devices with their start and end apart: 17, of which 7 were waited for; matrix products, arithmetic and copies ran while one was open for 0% of the time, Pallas kernels for 16%

profile of v5, /device:TPU:0, one launch (start us, length us, event | category | flops | bytes accessed | tf_op | source)
XLA Modules:
  0.0 38.6 jit_solution(14778058246996646869)
XLA Ops:
  0.0 0.0 copy-start
  0.0 0.0 copy-start.1
  0.0 2.0 %pack.1 = (bf16[96,256]{1,0:T(8,128)(2,1)S(1)}, bf16[96,256]{1,0:T(8,128)(2,1)S(1)}, bf16[96,256]{1,0:T(8,128)(2,1)S(1)}, bf16[96,256]{1,0:T(8,128)(2,1)S(1)}) custom-call(s32[16]{0:T(128)} %offsets_hbm.1, s32[16]{0:T(128)} %assign_hbm.5, bf16[27,24,192]{2,1,0:T(8,128)(2,1)} %bitcast.14, bf16[1,4096]{1,0:T(2,128)(2,1)} %lat_hbm.1), custom_call_target="tpu_custom_call" | custom-call | flops 2300000000 | tf_op jit(solution)/shard_map/pack/pallas_call | solution.py:204
  2.0 3.1 %collective-permute-start = (bf16[96,256]{1,0:T(8,128)(2,1)S(1)}, bf16[96,256]{1,0:T(8,128)(2,1)S(1)}, u32[]{:S(2)}, u32[]{:S(2)}) collective-permute-start(bf16[96,256]{1,0:T(8,128)(2,1)S(1)} %get-tuple-element.28), channel_id=1, source_target_pairs={{0,8},{2,10},{4,12},{6,14},{8,16},{10,18},{12,20},{14,22},{16,24},... | collective-permute-start | bytes 147464 | tf_op jit(solution)/shard_map/ppermute | solution.py:587
  5.1 2.6 %collective-permute-start.1 = (bf16[96,256]{1,0:T(8,128)(2,1)S(1)}, bf16[96,256]{1,0:T(8,128)(2,1)S(1)}, u32[]{:S(2)}, u32[]{:S(2)}) collective-permute-start(bf16[96,256]{1,0:T(8,128)(2,1)S(1)} %get-tuple-element.29), channel_id=1, source_target_pairs={{0,16},{2,18},{4,20},{6,22},{8,24},{10,26},{12,28},{14,30},{16,0},... | collective-permute-start | bytes 147464 | tf_op jit(solution)/shard_map/ppermute | solution.py:587
  7.6 1.3 %collective-permute-start.2 = (bf16[96,256]{1,0:T(8,128)(2,1)S(1)}, bf16[96,256]{1,0:T(8,128)(2,1)S(1)}, u32[]{:S(2)}, u32[]{:S(2)}) collective-permute-start(bf16[96,256]{1,0:T(8,128)(2,1)S(1)} %get-tuple-element.30), channel_id=1, source_target_pairs={{0,24},{2,26},{4,28},{6,30},{8,0},{10,2},{12,4},{14,6},{16,8},{18,... | collective-permute-start | bytes 147464 | tf_op jit(solution)/shard_map/ppermute | solution.py:587
  9.0 0.0 copy-done
  9.1 0.1 reshape.14
  9.2 1.6 %collective-permute-start.10 = (bf16[24,896]{1,0:T(8,128)(2,1)S(1)}, bf16[24,896]{1,0:T(8,128)(2,1)S(1)}, u32[]{:S(2)}, u32[]{:S(2)}) collective-permute-start(bf16[24,896]{1,0:T(8,128)(2,1)S(1)} %pad_bitcast_fusion.refs_0_), channel_id=1, source_target_pairs={{0,2},{2,0},{4,6},{6,4},{8,10},{10,8},{12,14},{14,12},{16,18},{18,... | collective-permute-start | bytes 129032 | tf_op jit(solution)/shard_map/ppermute | solution.py:591
  10.7 1.5 %collective-permute-start.11 = (bf16[24,896]{1,0:T(8,128)(2,1)S(1)}, bf16[24,896]{1,0:T(8,128)(2,1)S(1)}, u32[]{:S(2)}, u32[]{:S(2)}) collective-permute-start(bf16[24,896]{1,0:T(8,128)(2,1)S(1)} %pad_bitcast_fusion.refs_0_), channel_id=1, source_target_pairs={{0,4},{2,6},{4,0},{6,2},{8,12},{10,14},{12,8},{14,10},{16,20},{18,... | collective-permute-start | bytes 129032 | tf_op jit(solution)/shard_map/ppermute | solution.py:591
  12.3 0.0 copy-done.1
  12.3 0.0 collective-permute-done.refs_1_
  12.3 0.5 %collective-permute-start.12 = (bf16[24,896]{1,0:T(8,128)(2,1)S(1)}, bf16[24,896]{1,0:T(8,128)(2,1)S(1)}, u32[]{:S(2)}, u32[]{:S(2)}) collective-permute-start(bf16[24,896]{1,0:T(8,128)(2,1)S(1)} %pad_bitcast_fusion.refs_0_), channel_id=1, source_target_pairs={{0,6},{2,4},{4,2},{6,0},{8,14},{10,12},{12,10},{14,8},{16,22},{18,... | collective-permute-start | bytes 129032 | tf_op jit(solution)/shard_map/ppermute | solution.py:591
  12.8 0.0 collective-permute-done.1.refs_2_
  12.8 0.0 collective-permute-done.2.refs_3_
  12.8 0.1 join.1
  13.0 1.6 %collective-permute-start.3 = (bf16[304,256]{1,0:T(8,128)(2,1)S(1)}, bf16[304,256]{1,0:T(8,128)(2,1)S(1)}, u32[]{:S(2)}, u32[]{:S(2)}) collective-permute-start(bf16[304,256]{1,0:T(8,128)(2,1)S(1)} %get-tuple-element.32), channel_id=1, source_target_pairs={{0,2},{2,0},{4,6},{6,4},{8,10},{10,8},{12,14},{14,12},{16,18},{18,... | collective-permute-start | bytes 466952 | tf_op jit(solution)/shard_map/ppermute | solution.py:591
  14.5 1.5 %collective-permute-start.4 = (bf16[304,256]{1,0:T(8,128)(2,1)S(1)}, bf16[304,256]{1,0:T(8,128)(2,1)S(1)}, u32[]{:S(2)}, u32[]{:S(2)}) collective-permute-start(bf16[304,256]{1,0:T(8,128)(2,1)S(1)} %get-tuple-element.33), channel_id=1, source_target_pairs={{0,4},{2,6},{4,0},{6,2},{8,12},{10,14},{12,8},{14,10},{16,20},{18,... | collective-permute-start | bytes 466952 | tf_op jit(solution)/shard_map/ppermute | solution.py:591
  16.0 0.0 collective-permute-done.10.refs_1_
  16.0 0.5 %collective-permute-start.5 = (bf16[304,256]{1,0:T(8,128)(2,1)S(1)}, bf16[304,256]{1,0:T(8,128)(2,1)S(1)}, u32[]{:S(2)}, u32[]{:S(2)}) collective-permute-start(bf16[304,256]{1,0:T(8,128)(2,1)S(1)} %get-tuple-element.34), channel_id=1, source_target_pairs={{0,6},{2,4},{4,2},{6,0},{8,14},{10,12},{12,10},{14,8},{16,22},{18,... | collective-permute-start | bytes 466952 | tf_op jit(solution)/shard_map/ppermute | solution.py:591
  16.5 0.0 collective-permute-done.11.refs_2_
  16.5 0.9 %collective-permute-done.12.refs_3_ = bf16[24,896]{1,0:T(8,128)(2,1)S(1)} collective-permute-done((bf16[24,896]{1,0:T(8,128)(2,1)S(1)}, bf16[24,896]{1,0:T(8,128)(2,1)S(1)}, u32[]{:S(2)}, u32[]{:S(2)}) %collective-permute-start.12) | collective-permute-done | bytes 43040 | tf_op jit(solution)/shard_map/ppermute | solution.py:591
  17.5 0.6 %collective-permute-start.13 = (bf16[72,896]{1,0:T(8,128)(2,1)S(1)}, bf16[72,896]{1,0:T(8,128)(2,1)S(1)}, u32[]{:S(2)}, u32[]{:S(2)}) collective-permute-start(bf16[72,896]{1,0:T(8,128)(2,1)S(1)} %regroup.1.refs_0_), channel_id=1, source_target_pairs={{0,8},{2,10},{4,12},{6,14},{8,16},{10,18},{12,20},{14,22},{16,24},... | collective-permute-start | bytes 387080 | tf_op jit(solution)/shard_map/ppermute | solution.py:587
  18.1 1.2 %collective-permute-start.14 = (bf16[72,896]{1,0:T(8,128)(2,1)S(1)}, bf16[72,896]{1,0:T(8,128)(2,1)S(1)}, u32[]{:S(2)}, u32[]{:S(2)}) collective-permute-start(bf16[72,896]{1,0:T(8,128)(2,1)S(1)} %regroup.1.refs_0_), channel_id=1, source_target_pairs={{0,16},{2,18},{4,20},{6,22},{8,24},{10,26},{12,28},{14,30},{16,0},... | collective-permute-start | bytes 387080 | tf_op jit(solution)/shard_map/ppermute | solution.py:587
  19.3 0.4 %collective-permute-done.3.refs_1_ = bf16[304,256]{1,0:T(8,128)(2,1)S(1)} collective-permute-done((bf16[304,256]{1,0:T(8,128)(2,1)S(1)}, bf16[304,256]{1,0:T(8,128)(2,1)S(1)}, u32[]{:S(2)}, u32[]{:S(2)}) %collective-permute-start.3) | collective-permute-done | bytes 155680 | tf_op jit(solution)/shard_map/ppermute | solution.py:591
  19.6 2.2 %collective-permute-start.15 = (bf16[72,896]{1,0:T(8,128)(2,1)S(1)}, bf16[72,896]{1,0:T(8,128)(2,1)S(1)}, u32[]{:S(2)}, u32[]{:S(2)}) collective-permute-start(bf16[72,896]{1,0:T(8,128)(2,1)S(1)} %regroup.1.refs_0_), channel_id=1, source_target_pairs={{0,24},{2,26},{4,28},{6,30},{8,0},{10,2},{12,4},{14,6},{16,8},{18,... | collective-permute-start | bytes 387080 | tf_op jit(solution)/shard_map/ppermute | solution.py:587
  21.8 0.7 %collective-permute-done.4.refs_2_ = bf16[304,256]{1,0:T(8,128)(2,1)S(1)} collective-permute-done((bf16[304,256]{1,0:T(8,128)(2,1)S(1)}, bf16[304,256]{1,0:T(8,128)(2,1)S(1)}, u32[]{:S(2)}, u32[]{:S(2)}) %collective-permute-start.4) | collective-permute-done | bytes 155680 | tf_op jit(solution)/shard_map/ppermute | solution.py:591
  22.5 0.0 collective-permute-done.5.refs_3_
  22.5 3.7 %mid.1 = (bf16[96,256]{1,0:T(8,128)(2,1)S(1)}, bf16[96,256]{1,0:T(8,128)(2,1)S(1)}, bf16[96,256]{1,0:T(8,128)(2,1)S(1)}, bf16[96,256]{1,0:T(8,128)(2,1)S(1)}) custom-call(s32[16]{0:T(128)} %frames_hbm.3, s32[16]{0:T(128)} %assign_hbm.5, bf16[432,384]{1,0:T(8,128)(2,1)} %bitcast.15, f32[1,384]{1,0:T(1,128)S(1)} %broadcast_in_dim.9.gain_ref, ...), custom_call_target="tpu_custom_call" | custom-call | flops 5750000128 | tf_op jit(solution)/shard_map/mid/pallas_call | solution.py:348
  26.2 0.8 %collective-permute-start.6 = (bf16[96,256]{1,0:T(8,128)(2,1)S(1)}, bf16[96,256]{1,0:T(8,128)(2,1)S(1)}, u32[]{:S(2)}, u32[]{:S(2)}) collective-permute-start(bf16[96,256]{1,0:T(8,128)(2,1)S(1)} %get-tuple-element.36), channel_id=1, source_target_pairs={{0,8},{2,10},{4,12},{6,14},{8,16},{10,18},{12,20},{14,22},{16,24},... | collective-permute-start | bytes 147464 | tf_op jit(solution)/shard_map/ppermute | solution.py:587
  27.0 2.0 %collective-permute-start.7 = (bf16[96,256]{1,0:T(8,128)(2,1)S(1)}, bf16[96,256]{1,0:T(8,128)(2,1)S(1)}, u32[]{:S(2)}, u32[]{:S(2)}) collective-permute-start(bf16[96,256]{1,0:T(8,128)(2,1)S(1)} %get-tuple-element.37), channel_id=1, source_target_pairs={{0,16},{2,18},{4,20},{6,22},{8,24},{10,26},{12,28},{14,30},{16,0},... | collective-permute-start | bytes 147464 | tf_op jit(solution)/shard_map/ppermute | solution.py:587
  29.0 0.0 collective-permute-done.13.refs_1_
  29.0 1.1 %collective-permute-start.8 = (bf16[96,256]{1,0:T(8,128)(2,1)S(1)}, bf16[96,256]{1,0:T(8,128)(2,1)S(1)}, u32[]{:S(2)}, u32[]{:S(2)}) collective-permute-start(bf16[96,256]{1,0:T(8,128)(2,1)S(1)} %get-tuple-element.38), channel_id=1, source_target_pairs={{0,24},{2,26},{4,28},{6,30},{8,0},{10,2},{12,4},{14,6},{16,8},{18,... | collective-permute-start | bytes 147464 | tf_op jit(solution)/shard_map/ppermute | solution.py:587
  30.1 0.0 collective-permute-done.14.refs_2_
  30.1 0.0 collective-permute-done.15.refs_3_
  30.1 1.0 %prep.1 = (bf16[288,896]{1,0:T(8,128)(2,1)S(1)}, bf16[192,192]{1,0:T(8,128)(2,1)S(1)}, bf16[3,256,256]{2,1,0:T(8,128)(2,1)S(1)}, f32[192,128]{1,0:T(8,128)S(1)},...) custom-call(s32[16]{0:T(128)} %frames_hbm.3, s32[16]{0:T(128)} %assign_hbm.5, f32[1,192]{1,0:T(1,128)} %bitcast.12, ...), custom_call_target="tpu_custom_call" | custom-call | flops 11500000 | tf_op jit(solution)/shard_map/prep/pallas_call | solution.py:425
  31.1 0.1 collective-permute-start.16
  31.2 1.1 %collective-permute-done.6.refs_1_ = bf16[96,256]{1,0:T(8,128)(2,1)S(1)} collective-permute-done((bf16[96,256]{1,0:T(8,128)(2,1)S(1)}, bf16[96,256]{1,0:T(8,128)(2,1)S(1)}, u32[]{:S(2)}, u32[]{:S(2)}) %collective-permute-start.6) | collective-permute-done | bytes 49184 | tf_op jit(solution)/shard_map/ppermute | solution.py:587
  32.3 1.2 %collective-permute-done.7.refs_2_ = bf16[96,256]{1,0:T(8,128)(2,1)S(1)} collective-permute-done((bf16[96,256]{1,0:T(8,128)(2,1)S(1)}, bf16[96,256]{1,0:T(8,128)(2,1)S(1)}, u32[]{:S(2)}, u32[]{:S(2)}) %collective-permute-start.7) | collective-permute-done | bytes 49184 | tf_op jit(solution)/shard_map/ppermute | solution.py:587
  33.4 0.2 collective-permute-done.8.refs_3_
  33.6 0.1 collective-permute-start.9
  33.7 0.0 collective-permute-done.16.other
  33.7 1.2 %wide.1.w_all = bf16[576,1152]{1,0:T(8,128)(2,1)S(1)} custom-call(bf16[288,896]{1,0:T(8,128)(2,1)S(1)} %get-tuple-element.43.own, bf16[288,896]{1,0:T(8,128)(2,1)S(1)} %collective-permute-done.16.other, bf16[192,192]{1,0:T(8,128)(2,1)S(1)} %get-tuple-element.44.order), custom_call_target="tpu_custom_call" | custom-call | flops 11500000 | tf_op jit(solution)/shard_map/wide/pallas_call | solution.py:467
  34.9 0.2 collective-permute-done.9.other
  35.2 3.4 %finish.1 = bf16[1,4,8,6144]{3,2,1,0:T(8,128)(2,1)} custom-call(bf16[384,256]{1,0:T(8,128)(2,1)S(1)} %stack.1.own, bf16[384,256]{1,0:T(8,128)(2,1)S(1)} %collective-permute-done.9.other, bf16[576,1152]{1,0:T(8,128)(2,1)S(1)} %wide.1.w_all, bf16[3,256,256]{2,1,0:T(8,128)(2,1)S(1)} %get-tuple-element.45.pick, f32[192,128]{1,0:T(8,128)S(1)} %get-tuple-element.46.gmid_ref, ...), custom_call_target="tpu_custom_call" | custom-call | flops 5520000000 | tf_op jit(solution)/shard_map/finish/pallas_call | solution.py:570
  (7 shorter events, 0.1 us)
Async XLA Ops:
  0.0 9.0 %copy-start = (bf16[12,27,96]{2,1,0:T(8,128)(2,1)S(1)}, bf16[12,27,96]{2,1,0:T(8,128)(2,1)}, u32[]{:S(2)}) copy-start(bf16[12,27,96]{2,1,0:T(8,128)(2,1)} %param.16) | copy-start | bytes 186628
  0.0 12.3 %copy-start.1 = (f32[384]{0:T(512)S(1)}, f32[384]{0:T(512)}, u32[]{:S(2)}) copy-start(f32[384]{0:T(512)} %param.17) | copy-start | bytes 4612
  2.0 10.3 %collective-permute-start = (bf16[96,256]{1,0:T(8,128)(2,1)S(1)}, bf16[96,256]{1,0:T(8,128)(2,1)S(1)}, u32[]{:S(2)}, u32[]{:S(2)}) collective-permute-start(bf16[96,256]{1,0:T(8,128)(2,1)S(1)} %get-tuple-element.28), channel_id=1, source_target_pairs={{0,8},{2,10},{4,12},{6,14},{8,16},{10,18},{12,20},{14,22},{16,24},... | collective-permute-start | bytes 147464 | tf_op jit(solution)/shard_map/ppermute | solution.py:587
  5.1 7.8 %collective-permute-start.1 = (bf16[96,256]{1,0:T(8,128)(2,1)S(1)}, bf16[96,256]{1,0:T(8,128)(2,1)S(1)}, u32[]{:S(2)}, u32[]{:S(2)}) collective-permute-start(bf16[96,256]{1,0:T(8,128)(2,1)S(1)} %get-tuple-element.29), channel_id=1, source_target_pairs={{0,16},{2,18},{4,20},{6,22},{8,24},{10,26},{12,28},{14,30},{16,0},... | collective-permute-start | bytes 147464 | tf_op jit(solution)/shard_map/ppermute | solution.py:587
  7.6 5.2 %collective-permute-start.2 = (bf16[96,256]{1,0:T(8,128)(2,1)S(1)}, bf16[96,256]{1,0:T(8,128)(2,1)S(1)}, u32[]{:S(2)}, u32[]{:S(2)}) collective-permute-start(bf16[96,256]{1,0:T(8,128)(2,1)S(1)} %get-tuple-element.30), channel_id=1, source_target_pairs={{0,24},{2,26},{4,28},{6,30},{8,0},{10,2},{12,4},{14,6},{16,8},{18,... | collective-permute-start | bytes 147464 | tf_op jit(solution)/shard_map/ppermute | solution.py:587
  9.2 6.9 %collective-permute-start.10 = (bf16[24,896]{1,0:T(8,128)(2,1)S(1)}, bf16[24,896]{1,0:T(8,128)(2,1)S(1)}, u32[]{:S(2)}, u32[]{:S(2)}) collective-permute-start(bf16[24,896]{1,0:T(8,128)(2,1)S(1)} %pad_bitcast_fusion.refs_0_), channel_id=1, source_target_pairs={{0,2},{2,0},{4,6},{6,4},{8,10},{10,8},{12,14},{14,12},{16,18},{18,... | collective-permute-start | bytes 129032 | tf_op jit(solution)/shard_map/ppermute | solution.py:591
  10.7 5.8 %collective-permute-start.11 = (bf16[24,896]{1,0:T(8,128)(2,1)S(1)}, bf16[24,896]{1,0:T(8,128)(2,1)S(1)}, u32[]{:S(2)}, u32[]{:S(2)}) collective-permute-start(bf16[24,896]{1,0:T(8,128)(2,1)S(1)} %pad_bitcast_fusion.refs_0_), channel_id=1, source_target_pairs={{0,4},{2,6},{4,0},{6,2},{8,12},{10,14},{12,8},{14,10},{16,20},{18,... | collective-permute-start | bytes 129032 | tf_op jit(solution)/shard_map/ppermute | solution.py:591
  12.3 5.2 %collective-permute-start.12 = (bf16[24,896]{1,0:T(8,128)(2,1)S(1)}, bf16[24,896]{1,0:T(8,128)(2,1)S(1)}, u32[]{:S(2)}, u32[]{:S(2)}) collective-permute-start(bf16[24,896]{1,0:T(8,128)(2,1)S(1)} %pad_bitcast_fusion.refs_0_), channel_id=1, source_target_pairs={{0,6},{2,4},{4,2},{6,0},{8,14},{10,12},{12,10},{14,8},{16,22},{18,... | collective-permute-start | bytes 129032 | tf_op jit(solution)/shard_map/ppermute | solution.py:591
  13.0 6.7 %collective-permute-start.3 = (bf16[304,256]{1,0:T(8,128)(2,1)S(1)}, bf16[304,256]{1,0:T(8,128)(2,1)S(1)}, u32[]{:S(2)}, u32[]{:S(2)}) collective-permute-start(bf16[304,256]{1,0:T(8,128)(2,1)S(1)} %get-tuple-element.32), channel_id=1, source_target_pairs={{0,2},{2,0},{4,6},{6,4},{8,10},{10,8},{12,14},{14,12},{16,18},{18,... | collective-permute-start | bytes 466952 | tf_op jit(solution)/shard_map/ppermute | solution.py:591
  14.5 8.0 %collective-permute-start.4 = (bf16[304,256]{1,0:T(8,128)(2,1)S(1)}, bf16[304,256]{1,0:T(8,128)(2,1)S(1)}, u32[]{:S(2)}, u32[]{:S(2)}) collective-permute-start(bf16[304,256]{1,0:T(8,128)(2,1)S(1)} %get-tuple-element.33), channel_id=1, source_target_pairs={{0,4},{2,6},{4,0},{6,2},{8,12},{10,14},{12,8},{14,10},{16,20},{18,... | collective-permute-start | bytes 466952 | tf_op jit(solution)/shard_map/ppermute | solution.py:591
  16.0 6.5 %collective-permute-start.5 = (bf16[304,256]{1,0:T(8,128)(2,1)S(1)}, bf16[304,256]{1,0:T(8,128)(2,1)S(1)}, u32[]{:S(2)}, u32[]{:S(2)}) collective-permute-start(bf16[304,256]{1,0:T(8,128)(2,1)S(1)} %get-tuple-element.34), channel_id=1, source_target_pairs={{0,6},{2,4},{4,2},{6,0},{8,14},{10,12},{12,10},{14,8},{16,22},{18,... | collective-permute-start | bytes 466952 | tf_op jit(solution)/shard_map/ppermute | solution.py:591
  17.5 11.5 %collective-permute-start.13 = (bf16[72,896]{1,0:T(8,128)(2,1)S(1)}, bf16[72,896]{1,0:T(8,128)(2,1)S(1)}, u32[]{:S(2)}, u32[]{:S(2)}) collective-permute-start(bf16[72,896]{1,0:T(8,128)(2,1)S(1)} %regroup.1.refs_0_), channel_id=1, source_target_pairs={{0,8},{2,10},{4,12},{6,14},{8,16},{10,18},{12,20},{14,22},{16,24},... | collective-permute-start | bytes 387080 | tf_op jit(solution)/shard_map/ppermute | solution.py:587
  18.1 12.0 %collective-permute-start.14 = (bf16[72,896]{1,0:T(8,128)(2,1)S(1)}, bf16[72,896]{1,0:T(8,128)(2,1)S(1)}, u32[]{:S(2)}, u32[]{:S(2)}) collective-permute-start(bf16[72,896]{1,0:T(8,128)(2,1)S(1)} %regroup.1.refs_0_), channel_id=1, source_target_pairs={{0,16},{2,18},{4,20},{6,22},{8,24},{10,26},{12,28},{14,30},{16,0},... | collective-permute-start | bytes 387080 | tf_op jit(solution)/shard_map/ppermute | solution.py:587
  19.6 10.5 %collective-permute-start.15 = (bf16[72,896]{1,0:T(8,128)(2,1)S(1)}, bf16[72,896]{1,0:T(8,128)(2,1)S(1)}, u32[]{:S(2)}, u32[]{:S(2)}) collective-permute-start(bf16[72,896]{1,0:T(8,128)(2,1)S(1)} %regroup.1.refs_0_), channel_id=1, source_target_pairs={{0,24},{2,26},{4,28},{6,30},{8,0},{10,2},{12,4},{14,6},{16,8},{18,... | collective-permute-start | bytes 387080 | tf_op jit(solution)/shard_map/ppermute | solution.py:587
  26.2 6.0 %collective-permute-start.6 = (bf16[96,256]{1,0:T(8,128)(2,1)S(1)}, bf16[96,256]{1,0:T(8,128)(2,1)S(1)}, u32[]{:S(2)}, u32[]{:S(2)}) collective-permute-start(bf16[96,256]{1,0:T(8,128)(2,1)S(1)} %get-tuple-element.36), channel_id=1, source_target_pairs={{0,8},{2,10},{4,12},{6,14},{8,16},{10,18},{12,20},{14,22},{16,24},... | collective-permute-start | bytes 147464 | tf_op jit(solution)/shard_map/ppermute | solution.py:587
  27.0 6.4 %collective-permute-start.7 = (bf16[96,256]{1,0:T(8,128)(2,1)S(1)}, bf16[96,256]{1,0:T(8,128)(2,1)S(1)}, u32[]{:S(2)}, u32[]{:S(2)}) collective-permute-start(bf16[96,256]{1,0:T(8,128)(2,1)S(1)} %get-tuple-element.37), channel_id=1, source_target_pairs={{0,16},{2,18},{4,20},{6,22},{8,24},{10,26},{12,28},{14,30},{16,0},... | collective-permute-start | bytes 147464 | tf_op jit(solution)/shard_map/ppermute | solution.py:587
  29.0 4.6 %collective-permute-start.8 = (bf16[96,256]{1,0:T(8,128)(2,1)S(1)}, bf16[96,256]{1,0:T(8,128)(2,1)S(1)}, u32[]{:S(2)}, u32[]{:S(2)}) collective-permute-start(bf16[96,256]{1,0:T(8,128)(2,1)S(1)} %get-tuple-element.38), channel_id=1, source_target_pairs={{0,24},{2,26},{4,28},{6,30},{8,0},{10,2},{12,4},{14,6},{16,8},{18,... | collective-permute-start | bytes 147464 | tf_op jit(solution)/shard_map/ppermute | solution.py:587
  31.1 2.6 %collective-permute-start.16 = (bf16[288,896]{1,0:T(8,128)(2,1)S(1)}, bf16[288,896]{1,0:T(8,128)(2,1)S(1)}, u32[]{:S(2)}, u32[]{:S(2)}) collective-permute-start(bf16[288,896]{1,0:T(8,128)(2,1)S(1)} %get-tuple-element.43.own), channel_id=1, source_target_pairs={{0,1},{1,0},{2,3},{3,2},{4,5},{5,4},{6,7},{7,6},{8,9},{9,8},{10,11... | collective-permute-start | bytes 1548296 | tf_op jit(solution)/shard_map/ppermute | solution.py:595
  33.6 1.5 %collective-permute-start.9 = (bf16[384,256]{1,0:T(8,128)(2,1)S(1)}, bf16[384,256]{1,0:T(8,128)(2,1)S(1)}, u32[]{:S(2)}, u32[]{:S(2)}) collective-permute-start(bf16[384,256]{1,0:T(8,128)(2,1)S(1)} %stack.1.own), channel_id=1, source_target_pairs={{0,1},{1,0},{2,3},{3,2},{4,5},{5,4},{6,7},{7,6},{8,9},{9,8},{10,11... | collective-permute-start | bytes 589832 | tf_op jit(solution)/shard_map/ppermute | solution.py:595

commit v6 on v5

--- a/solution.py
+++ b/solution.py
@@ -118,9 +118,11 @@
 IN_SH = C1 // 16
 MID_SH = C2 // 16
 OUT_BLK = C2 // (2 * LINE)
-PIECE_ROWS = 96
+PIECE_ROWS = 80
+USED = 9 * (C2 // (2 * LINE))
+SPARE = 256 - USED
 W_ROWS = 3 * IN_SH
-B_ROWS = LINE * W_ROWS + LINE * LINE
+B_ROWS = LINE * W_ROWS
 WOUT_LANES = 896
 HALF_CH = C2 // 2
 F32, BF16 = jnp.float32, jnp.bfloat16
@@ -154,8 +156,22 @@
     return lax.dot_general(lhs, rhs, (((1,), (1,)), ((), ())), preferred_element_type=F32)
 
 
+def hidden_lanes(table, part):
+    moved = pltpu.roll(table, (USED - SPARE * part) % 256, 1)
+    return jnp.where(iota(table.shape, 1) >= USED, moved, 0.0)
+
+
+def found_lanes(rows, parts):
+    table = jnp.zeros((TOK, 256), F32)
+    for part in range(parts):
+        moved = pltpu.roll(rows[TOK * part : TOK * (part + 1)], (SPARE * part - USED) % 256, 1)
+        lane = iota((TOK, 256), 1)
+        table = jnp.where((lane >= SPARE * part) & (lane < SPARE * (part + 1)), moved, table)
+    return table
+
+
 def pack_kernel(offsets_hbm, assign_hbm, w_hbm, lat_hbm, *refs):
-    outs, (wf, lf, pf, w_ref, lat_ref, offsets, assign, sems) = refs[:LINE], refs[LINE:]
+    outs, (wf, lf, pf, tab, lat_rows, w_ref, lat_ref, offsets, assign, sems) = refs[:LINE], refs[LINE:]
     parts = [pl.ds(9 * a, 9) for a in range(3)]
     moves = [(w_hbm.at[p], w_ref.at[p]) for p in parts]
     moves = [(offsets_hbm, offsets), (assign_hbm, assign), (lat_hbm, lat_ref)] + moves
@@ -165,9 +181,8 @@
     z, _, c = place()
     lf[32:40, :] = jnp.zeros((8, 128), F32)
     for k in range(LINE):
-        pf[k, TOK:, :] = jnp.zeros((PIECE_ROWS - TOK, 256), F32)
+        pf[k, W_ROWS:, :] = jnp.zeros((PIECE_ROWS - W_ROWS, 256), F32)
     lane1 = iota((1, 128), 1)
-    lane = iota((IN_SH, 256), 1)
     for copy in copies[:3]:
         copy.wait()
     lat = lat_ref[...].astype(F32)
@@ -178,25 +193,42 @@
         row, rem = lax.div(off, 8), lax.rem(off, 8)
         x = pltpu.roll(lf[pl.ds(row, 8), :], lax.rem(128 - ZC * rem, 128), 1)
         keep = lane1 < 128 - ZC * rem
-        pf[0, g : g + 1, 0:128] = jnp.where(keep, x[0:1], x[1:2])
-        pf[0, g : g + 1, 128:256] = jnp.where(keep, x[1:2], x[2:3])
-    for k in range(1, LINE):
-        pf[k, 0:TOK, :] = pf[0, 0:TOK, :]
+        tab[g : g + 1, 0:128] = jnp.where(keep, x[0:1], x[1:2])
+        tab[g : g + 1, 128:256] = jnp.where(keep, x[1:2], x[2:3])
+    table = tab[...]
+    for part in range(4):
+        lat_rows[TOK * part : TOK * (part + 1), :] = hidden_lanes(table, part)
+    lat_rows[4 * TOK : W_ROWS, :] = jnp.zeros((W_ROWS - 4 * TOK, 256), F32)
+    low, high = pltpu.roll(table, 256 - 4 * SPARE, 1)[:8], pltpu.roll(table, 512 - 8 * SPARE, 1)[8:]
+    lat_rows[W_ROWS:, :] = jnp.where(iota((8, 256), 1) < 256 - 4 * SPARE, low, high)
     for a in range(3):
         copies[3 + a].wait()
         wf[9 * a : 9 * a + 9, :, :C2] = w_ref[9 * a : 9 * a + 9].astype(F32)
-        for k in range(LINE):
-            first = (lax.rem(z + k, LINE) * 2 + c) * OUT_BLK
+    lane = iota((IN_SH, 128), 1)
+
+    def choose(core):
+        for line in range(LINE):
+            start = (2 * line + core) * OUT_BLK
+            tile, into = start // 128, start % 128
             for b in range(3):
-                rows = slice(TOK + IN_SH * b, TOK + IN_SH * (b + 1))
-                acc = pf[k, rows, :]
-                for e in range(3):
-                    at = OUT_BLK * (3 * a + e)
-                    moved = pltpu.roll(wf[9 * a + 3 * b + e], lax.rem(at - first + 256, 256), 1)
-                    acc = jnp.where((lane >= at) & (lane < at + OUT_BLK), moved, acc)
-                pf[k, rows, :] = acc
+                acc = [jnp.zeros((IN_SH, 128), F32)] * 2
+                for j in range(9):
+                    tap = 9 * (j // 3) + 3 * b + j % 3
+                    x = wf[tap, :, 128 * tile : 128 * tile + 128]
+                    if into + OUT_BLK > 128:
+                        x = jnp.where(lane >= into, x, wf[tap, :, 128 : 256])
+                    at, to = OUT_BLK * j // 128, OUT_BLK * j % 128
+                    moved = pltpu.roll(x, (to - into) % 128, 1)
+                    acc[at] = jnp.where((lane >= to) & (lane < to + OUT_BLK), moved, acc[at])
+                    if to + OUT_BLK > 128:
+                        acc[at + 1] = jnp.where(lane < to + OUT_BLK - 128, moved, acc[at + 1])
+                for half in range(2):
+                    pf[line, IN_SH * b : IN_SH * (b + 1), 128 * half : 128 * half + 128] = acc[half]
+
+    for core in range(2):
+        pl.when(c == core)(functools.partial(choose, core))
     for k in range(LINE):
-        outs[k][...] = pf[k].astype(BF16)
+        outs[k][...] = (pf[lax.rem(z + k, LINE)] + lat_rows[...]).astype(BF16)
 
 
 def pack(offsets, assign, w_mid, latents):
@@ -210,6 +242,8 @@
             pltpu.VMEM((27, IN_SH, 256), F32),
             pltpu.VMEM((40, 128), F32),
             pltpu.VMEM((LINE, PIECE_ROWS, 256), F32),
+            pltpu.VMEM((TOK, 256), F32),
+            pltpu.VMEM((PIECE_ROWS, 256), F32),
             pltpu.VMEM((27, IN_SH, C2), BF16),
             pltpu.VMEM(latents.shape, BF16),
             pltpu.SMEM(offsets.shape, jnp.int32),
@@ -223,18 +257,26 @@
 
 
 def join_kernel(*refs):
-    pieces, outs, (pf, bf) = refs[:LINE], refs[LINE : LINE + PLANE], refs[LINE + PLANE :]
+    pieces, outs, (pf, bf, tab) = refs[:LINE], refs[LINE : LINE + PLANE], refs[LINE + PLANE :]
     _, q, _ = place()
+    lane = iota((8, 256), 1)
     for k in range(LINE):
         whole = pieces[k][...].astype(F32)
-        pf[TOK * k : TOK * (k + 1), :] = whole[:TOK]
-        bf[W_ROWS * k : W_ROWS * (k + 1), :] = whole[TOK : TOK + W_ROWS]
-    base = LINE * W_ROWS
+        bf[W_ROWS * k : W_ROWS * (k + 1), :] = whole[:W_ROWS]
+        table, rest = found_lanes(whole, 4), whole[W_ROWS:]
+        low, high = pltpu.roll(rest, 4 * SPARE, 1), pltpu.roll(rest, 8 * SPARE - 256, 1)
+        pf[TOK * k : TOK * k + 8, :] = jnp.where(lane >= 4 * SPARE, low, table[:8])
+        pf[TOK * k + 8 : TOK * (k + 1), :] = jnp.where(lane >= 4 * SPARE, high, table[8:])
     for d in range(PLANE):
         for k in range(LINE):
             for line in range(LINE):
-                at = base + LINE * k + line
-                bf[at : at + 1, :] = pf[pl.ds(TOK * k + PLANE * line + (q ^ d), 1), :]
+                at = LINE * k + line
+                tab[at : at + 1, :] = pf[pl.ds(TOK * k + PLANE * line + (q ^ d), 1), :]
+        table = tab[...]
+        keep = iota((TOK, 256), 1) < USED
+        for part in range(7):
+            rows = slice(TOK * part, TOK * (part + 1))
+            bf[rows, :] = jnp.where(keep, bf[rows, :], hidden_lanes(table, part))
         outs[d][...] = bf[...].astype(BF16)
 
 
@@ -245,7 +287,11 @@
         out_shape=[out] * PLANE,
         in_specs=[VMEM()] * LINE,
         out_specs=[VMEM()] * PLANE,
-        scratch_shapes=[pltpu.VMEM((LINE * TOK, 256), F32), pltpu.VMEM((B_ROWS, 256), F32)],
+        scratch_shapes=[
+            pltpu.VMEM((LINE * TOK, 256), F32),
+            pltpu.VMEM((B_ROWS, 256), F32),
+            pltpu.VMEM((TOK, 256), F32),
+        ],
         compiler_params=pltpu.CompilerParams(vmem_limit_bytes=32 << 20),
         cost_estimate=cost(5),
         name="join",
@@ -256,7 +302,6 @@
     parts, outs = refs[:PLANE], refs[PLANE : PLANE + LINE]
     lt, xs, tokens, shifted, w1, act, wf, frames, assign, sems = refs[PLANE + LINE :]
     z, q, _ = place()
-    base = LINE * W_ROWS
     moves = [(frames_hbm, frames), (assign_hbm, assign), (win_hbm, w1.at[0 : 27 * ZC])]
     loads = [pltpu.make_async_copy(src, dst, sems.at[i]) for i, (src, dst) in enumerate(moves)]
     for load in loads:
@@ -264,7 +309,7 @@
     w1[27 * ZC :, :] = jnp.zeros((512 - 27 * ZC, C1), BF16)
     for d in range(PLANE):
         part = parts[d][...].astype(F32)
-        lt[...] = part[base:]
+        lt[...] = found_lanes(part, 7)
         for k in range(LINE):
             shard = lax.rem(z - k + LINE, LINE) * PLANE + (q ^ d)
             for b in range(3):
@@ -368,27 +413,26 @@
     )(*in_hbm(frames, assign, w_in), gain_in, *parts)
 
 
-def regroup_kernel(*refs):
-    parts, out, rows = refs[:PLANE], refs[PLANE], refs[PLANE + 1]
-    for d in range(PLANE):
-        part = parts[d][...].astype(F32)
-        for b in range(3):
-            at = OUT_BLK * b + 6 * d
-            rows[at : at + 6, :] = part[8 * b : 8 * b + 6]
+def regroup_kernel(half, near, far, out, rows):
+    for b in range(3):
+        at = OUT_BLK * b
+        rows[at : at + 6, :] = half[8 * b : 8 * b + 6, :].astype(F32)
+        rows[at + 6 : at + 18, :] = near[16 * b : 16 * b + 16, :].astype(F32)[:MID_SH]
+        rows[at + 18 : at + 24, :] = far[8 * b : 8 * b + 6, :].astype(F32)
     out[...] = rows[...].astype(BF16)
 
 
-def regroup(parts):
+def regroup(half, near, far):
     return pl.pallas_call(
         regroup_kernel,
         out_shape=jax.ShapeDtypeStruct((3 * OUT_BLK, WOUT_LANES), BF16),
-        in_specs=[VMEM()] * PLANE,
+        in_specs=[VMEM()] * 3,
         out_specs=VMEM(),
         scratch_shapes=[pltpu.VMEM((3 * OUT_BLK, WOUT_LANES), F32)],
         cost_estimate=cost(5),
         compiler_params=pltpu.CompilerParams(vmem_limit_bytes=32 << 20),
         name="regroup",
-    )(*parts)
+    )(half, near, far)
 
 
 def prep_kernel(frames_hbm, assign_hbm, gmid_hbm, gout_hbm, *refs):
@@ -402,9 +446,12 @@
     for k in range(LINE):
         raw[3 * OUT_BLK * k : 3 * OUT_BLK * (k + 1), :] = parts[k][...]
     row, channel = iota((C2, C2), 0), iota((C2, C2), 1)
-    side, step = row // HALF_CH, row % HALF_CH // OUT_BLK
+    side, step, in_shard = row // HALF_CH, row % HALF_CH // OUT_BLK, row % MID_SH
     flip = q ^ (2 * (c ^ side) + row % OUT_BLK // MID_SH)
-    held = (c ^ (row % MID_SH // 6)) * HALF_CH + step * OUT_BLK + 6 * flip + row % 6
+    near = (flip == 1) | (flip == 2)
+    holder = jnp.where(near, flip - 1, in_shard // 6)
+    slot = jnp.where(near, 6 + in_shard, 6 * flip + in_shard % 6)
+    held = (c ^ holder) * HALF_CH + step * OUT_BLK + slot
     order_out[...] = (channel == held).astype(F32).astype(BF16)
     r, l = iota((256, 256), 0), iota((256, 256), 1)
     same = (r // 8) == ((l // 64) % 2) * WL + l % WL
@@ -495,7 +542,7 @@
     )(*parts)
 
 
-def out_kernel(own, other, w_all, pick, gmid_ref, gout_ref, limit_ref, out_ref, hid, lhs, prod):
+def out_kernel(own, other, w_all, pick, gmid_ref, gout_ref, limit_ref, out_hbm, hid, lhs, prod, out_ref, sems):
     for side, group in enumerate((own, other)):
         for k in range(LINE):
             part = group[96 * k : 96 * k + 96, :].astype(F32)
@@ -518,16 +565,20 @@
                 rows = dot_nt(pick[b], src).astype(BF16)
                 for half in range(2):
                     lhs[2 * tp + half, px, :, C2 * b : C2 * b + C2] = rows[128 * half : 128 * half + 128]
-    prod[0:2] = jnp.dot(lhs[0:2].reshape(512, 3 * C2), w_all[...], preferred_element_type=F32).reshape(2, 2, 128, 1152)
-    for t in (2, 3):
-        at = 384 * (t - 1)
-        prod[t, :, :, at:] = jnp.dot(
-            lhs[t].reshape(256, 3 * C2), w_all[:, at:], preferred_element_type=F32
-        ).reshape(2, 128, 1152 - at)
     lane = iota((1, 8, 128), 2)
     limit = limit_ref[...]
     below = [lane < 128 - 32 * i for i in range(4)]
-    for t in range(FMAX):
+    def multiply(t):
+        if t == 0:
+            both = jnp.dot(lhs[0:2].reshape(512, 3 * C2), w_all[...], preferred_element_type=F32)
+            prod[0:2] = both.reshape(2, 2, 128, 1152)
+        elif t > 1:
+            at = 384 * (t - 1)
+            prod[t, :, :, at:] = jnp.dot(
+                lhs[t].reshape(256, 3 * C2), w_all[:, at:], preferred_element_type=F32
+            ).reshape(2, 128, 1152 - at)
+
+    def combine(t):
         sums = []
         for px in range(2):
             row = []
@@ -565,17 +616,34 @@
             both = jnp.concatenate([tile[x] for tile in tiles], axis=1)
             out_ref[0, t, :, 384 * x : 384 * x + 384] = both.astype(BF16)
 
+    copies = [pltpu.make_async_copy(out_ref.at[:, t], out_hbm.at[:, t], sems.at[t]) for t in range(FMAX)]
+    multiply(0)
+    multiply(2)
+    combine(0)
+    copies[0].start()
+    multiply(3)
+    combine(1)
+    copies[1].start()
+    combine(2)
+    copies[2].start()
+    combine(3)
+    copies[3].start()
+    for copy in copies:
+        copy.wait()
+
 
 def finish(*rest):
     return pl.pallas_call(
         out_kernel,
         out_shape=jax.ShapeDtypeStruct((1, FMAX, 4 * RL, 4 * WL * C3), BF16),
         in_specs=[VMEM()] * len(rest),
-        out_specs=VMEM(),
+        out_specs=HBM(),
         scratch_shapes=[
             pltpu.VMEM((4, 2, C2, 128), F32),
             pltpu.VMEM((4, 2, 128, 3 * C2), BF16),
             pltpu.VMEM((4, 2, 128, 1152), F32),
+            pltpu.VMEM((1, FMAX, 4 * RL, 4 * WL * C3), BF16),
+            pltpu.SemaphoreType.DMA((FMAX,)),
         ],
         compiler_params=pltpu.CompilerParams(vmem_limit_bytes=48 << 20),
         cost_estimate=cost(4.8),
@@ -589,6 +657,11 @@
 
 def in_plane(value, flip):
     return lax.ppermute(value, "grp", [(g, g ^ flip) for g in range(LINE * PLANE)])
+
+
+def near_chip(value):
+    pairs = [(2 * g + c, 2 * (g ^ (1 + c)) + c) for g in range(LINE * PLANE) for c in range(2)]
+    return lax.ppermute(value, ("grp", "row"), pairs)
 
 
 def other_core(value):
@@ -601,10 +674,11 @@
     pieces = [pieces[0]] + [along_z(pieces[k], k) for k in range(1, LINE)]
     parts = join(pieces)
     parts = [parts[0]] + [in_plane(parts[d], d) for d in range(1, PLANE)]
-    rows = lax.dynamic_slice_in_dim(w_out, core * 6, 6, axis=0)
-    rows = rows.reshape(6, 3, 3, 3, C3).transpose(2, 0, 1, 3, 4).reshape(3, 6, 9 * C3)
-    half = jnp.pad(rows, ((0, 0), (0, 2), (0, WOUT_LANES - 9 * C3))).reshape(24, WOUT_LANES)
-    plane = regroup([half] + [in_plane(half, d) for d in range(1, PLANE)])
+    full = w_out.reshape(MID_SH, 3, 3, 3, C3).transpose(2, 0, 1, 3, 4).reshape(3, MID_SH, 9 * C3)
+    half = lax.dynamic_slice_in_dim(full, core * 6, 6, axis=1)
+    full = jnp.pad(full, ((0, 0), (0, 16 - MID_SH), (0, WOUT_LANES - 9 * C3))).reshape(48, WOUT_LANES)
+    half = jnp.pad(half, ((0, 0), (0, 2), (0, WOUT_LANES - 9 * C3))).reshape(24, WOUT_LANES)
+    plane = regroup(half, near_chip(full), in_plane(half, 3))
     own = [plane] + [along_z(plane, k) for k in range(1, LINE)]
     hidden = mid(frames, assign, parts, w_in.transpose(1, 0, 2).reshape(27 * ZC, C1), gain_in[None, :])
     own, _ = lax.optimization_barrier((own, hidden[0]))

time: 38.7 us -> 37.9 us (0.979)
  starting transfers between devices: 22.1 us -> 21.3 us
    ppermute x6 -> x4, starting transfers between devices: 7.17 us -> 6.07 us  [in_plane(): lax.ppermute(value, 'grp', [(g, g ^ flip) for g in range(LINE * PLANE)])]
    ppermute x0 -> x1, waiting for transfers between devices: none -> 1.05 us  [near_chip(): return lax.ppermute(value, ('grp', 'row'), pairs)]
    ppermute x0 -> x1, starting transfers between devices: none -> 0.6 us  [near_chip(): return lax.ppermute(value, ('grp', 'row'), pairs)]
    ppermute x6 -> x4, waiting for transfers between devices: 2.04 us -> 1.45 us  [in_plane(): lax.ppermute(value, 'grp', [(g, g ^ flip) for g in range(LINE * PLANE)])]
    pallas_call x1, Pallas kernels: 1.97 us -> 1.56 us  [pack(): pl.pallas_call(pack_kernel, out_shape=[piece] * LINE, in_specs=[HBM()] *...]
    ppermute x9, waiting for transfers between devices: 2.48 us -> 2.09 us  [along_z(): lax.ppermute(value, 'grp', [(g, (g + PLANE * step) % (LINE * PLANE)) for...]
  transfers between devices with their start and end apart: 17 -> 16, of which waited for: 7 -> 6; matrix products, arithmetic and copies ran while one was open for 0% -> 1% of each run, Pallas kernels for 16% -> 17%
where the time goes in v6:
time: 37.9 us; the launch traced here: 37.7 us
  starting transfers between devices  21.3 us (56%)
  Pallas kernels  11.2 us (30%)
  waiting for transfers between devices  4.83 us (13%)
    ppermute x9, starting transfers between devices, along_z(): lax.ppermute(value, 'grp', [(g, (g + PLANE * step) % (LINE * PLANE)) for...  14.5 us
    ppermute x4, starting transfers between devices, in_plane(): lax.ppermute(value, 'grp', [(g, g ^ flip) for g in range(LINE * PLANE)])  6.07 us
    pallas_call x1, Pallas kernels, mid(): pl.pallas_call(mid_kernel, out_shape=[out] * LINE, in_specs=[HBM()] * 3 +...  3.82 us
    pallas_call x1, Pallas kernels, finish(): pl.pallas_call(out_kernel, out_shape=jax.ShapeDtypeStruct((1, FMAX, 4 * R...  3.36 us
    ppermute x9, waiting for transfers between devices, along_z(): lax.ppermute(value, 'grp', [(g, (g + PLANE * step) % (LINE * PLANE)) for...  2.09 us
    pallas_call x1, Pallas kernels, pack(): pl.pallas_call(pack_kernel, out_shape=[piece] * LINE, in_specs=[HBM()] *...  1.56 us
    ppermute x4, waiting for transfers between devices, in_plane(): lax.ppermute(value, 'grp', [(g, g ^ flip) for g in range(LINE * PLANE)])  1.45 us
    pallas_call x1, Pallas kernels, wide(): pl.pallas_call(wide_kernel, out_shape=jax.ShapeDtypeStruct((3 * C2, 1152)...  1.17 us
  transfers between devices with their start and end apart: 16, of which 6 were waited for; matrix products, arithmetic and copies ran while one was open for 1% of the time, Pallas kernels for 17%

profile of v6, /device:TPU:0, one launch (start us, length us, event | category | flops | bytes accessed | tf_op | source)
XLA Modules:
  0.0 37.7 jit_solution(11402428339657848746)
XLA Ops:
  0.0 0.0 copy-start
  0.0 0.0 copy-start.1
  0.0 1.6 %pack.1 = (bf16[80,256]{1,0:T(8,128)(2,1)S(1)}, bf16[80,256]{1,0:T(8,128)(2,1)S(1)}, bf16[80,256]{1,0:T(8,128)(2,1)S(1)}, bf16[80,256]{1,0:T(8,128)(2,1)S(1)}) custom-call(s32[16]{0:T(128)} %offsets_hbm.1, s32[16]{0:T(128)} %assign_hbm.5, bf16[27,24,192]{2,1,0:T(8,128)(2,1)} %bitcast.14, bf16[1,4096]{1,0:T(2,128)(2,1)} %lat_hbm.1), custom_call_target="tpu_custom_call" | custom-call | flops 2300000000 | tf_op jit(solution)/shard_map/pack/pallas_call | solution.py:236
  1.6 3.1 %collective-permute-start = (bf16[80,256]{1,0:T(8,128)(2,1)S(1)}, bf16[80,256]{1,0:T(8,128)(2,1)S(1)}, u32[]{:S(2)}, u32[]{:S(2)}) collective-permute-start(bf16[80,256]{1,0:T(8,128)(2,1)S(1)} %get-tuple-element.28), channel_id=1, source_target_pairs={{0,8},{2,10},{4,12},{6,14},{8,16},{10,18},{12,20},{14,22},{16,24},... | collective-permute-start | bytes 122888 | tf_op jit(solution)/shard_map/ppermute | solution.py:655
  4.6 2.6 %collective-permute-start.1 = (bf16[80,256]{1,0:T(8,128)(2,1)S(1)}, bf16[80,256]{1,0:T(8,128)(2,1)S(1)}, u32[]{:S(2)}, u32[]{:S(2)}) collective-permute-start(bf16[80,256]{1,0:T(8,128)(2,1)S(1)} %get-tuple-element.29), channel_id=1, source_target_pairs={{0,16},{2,18},{4,20},{6,22},{8,24},{10,26},{12,28},{14,30},{16,0},... | collective-permute-start | bytes 122888 | tf_op jit(solution)/shard_map/ppermute | solution.py:655
  7.2 1.3 %collective-permute-start.2 = (bf16[80,256]{1,0:T(8,128)(2,1)S(1)}, bf16[80,256]{1,0:T(8,128)(2,1)S(1)}, u32[]{:S(2)}, u32[]{:S(2)}) collective-permute-start(bf16[80,256]{1,0:T(8,128)(2,1)S(1)} %get-tuple-element.30), channel_id=1, source_target_pairs={{0,24},{2,26},{4,28},{6,30},{8,0},{10,2},{12,4},{14,6},{16,8},{18,... | collective-permute-start | bytes 122888 | tf_op jit(solution)/shard_map/ppermute | solution.py:655
  8.6 0.0 copy-done
  8.6 0.1 reshape.16
  8.7 0.1 reshape.17
  8.9 2.5 %collective-permute-start.11 = (bf16[24,896]{1,0:T(8,128)(2,1)S(1)}, bf16[24,896]{1,0:T(8,128)(2,1)S(1)}, u32[]{:S(2)}, u32[]{:S(2)}) collective-permute-start(bf16[24,896]{1,0:T(8,128)(2,1)S(1)} %pad_bitcast_fusion.half), channel_id=1, source_target_pairs={{0,6},{2,4},{4,2},{6,0},{8,14},{10,12},{12,10},{14,8},{16,22},{18,... | collective-permute-start | bytes 129032 | tf_op jit(solution)/shard_map/ppermute | solution.py:659
  11.4 0.6 %collective-permute-start.10 = (bf16[48,896]{1,0:T(8,128)(2,1)S(1)}, bf16[48,896]{1,0:T(8,128)(2,1)S(1)}, u32[]{:S(2)}, u32[]{:S(2)}) collective-permute-start(bf16[48,896]{1,0:T(8,128)(2,1)S(1)} %bitcast.11), channel_id=1, source_target_pairs={{0,2},{1,5},{2,0},{3,7},{4,6},{5,1},{6,4},{7,3},{8,10},{9,13},{10,... | collective-permute-start | bytes 258056 | tf_op jit(solution)/shard_map/ppermute | solution.py:664
  12.0 0.0 copy-done.1
  12.0 0.0 collective-permute-done.refs_1_
  12.0 0.0 collective-permute-done.1.refs_2_
  12.0 0.0 collective-permute-done.2.refs_3_
  12.1 0.3 join.1
  12.3 1.6 %collective-permute-start.3 = (bf16[288,256]{1,0:T(8,128)(2,1)S(1)}, bf16[288,256]{1,0:T(8,128)(2,1)S(1)}, u32[]{:S(2)}, u32[]{:S(2)}) collective-permute-start(bf16[288,256]{1,0:T(8,128)(2,1)S(1)} %get-tuple-element.32), channel_id=1, source_target_pairs={{0,2},{2,0},{4,6},{6,4},{8,10},{10,8},{12,14},{14,12},{16,18},{18,... | collective-permute-start | bytes 442376 | tf_op jit(solution)/shard_map/ppermute | solution.py:659
  13.9 0.7 %collective-permute-start.4 = (bf16[288,256]{1,0:T(8,128)(2,1)S(1)}, bf16[288,256]{1,0:T(8,128)(2,1)S(1)}, u32[]{:S(2)}, u32[]{:S(2)}) collective-permute-start(bf16[288,256]{1,0:T(8,128)(2,1)S(1)} %get-tuple-element.33), channel_id=1, source_target_pairs={{0,4},{2,6},{4,0},{6,2},{8,12},{10,14},{12,8},{14,10},{16,20},{18,... | collective-permute-start | bytes 442376 | tf_op jit(solution)/shard_map/ppermute | solution.py:659
  14.6 1.3 %collective-permute-start.5 = (bf16[288,256]{1,0:T(8,128)(2,1)S(1)}, bf16[288,256]{1,0:T(8,128)(2,1)S(1)}, u32[]{:S(2)}, u32[]{:S(2)}) collective-permute-start(bf16[288,256]{1,0:T(8,128)(2,1)S(1)} %get-tuple-element.34), channel_id=1, source_target_pairs={{0,6},{2,4},{4,2},{6,0},{8,14},{10,12},{12,10},{14,8},{16,22},{18,... | collective-permute-start | bytes 442376 | tf_op jit(solution)/shard_map/ppermute | solution.py:659
  15.9 0.0 collective-permute-done.11.far
  15.9 1.0 %collective-permute-done.10.near = bf16[48,896]{1,0:T(8,128)(2,1)S(1)} collective-permute-done((bf16[48,896]{1,0:T(8,128)(2,1)S(1)}, bf16[48,896]{1,0:T(8,128)(2,1)S(1)}, u32[]{:S(2)}, u32[]{:S(2)}) %collective-permute-start.10) | collective-permute-done | bytes 86048 | tf_op jit(solution)/shard_map/ppermute | solution.py:664
  17.0 0.7 %collective-permute-start.12 = (bf16[72,896]{1,0:T(8,128)(2,1)S(1)}, bf16[72,896]{1,0:T(8,128)(2,1)S(1)}, u32[]{:S(2)}, u32[]{:S(2)}) collective-permute-start(bf16[72,896]{1,0:T(8,128)(2,1)S(1)} %regroup.1.refs_0_), channel_id=1, source_target_pairs={{0,8},{2,10},{4,12},{6,14},{8,16},{10,18},{12,20},{14,22},{16,24},... | collective-permute-start | bytes 387080 | tf_op jit(solution)/shard_map/ppermute | solution.py:655
  17.7 1.2 %collective-permute-start.13 = (bf16[72,896]{1,0:T(8,128)(2,1)S(1)}, bf16[72,896]{1,0:T(8,128)(2,1)S(1)}, u32[]{:S(2)}, u32[]{:S(2)}) collective-permute-start(bf16[72,896]{1,0:T(8,128)(2,1)S(1)} %regroup.1.refs_0_), channel_id=1, source_target_pairs={{0,16},{2,18},{4,20},{6,22},{8,24},{10,26},{12,28},{14,30},{16,0},... | collective-permute-start | bytes 387080 | tf_op jit(solution)/shard_map/ppermute | solution.py:655
  18.9 0.6 %collective-permute-done.3.refs_1_ = bf16[288,256]{1,0:T(8,128)(2,1)S(1)} collective-permute-done((bf16[288,256]{1,0:T(8,128)(2,1)S(1)}, bf16[288,256]{1,0:T(8,128)(2,1)S(1)}, u32[]{:S(2)}, u32[]{:S(2)}) %collective-permute-start.3) | collective-permute-done | bytes 147488 | tf_op jit(solution)/shard_map/ppermute | solution.py:659
  19.5 1.6 %collective-permute-start.14 = (bf16[72,896]{1,0:T(8,128)(2,1)S(1)}, bf16[72,896]{1,0:T(8,128)(2,1)S(1)}, u32[]{:S(2)}, u32[]{:S(2)}) collective-permute-start(bf16[72,896]{1,0:T(8,128)(2,1)S(1)} %regroup.1.refs_0_), channel_id=1, source_target_pairs={{0,24},{2,26},{4,28},{6,30},{8,0},{10,2},{12,4},{14,6},{16,8},{18,... | collective-permute-start | bytes 387080 | tf_op jit(solution)/shard_map/ppermute | solution.py:655
  21.2 0.8 %collective-permute-done.4.refs_2_ = bf16[288,256]{1,0:T(8,128)(2,1)S(1)} collective-permute-done((bf16[288,256]{1,0:T(8,128)(2,1)S(1)}, bf16[288,256]{1,0:T(8,128)(2,1)S(1)}, u32[]{:S(2)}, u32[]{:S(2)}) %collective-permute-start.4) | collective-permute-done | bytes 147488 | tf_op jit(solution)/shard_map/ppermute | solution.py:659
  22.0 0.0 collective-permute-done.5.refs_3_
  22.0 3.8 %mid.1 = (bf16[96,256]{1,0:T(8,128)(2,1)S(1)}, bf16[96,256]{1,0:T(8,128)(2,1)S(1)}, bf16[96,256]{1,0:T(8,128)(2,1)S(1)}, bf16[96,256]{1,0:T(8,128)(2,1)S(1)}) custom-call(s32[16]{0:T(128)} %frames_hbm.3, s32[16]{0:T(128)} %assign_hbm.5, bf16[432,384]{1,0:T(8,128)(2,1)} %bitcast.15, f32[1,384]{1,0:T(1,128)S(1)} %broadcast_in_dim.9.gain_ref, ...), custom_call_target="tpu_custom_call" | custom-call | flops 5750000128 | tf_op jit(solution)/shard_map/mid/pallas_call | solution.py:393
  25.8 0.7 %collective-permute-start.6 = (bf16[96,256]{1,0:T(8,128)(2,1)S(1)}, bf16[96,256]{1,0:T(8,128)(2,1)S(1)}, u32[]{:S(2)}, u32[]{:S(2)}) collective-permute-start(bf16[96,256]{1,0:T(8,128)(2,1)S(1)} %get-tuple-element.36), channel_id=1, source_target_pairs={{0,8},{2,10},{4,12},{6,14},{8,16},{10,18},{12,20},{14,22},{16,24},... | collective-permute-start | bytes 147464 | tf_op jit(solution)/shard_map/ppermute | solution.py:655
  26.5 1.8 %collective-permute-start.7 = (bf16[96,256]{1,0:T(8,128)(2,1)S(1)}, bf16[96,256]{1,0:T(8,128)(2,1)S(1)}, u32[]{:S(2)}, u32[]{:S(2)}) collective-permute-start(bf16[96,256]{1,0:T(8,128)(2,1)S(1)} %get-tuple-element.37), channel_id=1, source_target_pairs={{0,16},{2,18},{4,20},{6,22},{8,24},{10,26},{12,28},{14,30},{16,0},... | collective-permute-start | bytes 147464 | tf_op jit(solution)/shard_map/ppermute | solution.py:655
  28.4 0.0 collective-permute-done.12.refs_1_
  28.4 1.3 %collective-permute-start.8 = (bf16[96,256]{1,0:T(8,128)(2,1)S(1)}, bf16[96,256]{1,0:T(8,128)(2,1)S(1)}, u32[]{:S(2)}, u32[]{:S(2)}) collective-permute-start(bf16[96,256]{1,0:T(8,128)(2,1)S(1)} %get-tuple-element.38), channel_id=1, source_target_pairs={{0,24},{2,26},{4,28},{6,30},{8,0},{10,2},{12,4},{14,6},{16,8},{18,... | collective-permute-start | bytes 147464 | tf_op jit(solution)/shard_map/ppermute | solution.py:655
  29.7 0.0 collective-permute-done.13.refs_2_
  29.7 0.0 collective-permute-done.14.refs_3_
  29.7 1.0 %prep.1 = (bf16[288,896]{1,0:T(8,128)(2,1)S(1)}, bf16[192,192]{1,0:T(8,128)(2,1)S(1)}, bf16[3,256,256]{2,1,0:T(8,128)(2,1)S(1)}, f32[192,128]{1,0:T(8,128)S(1)},...) custom-call(s32[16]{0:T(128)} %frames_hbm.3, s32[16]{0:T(128)} %assign_hbm.5, f32[1,192]{1,0:T(1,128)} %bitcast.12, ...), custom_call_target="tpu_custom_call" | custom-call | flops 11500000 | tf_op jit(solution)/shard_map/prep/pallas_call | solution.py:472
  30.7 0.1 collective-permute-start.15
  30.8 1.1 %collective-permute-done.6.refs_1_ = bf16[96,256]{1,0:T(8,128)(2,1)S(1)} collective-permute-done((bf16[96,256]{1,0:T(8,128)(2,1)S(1)}, bf16[96,256]{1,0:T(8,128)(2,1)S(1)}, u32[]{:S(2)}, u32[]{:S(2)}) %collective-permute-start.6) | collective-permute-done | bytes 49184 | tf_op jit(solution)/shard_map/ppermute | solution.py:655
  31.8 1.0 %collective-permute-done.7.refs_2_ = bf16[96,256]{1,0:T(8,128)(2,1)S(1)} collective-permute-done((bf16[96,256]{1,0:T(8,128)(2,1)S(1)}, bf16[96,256]{1,0:T(8,128)(2,1)S(1)}, u32[]{:S(2)}, u32[]{:S(2)}) %collective-permute-start.7) | collective-permute-done | bytes 49184 | tf_op jit(solution)/shard_map/ppermute | solution.py:655
  32.8 0.0 collective-permute-done.8.refs_3_
  32.9 0.1 collective-permute-start.9
  32.9 0.0 collective-permute-done.15.other
  33.0 1.2 %wide.1.w_all = bf16[576,1152]{1,0:T(8,128)(2,1)S(1)} custom-call(bf16[288,896]{1,0:T(8,128)(2,1)S(1)} %get-tuple-element.43.own, bf16[288,896]{1,0:T(8,128)(2,1)S(1)} %collective-permute-done.15.other, bf16[192,192]{1,0:T(8,128)(2,1)S(1)} %get-tuple-element.44.order), custom_call_target="tpu_custom_call" | custom-call | flops 11500000 | tf_op jit(solution)/shard_map/wide/pallas_call | solution.py:514
  34.1 0.2 collective-permute-done.9.other
  34.4 3.4 %finish.1 = bf16[1,4,8,6144]{3,2,1,0:T(8,128)(2,1)} custom-call(bf16[384,256]{1,0:T(8,128)(2,1)S(1)} %stack.1.own, bf16[384,256]{1,0:T(8,128)(2,1)S(1)} %collective-permute-done.9.other, bf16[576,1152]{1,0:T(8,128)(2,1)S(1)} %wide.1.w_all, bf16[3,256,256]{2,1,0:T(8,128)(2,1)S(1)} %get-tuple-element.45.pick, f32[192,128]{1,0:T(8,128)S(1)} %get-tuple-element.46.gmid_ref, ...), custom_call_target="tpu_custom_call" | custom-call | flops 5520000000 | tf_op jit(solution)/shard_map/finish/pallas_call | solution.py:636
  (7 shorter events, 0.2 us)
Async XLA Ops:
  0.0 8.6 %copy-start = (bf16[12,27,96]{2,1,0:T(8,128)(2,1)S(1)}, bf16[12,27,96]{2,1,0:T(8,128)(2,1)}, u32[]{:S(2)}) copy-start(bf16[12,27,96]{2,1,0:T(8,128)(2,1)} %param.16) | copy-start | bytes 186628
  0.0 12.0 %copy-start.1 = (f32[384]{0:T(512)S(1)}, f32[384]{0:T(512)}, u32[]{:S(2)}) copy-start(f32[384]{0:T(512)} %param.17) | copy-start | bytes 4612
  1.6 10.5 %collective-permute-start = (bf16[80,256]{1,0:T(8,128)(2,1)S(1)}, bf16[80,256]{1,0:T(8,128)(2,1)S(1)}, u32[]{:S(2)}, u32[]{:S(2)}) collective-permute-start(bf16[80,256]{1,0:T(8,128)(2,1)S(1)} %get-tuple-element.28), channel_id=1, source_target_pairs={{0,8},{2,10},{4,12},{6,14},{8,16},{10,18},{12,20},{14,22},{16,24},... | collective-permute-start | bytes 122888 | tf_op jit(solution)/shard_map/ppermute | solution.py:655
  4.6 7.4 %collective-permute-start.1 = (bf16[80,256]{1,0:T(8,128)(2,1)S(1)}, bf16[80,256]{1,0:T(8,128)(2,1)S(1)}, u32[]{:S(2)}, u32[]{:S(2)}) collective-permute-start(bf16[80,256]{1,0:T(8,128)(2,1)S(1)} %get-tuple-element.29), channel_id=1, source_target_pairs={{0,16},{2,18},{4,20},{6,22},{8,24},{10,26},{12,28},{14,30},{16,0},... | collective-permute-start | bytes 122888 | tf_op jit(solution)/shard_map/ppermute | solution.py:655
  7.2 4.8 %collective-permute-start.2 = (bf16[80,256]{1,0:T(8,128)(2,1)S(1)}, bf16[80,256]{1,0:T(8,128)(2,1)S(1)}, u32[]{:S(2)}, u32[]{:S(2)}) collective-permute-start(bf16[80,256]{1,0:T(8,128)(2,1)S(1)} %get-tuple-element.30), channel_id=1, source_target_pairs={{0,24},{2,26},{4,28},{6,30},{8,0},{10,2},{12,4},{14,6},{16,8},{18,... | collective-permute-start | bytes 122888 | tf_op jit(solution)/shard_map/ppermute | solution.py:655
  8.9 7.0 %collective-permute-start.11 = (bf16[24,896]{1,0:T(8,128)(2,1)S(1)}, bf16[24,896]{1,0:T(8,128)(2,1)S(1)}, u32[]{:S(2)}, u32[]{:S(2)}) collective-permute-start(bf16[24,896]{1,0:T(8,128)(2,1)S(1)} %pad_bitcast_fusion.half), channel_id=1, source_target_pairs={{0,6},{2,4},{4,2},{6,0},{8,14},{10,12},{12,10},{14,8},{16,22},{18,... | collective-permute-start | bytes 129032 | tf_op jit(solution)/shard_map/ppermute | solution.py:659
  11.4 5.5 %collective-permute-start.10 = (bf16[48,896]{1,0:T(8,128)(2,1)S(1)}, bf16[48,896]{1,0:T(8,128)(2,1)S(1)}, u32[]{:S(2)}, u32[]{:S(2)}) collective-permute-start(bf16[48,896]{1,0:T(8,128)(2,1)S(1)} %bitcast.11), channel_id=1, source_target_pairs={{0,2},{1,5},{2,0},{3,7},{4,6},{5,1},{6,4},{7,3},{8,10},{9,13},{10,... | collective-permute-start | bytes 258056 | tf_op jit(solution)/shard_map/ppermute | solution.py:664
  12.3 7.2 %collective-permute-start.3 = (bf16[288,256]{1,0:T(8,128)(2,1)S(1)}, bf16[288,256]{1,0:T(8,128)(2,1)S(1)}, u32[]{:S(2)}, u32[]{:S(2)}) collective-permute-start(bf16[288,256]{1,0:T(8,128)(2,1)S(1)} %get-tuple-element.32), channel_id=1, source_target_pairs={{0,2},{2,0},{4,6},{6,4},{8,10},{10,8},{12,14},{14,12},{16,18},{18,... | collective-permute-start | bytes 442376 | tf_op jit(solution)/shard_map/ppermute | solution.py:659
  13.9 8.1 %collective-permute-start.4 = (bf16[288,256]{1,0:T(8,128)(2,1)S(1)}, bf16[288,256]{1,0:T(8,128)(2,1)S(1)}, u32[]{:S(2)}, u32[]{:S(2)}) collective-permute-start(bf16[288,256]{1,0:T(8,128)(2,1)S(1)} %get-tuple-element.33), channel_id=1, source_target_pairs={{0,4},{2,6},{4,0},{6,2},{8,12},{10,14},{12,8},{14,10},{16,20},{18,... | collective-permute-start | bytes 442376 | tf_op jit(solution)/shard_map/ppermute | solution.py:659
  14.6 7.4 %collective-permute-start.5 = (bf16[288,256]{1,0:T(8,128)(2,1)S(1)}, bf16[288,256]{1,0:T(8,128)(2,1)S(1)}, u32[]{:S(2)}, u32[]{:S(2)}) collective-permute-start(bf16[288,256]{1,0:T(8,128)(2,1)S(1)} %get-tuple-element.34), channel_id=1, source_target_pairs={{0,6},{2,4},{4,2},{6,0},{8,14},{10,12},{12,10},{14,8},{16,22},{18,... | collective-permute-start | bytes 442376 | tf_op jit(solution)/shard_map/ppermute | solution.py:659
  17.0 11.4 %collective-permute-start.12 = (bf16[72,896]{1,0:T(8,128)(2,1)S(1)}, bf16[72,896]{1,0:T(8,128)(2,1)S(1)}, u32[]{:S(2)}, u32[]{:S(2)}) collective-permute-start(bf16[72,896]{1,0:T(8,128)(2,1)S(1)} %regroup.1.refs_0_), channel_id=1, source_target_pairs={{0,8},{2,10},{4,12},{6,14},{8,16},{10,18},{12,20},{14,22},{16,24},... | collective-permute-start | bytes 387080 | tf_op jit(solution)/shard_map/ppermute | solution.py:655
  17.7 12.0 %collective-permute-start.13 = (bf16[72,896]{1,0:T(8,128)(2,1)S(1)}, bf16[72,896]{1,0:T(8,128)(2,1)S(1)}, u32[]{:S(2)}, u32[]{:S(2)}) collective-permute-start(bf16[72,896]{1,0:T(8,128)(2,1)S(1)} %regroup.1.refs_0_), channel_id=1, source_target_pairs={{0,16},{2,18},{4,20},{6,22},{8,24},{10,26},{12,28},{14,30},{16,0},... | collective-permute-start | bytes 387080 | tf_op jit(solution)/shard_map/ppermute | solution.py:655
  19.5 10.2 %collective-permute-start.14 = (bf16[72,896]{1,0:T(8,128)(2,1)S(1)}, bf16[72,896]{1,0:T(8,128)(2,1)S(1)}, u32[]{:S(2)}, u32[]{:S(2)}) collective-permute-start(bf16[72,896]{1,0:T(8,128)(2,1)S(1)} %regroup.1.refs_0_), channel_id=1, source_target_pairs={{0,24},{2,26},{4,28},{6,30},{8,0},{10,2},{12,4},{14,6},{16,8},{18,... | collective-permute-start | bytes 387080 | tf_op jit(solution)/shard_map/ppermute | solution.py:655
  25.8 6.0 %collective-permute-start.6 = (bf16[96,256]{1,0:T(8,128)(2,1)S(1)}, bf16[96,256]{1,0:T(8,128)(2,1)S(1)}, u32[]{:S(2)}, u32[]{:S(2)}) collective-permute-start(bf16[96,256]{1,0:T(8,128)(2,1)S(1)} %get-tuple-element.36), channel_id=1, source_target_pairs={{0,8},{2,10},{4,12},{6,14},{8,16},{10,18},{12,20},{14,22},{16,24},... | collective-permute-start | bytes 147464 | tf_op jit(solution)/shard_map/ppermute | solution.py:655
  26.5 6.3 %collective-permute-start.7 = (bf16[96,256]{1,0:T(8,128)(2,1)S(1)}, bf16[96,256]{1,0:T(8,128)(2,1)S(1)}, u32[]{:S(2)}, u32[]{:S(2)}) collective-permute-start(bf16[96,256]{1,0:T(8,128)(2,1)S(1)} %get-tuple-element.37), channel_id=1, source_target_pairs={{0,16},{2,18},{4,20},{6,22},{8,24},{10,26},{12,28},{14,30},{16,0},... | collective-permute-start | bytes 147464 | tf_op jit(solution)/shard_map/ppermute | solution.py:655
  28.4 4.5 %collective-permute-start.8 = (bf16[96,256]{1,0:T(8,128)(2,1)S(1)}, bf16[96,256]{1,0:T(8,128)(2,1)S(1)}, u32[]{:S(2)}, u32[]{:S(2)}) collective-permute-start(bf16[96,256]{1,0:T(8,128)(2,1)S(1)} %get-tuple-element.38), channel_id=1, source_target_pairs={{0,24},{2,26},{4,28},{6,30},{8,0},{10,2},{12,4},{14,6},{16,8},{18,... | collective-permute-start | bytes 147464 | tf_op jit(solution)/shard_map/ppermute | solution.py:655
  30.7 2.2 %collective-permute-start.15 = (bf16[288,896]{1,0:T(8,128)(2,1)S(1)}, bf16[288,896]{1,0:T(8,128)(2,1)S(1)}, u32[]{:S(2)}, u32[]{:S(2)}) collective-permute-start(bf16[288,896]{1,0:T(8,128)(2,1)S(1)} %get-tuple-element.43.own), channel_id=1, source_target_pairs={{0,1},{1,0},{2,3},{3,2},{4,5},{5,4},{6,7},{7,6},{8,9},{9,8},{10,11... | collective-permute-start | bytes 1548296 | tf_op jit(solution)/shard_map/ppermute | solution.py:668
  32.9 1.5 %collective-permute-start.9 = (bf16[384,256]{1,0:T(8,128)(2,1)S(1)}, bf16[384,256]{1,0:T(8,128)(2,1)S(1)}, u32[]{:S(2)}, u32[]{:S(2)}) collective-permute-start(bf16[384,256]{1,0:T(8,128)(2,1)S(1)} %stack.1.own), channel_id=1, source_target_pairs={{0,1},{1,0},{2,3},{3,2},{4,5},{5,4},{6,7},{7,6},{8,9},{9,8},{10,11... | collective-permute-start | bytes 589832 | tf_op jit(solution)/shard_map/ppermute | solution.py:668

commit v7 on v6

--- a/solution.py
+++ b/solution.py
@@ -170,16 +170,18 @@
     return table
 
 
-def pack_kernel(offsets_hbm, assign_hbm, w_hbm, lat_hbm, *refs):
-    outs, (wf, lf, pf, tab, lat_rows, w_ref, lat_ref, offsets, assign, sems) = refs[:LINE], refs[LINE:]
+def pack_kernel(offsets_hbm, assign_hbm, w_hbm, lat_hbm, win_hbm, frames_hbm, *refs):
+    outs, w1, fills, (frames, wf, lf, pf, tab, lat_rows, w_ref, lat_ref, offsets, assign, sems) = refs[:LINE], refs[LINE], refs[LINE + 1], refs[LINE + 2 :]
     parts = [pl.ds(9 * a, 9) for a in range(3)]
     moves = [(w_hbm.at[p], w_ref.at[p]) for p in parts]
     moves = [(offsets_hbm, offsets), (assign_hbm, assign), (lat_hbm, lat_ref)] + moves
+    moves += [(win_hbm, w1.at[0 : 27 * ZC]), (frames_hbm, frames)]
     copies = [pltpu.make_async_copy(src, dst, sems.at[i]) for i, (src, dst) in enumerate(moves)]
     for copy in copies:
         copy.start()
-    z, _, c = place()
+    z, q, c = place()
     lf[32:40, :] = jnp.zeros((8, 128), F32)
+    w1[27 * ZC :, :] = jnp.zeros((512 - 27 * ZC, C1), BF16)
     for k in range(LINE):
         pf[k, W_ROWS:, :] = jnp.zeros((PIECE_ROWS - W_ROWS, 256), F32)
     lane1 = iota((1, 128), 1)
@@ -229,16 +231,22 @@
         pl.when(c == core)(functools.partial(choose, core))
     for k in range(LINE):
         outs[k][...] = (pf[lax.rem(z + k, LINE)] + lat_rows[...]).astype(BF16)
-
-
-def pack(offsets, assign, w_mid, latents):
+    copies[6].wait()
+    copies[7].wait()
+    for i in range(LINE):
+        fill = frames[assign[lax.rem(z + i, LINE) * PLANE + q]] * (TOK // FMAX)
+        fills[i : i + 1, :] = jnp.full((1, 128), fill, jnp.int32).astype(F32)
+
+
+def pack(offsets, assign, w_mid, latents, w_in, frames):
     piece = jax.ShapeDtypeStruct((PIECE_ROWS, 256), BF16)
     return pl.pallas_call(
         pack_kernel,
-        out_shape=[piece] * LINE,
-        in_specs=[HBM()] * 4,
-        out_specs=[VMEM()] * LINE,
+        out_shape=[piece] * LINE + [jax.ShapeDtypeStruct((512, C1), BF16), jax.ShapeDtypeStruct((LINE, 128), F32)],
+        in_specs=[HBM()] * 6,
+        out_specs=[VMEM()] * (LINE + 2),
         scratch_shapes=[
+            pltpu.SMEM(frames.shape, jnp.int32),
             pltpu.VMEM((27, IN_SH, 256), F32),
             pltpu.VMEM((40, 128), F32),
             pltpu.VMEM((LINE, PIECE_ROWS, 256), F32),
@@ -248,12 +256,12 @@
             pltpu.VMEM(latents.shape, BF16),
             pltpu.SMEM(offsets.shape, jnp.int32),
             pltpu.SMEM(assign.shape, jnp.int32),
-            pltpu.SemaphoreType.DMA((6,)),
+            pltpu.SemaphoreType.DMA((8,)),
         ],
         cost_estimate=cost(2),
         compiler_params=pltpu.CompilerParams(vmem_limit_bytes=32 << 20),
         name="pack",
-    )(*in_hbm(offsets, assign, w_mid, latents))
+    )(*in_hbm(offsets, assign, w_mid, latents, w_in, frames))
 
 
 def join_kernel(*refs):
@@ -298,15 +306,10 @@
     )(*pieces)
 
 
-def mid_kernel(frames_hbm, assign_hbm, win_hbm, gain_ref, *refs):
+def mid_kernel(fills, w1, gain_ref, *refs):
     parts, outs = refs[:PLANE], refs[PLANE : PLANE + LINE]
-    lt, xs, tokens, shifted, w1, act, wf, frames, assign, sems = refs[PLANE + LINE :]
+    lt, xs, tokens, shifted, act, wf = refs[PLANE + LINE :]
     z, q, _ = place()
-    moves = [(frames_hbm, frames), (assign_hbm, assign), (win_hbm, w1.at[0 : 27 * ZC])]
-    loads = [pltpu.make_async_copy(src, dst, sems.at[i]) for i, (src, dst) in enumerate(moves)]
-    for load in loads:
-        load.start()
-    w1[27 * ZC :, :] = jnp.zeros((512 - 27 * ZC, C1), BF16)
     for d in range(PLANE):
         part = parts[d][...].astype(F32)
         lt[...] = found_lanes(part, 7)
@@ -317,8 +320,9 @@
                 wf[b, pl.ds(pl.multiple_of(shard * IN_SH, 8), IN_SH), :] = part[at : at + IN_SH]
             for i in range(LINE):
                 xs[i, pl.ds(shard, 1), :] = lt[pl.ds(LINE * k + lax.rem(z + i, LINE), 1), :]
-    own_lane = iota((16, 16, 256), 1) == iota((16, 16, 256), 2) // ZC
     repeat = (iota((256, 128), 0) % ZC == iota((256, 128), 1) % ZC).astype(F32).astype(BF16)
+    pos16, shard16 = iota((256, 16), 0).astype(F32), iota((256, 16), 1).astype(F32)
+    pos, token = iota((256, 256), 0).astype(F32), (iota((256, 256), 1) // ZC).astype(F32)
     lane, col = iota((256, 128), 1), iota((256, 128), 0) % WL
     inner_l, inner_r = col > 0, col < WL - 1
     block = lane // ZC
@@ -326,16 +330,14 @@
     lane1 = iota((1, 128), 1)
     zero_rows = jnp.zeros((2, 6, WL, 128), BF16)
     zero_cols = jnp.zeros((4, 1, WL, 128), BF16)
-    for load in loads[:2]:
-        load.wait()
     for i in range(LINE):
-        fill = frames[assign[lax.rem(z + i, LINE) * PLANE + q]] * (TOK // FMAX)
-        spread = jnp.where(own_lane, jnp.broadcast_to(xs[i][:, None, :], (16, 16, 256)), 0.0)
-        rows = jnp.dot(spread.reshape(256, 256).astype(BF16), repeat, preferred_element_type=F32)
-        tokens[i] = jnp.zeros((288, 128), F32)
-        for shard in range(16):
-            tokens[i, pl.ds(8 + shard * fill, TOK), :] = rows[TOK * shard : TOK * (shard + 1)]
-        tokens[i, pl.ds(8 + 16 * fill, TOK), :] = jnp.zeros((TOK, 128), F32)
+        fill = fills[i : i + 1, 0:16]
+        start = fill * shard16
+        hit = (pos16 >= start) & (pos16 < start + fill)
+        first = jnp.sum(jnp.where(hit, start, 0.0), axis=1, keepdims=True)
+        rows = jnp.dot(hit.astype(F32).astype(BF16), xs[i].astype(BF16), preferred_element_type=F32)
+        own = jnp.where(pos - first == token, rows, 0.0).astype(BF16)
+        tokens[i, 8:264, :] = jnp.dot(own, repeat, preferred_element_type=F32)
         here = tokens[i, 8:264, :]
         left = jnp.where(inner_l, tokens[i, 7:263, :], 0.0)
         right = jnp.where(inner_r, tokens[i, 9:265, :], 0.0)
@@ -345,8 +347,6 @@
             shifted[i, r, 2:6, 0:1] = zero_cols
             shifted[i, r, 2:6, 5:6] = zero_cols
             shifted[i, r, 2:6, 1:5] = v.reshape(4, 4, WL, 128)
-    for load in loads[2:]:
-        load.wait()
     for i in range(LINE):
         tiles = []
         for j in range(4):
@@ -360,57 +360,59 @@
             tiles.append(tile)
         h = jnp.dot(jnp.concatenate(tiles, axis=1), w1[...], preferred_element_type=F32)
         scale = lax.rsqrt(jnp.mean(h * h, axis=1, keepdims=True) + 1e-6)
-        act[256 * i : 256 * i + 256, :] = silu(h * scale * gain_ref[...]).astype(BF16)
-    lanes = LINE * 256
-    at = iota((OUT_BLK, lanes), 1)
-    frame, row, column = (at // 64) % FMAX, (at // WL) % 4, at % WL
-    summed = []
+        out = silu(h * scale * gain_ref[...]).astype(BF16)
+        for tp in range(2):
+            act[512 * tp + 128 * i : 512 * tp + 128 * i + 128, :] = out[128 * tp : 128 * tp + 128]
+    lane = iota((OUT_BLK, 128), 1)
+    second, row, column = lane >= 64, lane // WL % 4, lane % WL
+    sums = [[[] for _ in range(2)] for _ in range(LINE)]
     for b in range(3):
-        prod = dot_nt(wf[b].T.astype(BF16), act[...])
-        for e in range(3):
-            now, before, two = (prod[OUT_BLK * (3 * a + e) : OUT_BLK * (3 * a + e + 1)] for a in (2, 1, 0))
-            summed.append(
-                now
-                + jnp.where(frame >= 1, pltpu.roll(before, 64, 1), 0.0)
-                + jnp.where(frame >= 2, pltpu.roll(two, 128, 1), 0.0)
-            )
-    halves = [[], []]
-    for b in range(3):
-        e0, e1, e2 = summed[3 * b : 3 * b + 3]
-        halves[0].append(jnp.where(column > 0, pltpu.roll(e0, 1, 1), 0.0) + e1 + e2)
-        halves[1].append(e0 + e1 + jnp.where(column < WL - 1, pltpu.roll(e2, lanes - 1, 1), 0.0))
-    phases = [None] * 4
-    for px in range(2):
-        b0, b1, b2 = halves[px]
-        phases[px] = jnp.where(row > 0, pltpu.roll(b0, WL, 1), 0.0) + b1 + b2
-        phases[2 + px] = b0 + b1 + jnp.where(row < 3, pltpu.roll(b2, lanes - WL, 1), 0.0)
+        turned = wf[b].T.astype(BF16)
+        prods = [dot_nt(turned[0:224], act[0:512, :]), dot_nt(turned[64:224], act[512:1024, :])]
+
+        def tile(i, tp, a, e):
+            at = OUT_BLK * (3 * a + e) - 64 * tp
+            return prods[tp][at : at + OUT_BLK, 128 * i : 128 * i + 128]
+
+        for i in range(LINE):
+            for e in range(3):
+                early, late = (pltpu.roll(tile(i, tp, 1, e), 64, 1) for tp in range(2))
+                sums[i][0].append(tile(i, 0, 2, e) + jnp.where(second, early, 0.0))
+                sums[i][1].append(tile(i, 1, 2, e) + jnp.where(second, late, early) + tile(i, 0, 0, e))
     for i in range(LINE):
-        outs[i][...] = jnp.concatenate([p[:, 256 * i : 256 * i + 256] for p in phases], axis=0).astype(BF16)
-
-
-def mid(frames, assign, parts, w_in, gain_in):
+        for tp in range(2):
+            halves = [[], []]
+            for b in range(3):
+                e0, e1, e2 = sums[i][tp][3 * b : 3 * b + 3]
+                halves[0].append(jnp.where(column > 0, pltpu.roll(e0, 1, 1), 0.0) + e1 + e2)
+                halves[1].append(e0 + e1 + jnp.where(column < WL - 1, pltpu.roll(e2, 127, 1), 0.0))
+            phases = [None] * 4
+            for px in range(2):
+                b0, b1, b2 = halves[px]
+                phases[px] = jnp.where(row > 0, pltpu.roll(b0, WL, 1), 0.0) + b1 + b2
+                phases[2 + px] = b0 + b1 + jnp.where(row < 3, pltpu.roll(b2, 128 - WL, 1), 0.0)
+            outs[i][:, 128 * tp : 128 * tp + 128] = jnp.concatenate(phases, axis=0).astype(BF16)
+
+
+def mid(fills, parts, w_in, gain_in):
     out = jax.ShapeDtypeStruct((4 * OUT_BLK, 256), BF16)
     return pl.pallas_call(
         mid_kernel,
         out_shape=[out] * LINE,
-        in_specs=[HBM()] * 3 + [VMEM()] * (PLANE + 1),
+        in_specs=[VMEM()] * (PLANE + 3),
         out_specs=[VMEM()] * LINE,
         scratch_shapes=[
             pltpu.VMEM((LINE * LINE, 256), F32),
             pltpu.VMEM((LINE, 16, 256), F32),
             pltpu.VMEM((LINE, 288, 128), F32),
             pltpu.VMEM((LINE, 3, 6, 6, WL, 128), BF16),
-            pltpu.VMEM((512, C1), BF16),
             pltpu.VMEM((LINE * 256, C1), BF16),
             pltpu.VMEM((3, C1, 256), F32),
-            pltpu.SMEM(frames.shape, jnp.int32),
-            pltpu.SMEM(assign.shape, jnp.int32),
-            pltpu.SemaphoreType.DMA((3,)),
         ],
         compiler_params=pltpu.CompilerParams(vmem_limit_bytes=48 << 20),
         cost_estimate=cost(5),
         name="mid",
-    )(*in_hbm(frames, assign, w_in), gain_in, *parts)
+    )(fills, w_in, gain_in, *parts)
 
 
 def regroup_kernel(half, near, far, out, rows):
@@ -670,7 +672,8 @@
 
 def per_device_fast(latents, frames, offsets, assign, w_in, w_mid, w_out, gain_in, gain_mid, gain_out):
     core = lax.axis_index("row")
-    pieces = pack(offsets, assign, jnp.transpose(w_mid, (1, 0, 2)), latents)
+    w_in = w_in.transpose(1, 0, 2).reshape(27 * ZC, C1)
+    *pieces, w_in, fills = pack(offsets, assign, jnp.transpose(w_mid, (1, 0, 2)), latents, w_in, frames)
     pieces = [pieces[0]] + [along_z(pieces[k], k) for k in range(1, LINE)]
     parts = join(pieces)
     parts = [parts[0]] + [in_plane(parts[d], d) for d in range(1, PLANE)]
@@ -680,7 +683,7 @@
     half = jnp.pad(half, ((0, 0), (0, 2), (0, WOUT_LANES - 9 * C3))).reshape(24, WOUT_LANES)
     plane = regroup(half, near_chip(full), in_plane(half, 3))
     own = [plane] + [along_z(plane, k) for k in range(1, LINE)]
-    hidden = mid(frames, assign, parts, w_in.transpose(1, 0, 2).reshape(27 * ZC, C1), gain_in[None, :])
+    hidden = mid(fills, parts, w_in, gain_in[None, :])
     own, _ = lax.optimization_barrier((own, hidden[0]))
     raw, order, pick, gmid, gout, limit = prep(frames, assign, gain_mid[None, :], gain_out[None, :], own)
     w_last = wide(raw, other_core(raw), order)

time: 37.9 us -> 37.8 us (level)
  Pallas kernels: 11.2 us -> 10.8 us
    pallas_call x2, Pallas kernels: 5.38 us -> 4.99 us  [the longest x1 3.39 us: mid(): pl.pallas_call(mid_kernel, out_shape=[out] * LINE, in_specs=[VMEM()] * (P...]
  transfers between devices with their start and end apart: 16 -> 16, of which waited for: 6 -> 6; matrix products, arithmetic and copies ran while one was open for 1% -> 1% of each run, Pallas kernels for 17% -> 16%
where the time goes in v7:
time: 37.8 us; the launch traced here: 37.7 us
  starting transfers between devices  21.3 us (56%)
  Pallas kernels  10.8 us (29%)
  waiting for transfers between devices  5.16 us (14%)
    ppermute x9, starting transfers between devices, along_z(): lax.ppermute(value, 'grp', [(g, (g + PLANE * step) % (LINE * PLANE)) for...  14.5 us
    ppermute x4, starting transfers between devices, in_plane(): lax.ppermute(value, 'grp', [(g, g ^ flip) for g in range(LINE * PLANE)])  6.07 us
    pallas_call x1, Pallas kernels, mid(): pl.pallas_call(mid_kernel, out_shape=[out] * LINE, in_specs=[VMEM()] * (P...  3.39 us
    pallas_call x1, Pallas kernels, finish(): pl.pallas_call(out_kernel, out_shape=jax.ShapeDtypeStruct((1, FMAX, 4 * R...  3.35 us
    ppermute x9, waiting for transfers between devices, along_z(): lax.ppermute(value, 'grp', [(g, (g + PLANE * step) % (LINE * PLANE)) for...  2.41 us
    pallas_call x1, Pallas kernels, pack(): pl.pallas_call(pack_kernel, out_shape=[piece] * LINE + [jax.ShapeDtypeStr...  1.6 us
    ppermute x4, waiting for transfers between devices, in_plane(): lax.ppermute(value, 'grp', [(g, g ^ flip) for g in range(LINE * PLANE)])  1.45 us
    pallas_call x1, Pallas kernels, wide(): pl.pallas_call(wide_kernel, out_shape=jax.ShapeDtypeStruct((3 * C2, 1152)...  1.16 us
  transfers between devices with their start and end apart: 16, of which 6 were waited for; matrix products, arithmetic and copies ran while one was open for 1% of the time, Pallas kernels for 16%

profile of v7, /device:TPU:0, one launch (start us, length us, event | category | flops | bytes accessed | tf_op | source)
XLA Modules:
  0.0 37.7 jit_solution(15265639022997353728)
XLA Ops:
  0.0 0.0 copy-start
  0.0 0.0 copy-start.1
  0.0 1.6 %pack.1 = (bf16[80,256]{1,0:T(8,128)(2,1)S(1)}, bf16[80,256]{1,0:T(8,128)(2,1)S(1)}, bf16[80,256]{1,0:T(8,128)(2,1)S(1)}, bf16[80,256]{1,0:T(8,128)(2,1)S(1)}, b...) custom-call(s32[16]{0:T(128)} %offsets_hbm.1, s32[16]{0:T(128)} %assign_hbm.3, bf16[27,24,192]{2,1,0:T(8,128)(2,1)} %bitcast.14, ...), custom_call_target="tpu_custom_call" | custom-call | flops 2300000000 | tf_op jit(solution)/shard_map/pack/pallas_call | solution.py:243
  1.6 3.1 %collective-permute-start = (bf16[80,256]{1,0:T(8,128)(2,1)S(1)}, bf16[80,256]{1,0:T(8,128)(2,1)S(1)}, u32[]{:S(2)}, u32[]{:S(2)}) collective-permute-start(bf16[80,256]{1,0:T(8,128)(2,1)S(1)} %get-tuple-element.32), channel_id=1, source_target_pairs={{0,8},{2,10},{4,12},{6,14},{8,16},{10,18},{12,20},{14,22},{16,24},... | collective-permute-start | bytes 122888 | tf_op jit(solution)/shard_map/ppermute | solution.py:657
  4.7 2.6 %collective-permute-start.1 = (bf16[80,256]{1,0:T(8,128)(2,1)S(1)}, bf16[80,256]{1,0:T(8,128)(2,1)S(1)}, u32[]{:S(2)}, u32[]{:S(2)}) collective-permute-start(bf16[80,256]{1,0:T(8,128)(2,1)S(1)} %get-tuple-element.33), channel_id=1, source_target_pairs={{0,16},{2,18},{4,20},{6,22},{8,24},{10,26},{12,28},{14,30},{16,0},... | collective-permute-start | bytes 122888 | tf_op jit(solution)/shard_map/ppermute | solution.py:657
  7.3 1.3 %collective-permute-start.2 = (bf16[80,256]{1,0:T(8,128)(2,1)S(1)}, bf16[80,256]{1,0:T(8,128)(2,1)S(1)}, u32[]{:S(2)}, u32[]{:S(2)}) collective-permute-start(bf16[80,256]{1,0:T(8,128)(2,1)S(1)} %get-tuple-element.34), channel_id=1, source_target_pairs={{0,24},{2,26},{4,28},{6,30},{8,0},{10,2},{12,4},{14,6},{16,8},{18,... | collective-permute-start | bytes 122888 | tf_op jit(solution)/shard_map/ppermute | solution.py:657
  8.6 0.0 copy-done
  8.6 0.1 reshape.16
  8.7 0.1 reshape.17
  8.9 2.5 %collective-permute-start.11 = (bf16[24,896]{1,0:T(8,128)(2,1)S(1)}, bf16[24,896]{1,0:T(8,128)(2,1)S(1)}, u32[]{:S(2)}, u32[]{:S(2)}) collective-permute-start(bf16[24,896]{1,0:T(8,128)(2,1)S(1)} %pad_bitcast_fusion.half), channel_id=1, source_target_pairs={{0,6},{2,4},{4,2},{6,0},{8,14},{10,12},{12,10},{14,8},{16,22},{18,... | collective-permute-start | bytes 129032 | tf_op jit(solution)/shard_map/ppermute | solution.py:661
  11.5 0.6 %collective-permute-start.10 = (bf16[48,896]{1,0:T(8,128)(2,1)S(1)}, bf16[48,896]{1,0:T(8,128)(2,1)S(1)}, u32[]{:S(2)}, u32[]{:S(2)}) collective-permute-start(bf16[48,896]{1,0:T(8,128)(2,1)S(1)} %bitcast.11), channel_id=1, source_target_pairs={{0,2},{1,5},{2,0},{3,7},{4,6},{5,1},{6,4},{7,3},{8,10},{9,13},{10,... | collective-permute-start | bytes 258056 | tf_op jit(solution)/shard_map/ppermute | solution.py:666
  12.1 0.0 copy-done.1
  12.1 0.0 collective-permute-done.refs_1_
  12.1 0.0 collective-permute-done.1.refs_2_
  12.1 0.0 collective-permute-done.2.refs_3_
  12.1 0.3 join.1
  12.4 1.6 %collective-permute-start.3 = (bf16[288,256]{1,0:T(8,128)(2,1)S(1)}, bf16[288,256]{1,0:T(8,128)(2,1)S(1)}, u32[]{:S(2)}, u32[]{:S(2)}) collective-permute-start(bf16[288,256]{1,0:T(8,128)(2,1)S(1)} %get-tuple-element.36), channel_id=1, source_target_pairs={{0,2},{2,0},{4,6},{6,4},{8,10},{10,8},{12,14},{14,12},{16,18},{18,... | collective-permute-start | bytes 442376 | tf_op jit(solution)/shard_map/ppermute | solution.py:661
  13.9 0.7 %collective-permute-start.4 = (bf16[288,256]{1,0:T(8,128)(2,1)S(1)}, bf16[288,256]{1,0:T(8,128)(2,1)S(1)}, u32[]{:S(2)}, u32[]{:S(2)}) collective-permute-start(bf16[288,256]{1,0:T(8,128)(2,1)S(1)} %get-tuple-element.37), channel_id=1, source_target_pairs={{0,4},{2,6},{4,0},{6,2},{8,12},{10,14},{12,8},{14,10},{16,20},{18,... | collective-permute-start | bytes 442376 | tf_op jit(solution)/shard_map/ppermute | solution.py:661
  14.6 1.3 %collective-permute-start.5 = (bf16[288,256]{1,0:T(8,128)(2,1)S(1)}, bf16[288,256]{1,0:T(8,128)(2,1)S(1)}, u32[]{:S(2)}, u32[]{:S(2)}) collective-permute-start(bf16[288,256]{1,0:T(8,128)(2,1)S(1)} %get-tuple-element.38), channel_id=1, source_target_pairs={{0,6},{2,4},{4,2},{6,0},{8,14},{10,12},{12,10},{14,8},{16,22},{18,... | collective-permute-start | bytes 442376 | tf_op jit(solution)/shard_map/ppermute | solution.py:661
  15.9 0.0 collective-permute-done.11.far
  15.9 1.1 %collective-permute-done.10.near = bf16[48,896]{1,0:T(8,128)(2,1)S(1)} collective-permute-done((bf16[48,896]{1,0:T(8,128)(2,1)S(1)}, bf16[48,896]{1,0:T(8,128)(2,1)S(1)}, u32[]{:S(2)}, u32[]{:S(2)}) %collective-permute-start.10) | collective-permute-done | bytes 86048 | tf_op jit(solution)/shard_map/ppermute | solution.py:666
  17.0 0.7 %collective-permute-start.12 = (bf16[72,896]{1,0:T(8,128)(2,1)S(1)}, bf16[72,896]{1,0:T(8,128)(2,1)S(1)}, u32[]{:S(2)}, u32[]{:S(2)}) collective-permute-start(bf16[72,896]{1,0:T(8,128)(2,1)S(1)} %regroup.1.refs_0_), channel_id=1, source_target_pairs={{0,8},{2,10},{4,12},{6,14},{8,16},{10,18},{12,20},{14,22},{16,24},... | collective-permute-start | bytes 387080 | tf_op jit(solution)/shard_map/ppermute | solution.py:657
  17.8 1.2 %collective-permute-start.13 = (bf16[72,896]{1,0:T(8,128)(2,1)S(1)}, bf16[72,896]{1,0:T(8,128)(2,1)S(1)}, u32[]{:S(2)}, u32[]{:S(2)}) collective-permute-start(bf16[72,896]{1,0:T(8,128)(2,1)S(1)} %regroup.1.refs_0_), channel_id=1, source_target_pairs={{0,16},{2,18},{4,20},{6,22},{8,24},{10,26},{12,28},{14,30},{16,0},... | collective-permute-start | bytes 387080 | tf_op jit(solution)/shard_map/ppermute | solution.py:657
  18.9 0.6 %collective-permute-done.3.refs_1_ = bf16[288,256]{1,0:T(8,128)(2,1)S(1)} collective-permute-done((bf16[288,256]{1,0:T(8,128)(2,1)S(1)}, bf16[288,256]{1,0:T(8,128)(2,1)S(1)}, u32[]{:S(2)}, u32[]{:S(2)}) %collective-permute-start.3) | collective-permute-done | bytes 147488 | tf_op jit(solution)/shard_map/ppermute | solution.py:661
  19.6 1.6 %collective-permute-start.14 = (bf16[72,896]{1,0:T(8,128)(2,1)S(1)}, bf16[72,896]{1,0:T(8,128)(2,1)S(1)}, u32[]{:S(2)}, u32[]{:S(2)}) collective-permute-start(bf16[72,896]{1,0:T(8,128)(2,1)S(1)} %regroup.1.refs_0_), channel_id=1, source_target_pairs={{0,24},{2,26},{4,28},{6,30},{8,0},{10,2},{12,4},{14,6},{16,8},{18,... | collective-permute-start | bytes 387080 | tf_op jit(solution)/shard_map/ppermute | solution.py:657
  21.2 0.8 %collective-permute-done.4.refs_2_ = bf16[288,256]{1,0:T(8,128)(2,1)S(1)} collective-permute-done((bf16[288,256]{1,0:T(8,128)(2,1)S(1)}, bf16[288,256]{1,0:T(8,128)(2,1)S(1)}, u32[]{:S(2)}, u32[]{:S(2)}) %collective-permute-start.4) | collective-permute-done | bytes 147488 | tf_op jit(solution)/shard_map/ppermute | solution.py:661
  22.0 0.0 collective-permute-done.5.refs_3_
  22.0 3.4 %mid.1 = (bf16[96,256]{1,0:T(8,128)(2,1)S(1)}, bf16[96,256]{1,0:T(8,128)(2,1)S(1)}, bf16[96,256]{1,0:T(8,128)(2,1)S(1)}, bf16[96,256]{1,0:T(8,128)(2,1)S(1)}) custom-call(f32[4,128]{1,0:T(4,128)S(1)} %get-tuple-element.29.fills, bf16[512,384]{1,0:T(8,128)(2,1)S(1)} %get-tuple-element.30.w1, f32[1,384]{1,0:T(1,128)S(1)} %broadcast_in_dim.9.gain_ref, ...), custom_call_target="tpu_custom_call" | custom-call | flops 5750000128 | tf_op jit(solution)/shard_map/mid/pallas_call | solution.py:399
  25.4 0.7 %collective-permute-start.6 = (bf16[96,256]{1,0:T(8,128)(2,1)S(1)}, bf16[96,256]{1,0:T(8,128)(2,1)S(1)}, u32[]{:S(2)}, u32[]{:S(2)}) collective-permute-start(bf16[96,256]{1,0:T(8,128)(2,1)S(1)} %get-tuple-element.40), channel_id=1, source_target_pairs={{0,8},{2,10},{4,12},{6,14},{8,16},{10,18},{12,20},{14,22},{16,24},... | collective-permute-start | bytes 147464 | tf_op jit(solution)/shard_map/ppermute | solution.py:657
  26.1 1.9 %collective-permute-start.7 = (bf16[96,256]{1,0:T(8,128)(2,1)S(1)}, bf16[96,256]{1,0:T(8,128)(2,1)S(1)}, u32[]{:S(2)}, u32[]{:S(2)}) collective-permute-start(bf16[96,256]{1,0:T(8,128)(2,1)S(1)} %get-tuple-element.41), channel_id=1, source_target_pairs={{0,16},{2,18},{4,20},{6,22},{8,24},{10,26},{12,28},{14,30},{16,0},... | collective-permute-start | bytes 147464 | tf_op jit(solution)/shard_map/ppermute | solution.py:657
  28.0 0.0 collective-permute-done.12.refs_1_
  28.0 1.4 %collective-permute-start.8 = (bf16[96,256]{1,0:T(8,128)(2,1)S(1)}, bf16[96,256]{1,0:T(8,128)(2,1)S(1)}, u32[]{:S(2)}, u32[]{:S(2)}) collective-permute-start(bf16[96,256]{1,0:T(8,128)(2,1)S(1)} %get-tuple-element.42), channel_id=1, source_target_pairs={{0,24},{2,26},{4,28},{6,30},{8,0},{10,2},{12,4},{14,6},{16,8},{18,... | collective-permute-start | bytes 147464 | tf_op jit(solution)/shard_map/ppermute | solution.py:657
  29.3 0.0 collective-permute-done.13.refs_2_
  29.3 0.0 collective-permute-done.14.refs_3_
  29.3 1.0 %prep.1 = (bf16[288,896]{1,0:T(8,128)(2,1)S(1)}, bf16[192,192]{1,0:T(8,128)(2,1)S(1)}, bf16[3,256,256]{2,1,0:T(8,128)(2,1)S(1)}, f32[192,128]{1,0:T(8,128)S(1)},...) custom-call(s32[16]{0:T(128)} %frames_hbm.3, s32[16]{0:T(128)} %assign_hbm.3, f32[1,192]{1,0:T(1,128)} %bitcast.12, ...), custom_call_target="tpu_custom_call" | custom-call | flops 11500000 | tf_op jit(solution)/shard_map/prep/pallas_call | solution.py:474
  30.3 0.1 collective-permute-start.15
  30.4 1.0 %collective-permute-done.6.refs_1_ = bf16[96,256]{1,0:T(8,128)(2,1)S(1)} collective-permute-done((bf16[96,256]{1,0:T(8,128)(2,1)S(1)}, bf16[96,256]{1,0:T(8,128)(2,1)S(1)}, u32[]{:S(2)}, u32[]{:S(2)}) %collective-permute-start.6) | collective-permute-done | bytes 49184 | tf_op jit(solution)/shard_map/ppermute | solution.py:657
  31.4 1.3 %collective-permute-done.7.refs_2_ = bf16[96,256]{1,0:T(8,128)(2,1)S(1)} collective-permute-done((bf16[96,256]{1,0:T(8,128)(2,1)S(1)}, bf16[96,256]{1,0:T(8,128)(2,1)S(1)}, u32[]{:S(2)}, u32[]{:S(2)}) %collective-permute-start.7) | collective-permute-done | bytes 49184 | tf_op jit(solution)/shard_map/ppermute | solution.py:657
  32.8 0.0 collective-permute-done.8.refs_3_
  32.8 0.1 collective-permute-start.9
  32.9 0.0 collective-permute-done.15.other
  32.9 1.2 %wide.1.w_all = bf16[576,1152]{1,0:T(8,128)(2,1)S(1)} custom-call(bf16[288,896]{1,0:T(8,128)(2,1)S(1)} %get-tuple-element.47.own, bf16[288,896]{1,0:T(8,128)(2,1)S(1)} %collective-permute-done.15.other, bf16[192,192]{1,0:T(8,128)(2,1)S(1)} %get-tuple-element.48.order), custom_call_target="tpu_custom_call" | custom-call | flops 11500000 | tf_op jit(solution)/shard_map/wide/pallas_call | solution.py:516
  34.1 0.2 collective-permute-done.9.other
  34.3 3.4 %finish.1 = bf16[1,4,8,6144]{3,2,1,0:T(8,128)(2,1)} custom-call(bf16[384,256]{1,0:T(8,128)(2,1)S(1)} %stack.1.own, bf16[384,256]{1,0:T(8,128)(2,1)S(1)} %collective-permute-done.9.other, bf16[576,1152]{1,0:T(8,128)(2,1)S(1)} %wide.1.w_all, bf16[3,256,256]{2,1,0:T(8,128)(2,1)S(1)} %get-tuple-element.49.pick, f32[192,128]{1,0:T(8,128)S(1)} %get-tuple-element.50.gmid_ref, ...), custom_call_target="tpu_custom_call" | custom-call | flops 5520000000 | tf_op jit(solution)/shard_map/finish/pallas_call | solution.py:638
  (7 shorter events, 0.2 us)
Async XLA Ops:
  0.0 8.6 %copy-start = (bf16[12,27,96]{2,1,0:T(8,128)(2,1)S(1)}, bf16[12,27,96]{2,1,0:T(8,128)(2,1)}, u32[]{:S(2)}) copy-start(bf16[12,27,96]{2,1,0:T(8,128)(2,1)} %param.16) | copy-start | bytes 186628
  0.0 12.1 %copy-start.1 = (f32[384]{0:T(512)S(1)}, f32[384]{0:T(512)}, u32[]{:S(2)}) copy-start(f32[384]{0:T(512)} %param.17) | copy-start | bytes 4612
  1.6 10.5 %collective-permute-start = (bf16[80,256]{1,0:T(8,128)(2,1)S(1)}, bf16[80,256]{1,0:T(8,128)(2,1)S(1)}, u32[]{:S(2)}, u32[]{:S(2)}) collective-permute-start(bf16[80,256]{1,0:T(8,128)(2,1)S(1)} %get-tuple-element.32), channel_id=1, source_target_pairs={{0,8},{2,10},{4,12},{6,14},{8,16},{10,18},{12,20},{14,22},{16,24},... | collective-permute-start | bytes 122888 | tf_op jit(solution)/shard_map/ppermute | solution.py:657
  4.7 7.4 %collective-permute-start.1 = (bf16[80,256]{1,0:T(8,128)(2,1)S(1)}, bf16[80,256]{1,0:T(8,128)(2,1)S(1)}, u32[]{:S(2)}, u32[]{:S(2)}) collective-permute-start(bf16[80,256]{1,0:T(8,128)(2,1)S(1)} %get-tuple-element.33), channel_id=1, source_target_pairs={{0,16},{2,18},{4,20},{6,22},{8,24},{10,26},{12,28},{14,30},{16,0},... | collective-permute-start | bytes 122888 | tf_op jit(solution)/shard_map/ppermute | solution.py:657
  7.3 4.8 %collective-permute-start.2 = (bf16[80,256]{1,0:T(8,128)(2,1)S(1)}, bf16[80,256]{1,0:T(8,128)(2,1)S(1)}, u32[]{:S(2)}, u32[]{:S(2)}) collective-permute-start(bf16[80,256]{1,0:T(8,128)(2,1)S(1)} %get-tuple-element.34), channel_id=1, source_target_pairs={{0,24},{2,26},{4,28},{6,30},{8,0},{10,2},{12,4},{14,6},{16,8},{18,... | collective-permute-start | bytes 122888 | tf_op jit(solution)/shard_map/ppermute | solution.py:657
  8.9 7.0 %collective-permute-start.11 = (bf16[24,896]{1,0:T(8,128)(2,1)S(1)}, bf16[24,896]{1,0:T(8,128)(2,1)S(1)}, u32[]{:S(2)}, u32[]{:S(2)}) collective-permute-start(bf16[24,896]{1,0:T(8,128)(2,1)S(1)} %pad_bitcast_fusion.half), channel_id=1, source_target_pairs={{0,6},{2,4},{4,2},{6,0},{8,14},{10,12},{12,10},{14,8},{16,22},{18,... | collective-permute-start | bytes 129032 | tf_op jit(solution)/shard_map/ppermute | solution.py:661
  11.5 5.5 %collective-permute-start.10 = (bf16[48,896]{1,0:T(8,128)(2,1)S(1)}, bf16[48,896]{1,0:T(8,128)(2,1)S(1)}, u32[]{:S(2)}, u32[]{:S(2)}) collective-permute-start(bf16[48,896]{1,0:T(8,128)(2,1)S(1)} %bitcast.11), channel_id=1, source_target_pairs={{0,2},{1,5},{2,0},{3,7},{4,6},{5,1},{6,4},{7,3},{8,10},{9,13},{10,... | collective-permute-start | bytes 258056 | tf_op jit(solution)/shard_map/ppermute | solution.py:666
  12.4 7.2 %collective-permute-start.3 = (bf16[288,256]{1,0:T(8,128)(2,1)S(1)}, bf16[288,256]{1,0:T(8,128)(2,1)S(1)}, u32[]{:S(2)}, u32[]{:S(2)}) collective-permute-start(bf16[288,256]{1,0:T(8,128)(2,1)S(1)} %get-tuple-element.36), channel_id=1, source_target_pairs={{0,2},{2,0},{4,6},{6,4},{8,10},{10,8},{12,14},{14,12},{16,18},{18,... | collective-permute-start | bytes 442376 | tf_op jit(solution)/shard_map/ppermute | solution.py:661
  13.9 8.1 %collective-permute-start.4 = (bf16[288,256]{1,0:T(8,128)(2,1)S(1)}, bf16[288,256]{1,0:T(8,128)(2,1)S(1)}, u32[]{:S(2)}, u32[]{:S(2)}) collective-permute-start(bf16[288,256]{1,0:T(8,128)(2,1)S(1)} %get-tuple-element.37), channel_id=1, source_target_pairs={{0,4},{2,6},{4,0},{6,2},{8,12},{10,14},{12,8},{14,10},{16,20},{18,... | collective-permute-start | bytes 442376 | tf_op jit(solution)/shard_map/ppermute | solution.py:661
  14.6 7.4 %collective-permute-start.5 = (bf16[288,256]{1,0:T(8,128)(2,1)S(1)}, bf16[288,256]{1,0:T(8,128)(2,1)S(1)}, u32[]{:S(2)}, u32[]{:S(2)}) collective-permute-start(bf16[288,256]{1,0:T(8,128)(2,1)S(1)} %get-tuple-element.38), channel_id=1, source_target_pairs={{0,6},{2,4},{4,2},{6,0},{8,14},{10,12},{12,10},{14,8},{16,22},{18,... | collective-permute-start | bytes 442376 | tf_op jit(solution)/shard_map/ppermute | solution.py:661
  17.0 10.9 %collective-permute-start.12 = (bf16[72,896]{1,0:T(8,128)(2,1)S(1)}, bf16[72,896]{1,0:T(8,128)(2,1)S(1)}, u32[]{:S(2)}, u32[]{:S(2)}) collective-permute-start(bf16[72,896]{1,0:T(8,128)(2,1)S(1)} %regroup.1.refs_0_), channel_id=1, source_target_pairs={{0,8},{2,10},{4,12},{6,14},{8,16},{10,18},{12,20},{14,22},{16,24},... | collective-permute-start | bytes 387080 | tf_op jit(solution)/shard_map/ppermute | solution.py:657
  17.8 11.6 %collective-permute-start.13 = (bf16[72,896]{1,0:T(8,128)(2,1)S(1)}, bf16[72,896]{1,0:T(8,128)(2,1)S(1)}, u32[]{:S(2)}, u32[]{:S(2)}) collective-permute-start(bf16[72,896]{1,0:T(8,128)(2,1)S(1)} %regroup.1.refs_0_), channel_id=1, source_target_pairs={{0,16},{2,18},{4,20},{6,22},{8,24},{10,26},{12,28},{14,30},{16,0},... | collective-permute-start | bytes 387080 | tf_op jit(solution)/shard_map/ppermute | solution.py:657
  19.6 9.8 %collective-permute-start.14 = (bf16[72,896]{1,0:T(8,128)(2,1)S(1)}, bf16[72,896]{1,0:T(8,128)(2,1)S(1)}, u32[]{:S(2)}, u32[]{:S(2)}) collective-permute-start(bf16[72,896]{1,0:T(8,128)(2,1)S(1)} %regroup.1.refs_0_), channel_id=1, source_target_pairs={{0,24},{2,26},{4,28},{6,30},{8,0},{10,2},{12,4},{14,6},{16,8},{18,... | collective-permute-start | bytes 387080 | tf_op jit(solution)/shard_map/ppermute | solution.py:657
  25.4 6.0 %collective-permute-start.6 = (bf16[96,256]{1,0:T(8,128)(2,1)S(1)}, bf16[96,256]{1,0:T(8,128)(2,1)S(1)}, u32[]{:S(2)}, u32[]{:S(2)}) collective-permute-start(bf16[96,256]{1,0:T(8,128)(2,1)S(1)} %get-tuple-element.40), channel_id=1, source_target_pairs={{0,8},{2,10},{4,12},{6,14},{8,16},{10,18},{12,20},{14,22},{16,24},... | collective-permute-start | bytes 147464 | tf_op jit(solution)/shard_map/ppermute | solution.py:657
  26.1 6.7 %collective-permute-start.7 = (bf16[96,256]{1,0:T(8,128)(2,1)S(1)}, bf16[96,256]{1,0:T(8,128)(2,1)S(1)}, u32[]{:S(2)}, u32[]{:S(2)}) collective-permute-start(bf16[96,256]{1,0:T(8,128)(2,1)S(1)} %get-tuple-element.41), channel_id=1, source_target_pairs={{0,16},{2,18},{4,20},{6,22},{8,24},{10,26},{12,28},{14,30},{16,0},... | collective-permute-start | bytes 147464 | tf_op jit(solution)/shard_map/ppermute | solution.py:657
  28.0 4.8 %collective-permute-start.8 = (bf16[96,256]{1,0:T(8,128)(2,1)S(1)}, bf16[96,256]{1,0:T(8,128)(2,1)S(1)}, u32[]{:S(2)}, u32[]{:S(2)}) collective-permute-start(bf16[96,256]{1,0:T(8,128)(2,1)S(1)} %get-tuple-element.42), channel_id=1, source_target_pairs={{0,24},{2,26},{4,28},{6,30},{8,0},{10,2},{12,4},{14,6},{16,8},{18,... | collective-permute-start | bytes 147464 | tf_op jit(solution)/shard_map/ppermute | solution.py:657
  30.3 2.6 %collective-permute-start.15 = (bf16[288,896]{1,0:T(8,128)(2,1)S(1)}, bf16[288,896]{1,0:T(8,128)(2,1)S(1)}, u32[]{:S(2)}, u32[]{:S(2)}) collective-permute-start(bf16[288,896]{1,0:T(8,128)(2,1)S(1)} %get-tuple-element.47.own), channel_id=1, source_target_pairs={{0,1},{1,0},{2,3},{3,2},{4,5},{5,4},{6,7},{7,6},{8,9},{9,8},{10,11... | collective-permute-start | bytes 1548296 | tf_op jit(solution)/shard_map/ppermute | solution.py:670
  32.8 1.5 %collective-permute-start.9 = (bf16[384,256]{1,0:T(8,128)(2,1)S(1)}, bf16[384,256]{1,0:T(8,128)(2,1)S(1)}, u32[]{:S(2)}, u32[]{:S(2)}) collective-permute-start(bf16[384,256]{1,0:T(8,128)(2,1)S(1)} %stack.1.own), channel_id=1, source_target_pairs={{0,1},{1,0},{2,3},{3,2},{4,5},{5,4},{6,7},{7,6},{8,9},{9,8},{10,11... | collective-permute-start | bytes 589832 | tf_op jit(solution)/shard_map/ppermute | solution.py:670

commit v8 on v7

--- a/solution.py
+++ b/solution.py
@@ -265,7 +265,7 @@
 
 
 def join_kernel(*refs):
-    pieces, outs, (pf, bf, tab) = refs[:LINE], refs[LINE : LINE + PLANE], refs[LINE + PLANE :]
+    pieces, outs, (pf, bf, tab) = dict(zip((0, 1, 3, 2), refs[:LINE])), refs[LINE : LINE + PLANE], refs[LINE + PLANE :]
     _, q, _ = place()
     lane = iota((8, 256), 1)
     for k in range(LINE):
@@ -303,7 +303,7 @@
         compiler_params=pltpu.CompilerParams(vmem_limit_bytes=32 << 20),
         cost_estimate=cost(5),
         name="join",
-    )(*pieces)
+    )(*(pieces[k] for k in (0, 1, 3, 2)))
 
 
 def mid_kernel(fills, w1, gain_ref, *refs):

time: 37.8 us -> 37.7 us (level)
  waiting for transfers between devices: 5.16 us -> 3.94 us
  starting transfers between devices: 21.3 us -> 22.4 us
    ppermute x9, starting transfers between devices: 14.5 us -> 15.5 us  [along_z(): lax.ppermute(value, 'grp', [(g, (g + PLANE * step) % (LINE * PLANE)) for...]
    ppermute x1, waiting for transfers between devices: 1.05 us -> 0.36 us  [near_chip(): return lax.ppermute(value, ('grp', 'row'), pairs)]
    ppermute x4, waiting for transfers between devices: 1.45 us -> 0.98 us  [in_plane(): lax.ppermute(value, 'grp', [(g, g ^ flip) for g in range(LINE * PLANE)])]
  transfers between devices with their start and end apart: 16 -> 16, of which waited for: 6 -> 7; matrix products, arithmetic and copies ran while one was open for 1% -> 1% of each run, Pallas kernels for 16% -> 16%
where the time goes in v8:
time: 37.7 us; the launch traced here: 37.5 us
  starting transfers between devices  22.4 us (59%)
  Pallas kernels  10.8 us (29%)
  waiting for transfers between devices  3.94 us (10%)
    ppermute x9, starting transfers between devices, along_z(): lax.ppermute(value, 'grp', [(g, (g + PLANE * step) % (LINE * PLANE)) for...  15.5 us
    ppermute x4, starting transfers between devices, in_plane(): lax.ppermute(value, 'grp', [(g, g ^ flip) for g in range(LINE * PLANE)])  6.07 us
    pallas_call x1, Pallas kernels, mid(): pl.pallas_call(mid_kernel, out_shape=[out] * LINE, in_specs=[VMEM()] * (P...  3.39 us
    pallas_call x1, Pallas kernels, finish(): pl.pallas_call(out_kernel, out_shape=jax.ShapeDtypeStruct((1, FMAX, 4 * R...  3.35 us
    ppermute x9, waiting for transfers between devices, along_z(): lax.ppermute(value, 'grp', [(g, (g + PLANE * step) % (LINE * PLANE)) for...  2.35 us
    pallas_call x1, Pallas kernels, pack(): pl.pallas_call(pack_kernel, out_shape=[piece] * LINE + [jax.ShapeDtypeStr...  1.6 us
    pallas_call x1, Pallas kernels, wide(): pl.pallas_call(wide_kernel, out_shape=jax.ShapeDtypeStruct((3 * C2, 1152)...  1.17 us
    ppermute x4, waiting for transfers between devices, in_plane(): lax.ppermute(value, 'grp', [(g, g ^ flip) for g in range(LINE * PLANE)])  0.98 us
  transfers between devices with their start and end apart: 16, of which 7 were waited for; matrix products, arithmetic and copies ran while one was open for 1% of the time, Pallas kernels for 16%

profile of v8, /device:TPU:0, one launch (start us, length us, event | category | flops | bytes accessed | tf_op | source)
XLA Modules:
  0.0 37.5 jit_solution(6037015850307446840)
XLA Ops:
  0.0 0.0 copy-start
  0.0 0.0 copy-start.1
  0.0 1.6 %pack.1 = (bf16[80,256]{1,0:T(8,128)(2,1)S(1)}, bf16[80,256]{1,0:T(8,128)(2,1)S(1)}, bf16[80,256]{1,0:T(8,128)(2,1)S(1)}, bf16[80,256]{1,0:T(8,128)(2,1)S(1)}, b...) custom-call(s32[16]{0:T(128)} %offsets_hbm.1, s32[16]{0:T(128)} %assign_hbm.3, bf16[27,24,192]{2,1,0:T(8,128)(2,1)} %bitcast.14, ...), custom_call_target="tpu_custom_call" | custom-call | flops 2300000000 | tf_op jit(solution)/shard_map/pack/pallas_call | solution.py:243
  1.6 3.1 %collective-permute-start = (bf16[80,256]{1,0:T(8,128)(2,1)S(1)}, bf16[80,256]{1,0:T(8,128)(2,1)S(1)}, u32[]{:S(2)}, u32[]{:S(2)}) collective-permute-start(bf16[80,256]{1,0:T(8,128)(2,1)S(1)} %get-tuple-element.32), channel_id=1, source_target_pairs={{0,8},{2,10},{4,12},{6,14},{8,16},{10,18},{12,20},{14,22},{16,24},... | collective-permute-start | bytes 122888 | tf_op jit(solution)/shard_map/ppermute | solution.py:657
  4.7 2.1 %collective-permute-start.1 = (bf16[80,256]{1,0:T(8,128)(2,1)S(1)}, bf16[80,256]{1,0:T(8,128)(2,1)S(1)}, u32[]{:S(2)}, u32[]{:S(2)}) collective-permute-start(bf16[80,256]{1,0:T(8,128)(2,1)S(1)} %get-tuple-element.33), channel_id=1, source_target_pairs={{0,24},{2,26},{4,28},{6,30},{8,0},{10,2},{12,4},{14,6},{16,8},{18,... | collective-permute-start | bytes 122888 | tf_op jit(solution)/shard_map/ppermute | solution.py:657
  6.8 0.9 %collective-permute-start.2 = (bf16[80,256]{1,0:T(8,128)(2,1)S(1)}, bf16[80,256]{1,0:T(8,128)(2,1)S(1)}, u32[]{:S(2)}, u32[]{:S(2)}) collective-permute-start(bf16[80,256]{1,0:T(8,128)(2,1)S(1)} %get-tuple-element.34), channel_id=1, source_target_pairs={{0,16},{2,18},{4,20},{6,22},{8,24},{10,26},{12,28},{14,30},{16,0},... | collective-permute-start | bytes 122888 | tf_op jit(solution)/shard_map/ppermute | solution.py:657
  7.7 0.0 copy-done
  7.7 0.1 reshape.16
  7.8 0.1 reshape.17
  8.0 2.5 %collective-permute-start.11 = (bf16[24,896]{1,0:T(8,128)(2,1)S(1)}, bf16[24,896]{1,0:T(8,128)(2,1)S(1)}, u32[]{:S(2)}, u32[]{:S(2)}) collective-permute-start(bf16[24,896]{1,0:T(8,128)(2,1)S(1)} %pad_bitcast_fusion.half), channel_id=1, source_target_pairs={{0,6},{2,4},{4,2},{6,0},{8,14},{10,12},{12,10},{14,8},{16,22},{18,... | collective-permute-start | bytes 129032 | tf_op jit(solution)/shard_map/ppermute | solution.py:661
  10.6 0.6 %collective-permute-start.10 = (bf16[48,896]{1,0:T(8,128)(2,1)S(1)}, bf16[48,896]{1,0:T(8,128)(2,1)S(1)}, u32[]{:S(2)}, u32[]{:S(2)}) collective-permute-start(bf16[48,896]{1,0:T(8,128)(2,1)S(1)} %bitcast.11), channel_id=1, source_target_pairs={{0,2},{1,5},{2,0},{3,7},{4,6},{5,1},{6,4},{7,3},{8,10},{9,13},{10,... | collective-permute-start | bytes 258056 | tf_op jit(solution)/shard_map/ppermute | solution.py:666
  11.2 0.0 copy-done.1
  11.2 0.0 collective-permute-done.refs_1_
  11.2 0.0 collective-permute-done.1.refs_2_
  11.2 0.5 %collective-permute-done.2.refs_3_ = bf16[80,256]{1,0:T(8,128)(2,1)S(1)} collective-permute-done((bf16[80,256]{1,0:T(8,128)(2,1)S(1)}, bf16[80,256]{1,0:T(8,128)(2,1)S(1)}, u32[]{:S(2)}, u32[]{:S(2)}) %collective-permute-start.2) | collective-permute-done | bytes 40992 | tf_op jit(solution)/shard_map/ppermute | solution.py:657
  11.7 0.3 join.1
  12.0 1.7 %collective-permute-start.3 = (bf16[288,256]{1,0:T(8,128)(2,1)S(1)}, bf16[288,256]{1,0:T(8,128)(2,1)S(1)}, u32[]{:S(2)}, u32[]{:S(2)}) collective-permute-start(bf16[288,256]{1,0:T(8,128)(2,1)S(1)} %get-tuple-element.36), channel_id=1, source_target_pairs={{0,2},{2,0},{4,6},{6,4},{8,10},{10,8},{12,14},{14,12},{16,18},{18,... | collective-permute-start | bytes 442376 | tf_op jit(solution)/shard_map/ppermute | solution.py:661
  13.7 1.5 %collective-permute-start.4 = (bf16[288,256]{1,0:T(8,128)(2,1)S(1)}, bf16[288,256]{1,0:T(8,128)(2,1)S(1)}, u32[]{:S(2)}, u32[]{:S(2)}) collective-permute-start(bf16[288,256]{1,0:T(8,128)(2,1)S(1)} %get-tuple-element.37), channel_id=1, source_target_pairs={{0,4},{2,6},{4,0},{6,2},{8,12},{10,14},{12,8},{14,10},{16,20},{18,... | collective-permute-start | bytes 442376 | tf_op jit(solution)/shard_map/ppermute | solution.py:661
  15.2 0.3 collective-permute-start.5
  15.5 0.0 collective-permute-done.11.far
  15.5 0.4 collective-permute-done.10.near
  15.9 1.8 %collective-permute-start.12 = (bf16[72,896]{1,0:T(8,128)(2,1)S(1)}, bf16[72,896]{1,0:T(8,128)(2,1)S(1)}, u32[]{:S(2)}, u32[]{:S(2)}) collective-permute-start(bf16[72,896]{1,0:T(8,128)(2,1)S(1)} %regroup.1.refs_0_), channel_id=1, source_target_pairs={{0,8},{2,10},{4,12},{6,14},{8,16},{10,18},{12,20},{14,22},{16,24},... | collective-permute-start | bytes 387080 | tf_op jit(solution)/shard_map/ppermute | solution.py:657
  17.8 0.7 %collective-permute-start.13 = (bf16[72,896]{1,0:T(8,128)(2,1)S(1)}, bf16[72,896]{1,0:T(8,128)(2,1)S(1)}, u32[]{:S(2)}, u32[]{:S(2)}) collective-permute-start(bf16[72,896]{1,0:T(8,128)(2,1)S(1)} %regroup.1.refs_0_), channel_id=1, source_target_pairs={{0,16},{2,18},{4,20},{6,22},{8,24},{10,26},{12,28},{14,30},{16,0},... | collective-permute-start | bytes 387080 | tf_op jit(solution)/shard_map/ppermute | solution.py:657
  18.5 0.5 %collective-permute-done.3.refs_1_ = bf16[288,256]{1,0:T(8,128)(2,1)S(1)} collective-permute-done((bf16[288,256]{1,0:T(8,128)(2,1)S(1)}, bf16[288,256]{1,0:T(8,128)(2,1)S(1)}, u32[]{:S(2)}, u32[]{:S(2)}) %collective-permute-start.3) | collective-permute-done | bytes 147488 | tf_op jit(solution)/shard_map/ppermute | solution.py:661
  19.0 2.2 %collective-permute-start.14 = (bf16[72,896]{1,0:T(8,128)(2,1)S(1)}, bf16[72,896]{1,0:T(8,128)(2,1)S(1)}, u32[]{:S(2)}, u32[]{:S(2)}) collective-permute-start(bf16[72,896]{1,0:T(8,128)(2,1)S(1)} %regroup.1.refs_0_), channel_id=1, source_target_pairs={{0,24},{2,26},{4,28},{6,30},{8,0},{10,2},{12,4},{14,6},{16,8},{18,... | collective-permute-start | bytes 387080 | tf_op jit(solution)/shard_map/ppermute | solution.py:657
  21.3 0.4 %collective-permute-done.4.refs_2_ = bf16[288,256]{1,0:T(8,128)(2,1)S(1)} collective-permute-done((bf16[288,256]{1,0:T(8,128)(2,1)S(1)}, bf16[288,256]{1,0:T(8,128)(2,1)S(1)}, u32[]{:S(2)}, u32[]{:S(2)}) %collective-permute-start.4) | collective-permute-done | bytes 147488 | tf_op jit(solution)/shard_map/ppermute | solution.py:661
  21.7 0.0 collective-permute-done.5.refs_3_
  21.7 3.4 %mid.1 = (bf16[96,256]{1,0:T(8,128)(2,1)S(1)}, bf16[96,256]{1,0:T(8,128)(2,1)S(1)}, bf16[96,256]{1,0:T(8,128)(2,1)S(1)}, bf16[96,256]{1,0:T(8,128)(2,1)S(1)}) custom-call(f32[4,128]{1,0:T(4,128)S(1)} %get-tuple-element.29.fills, bf16[512,384]{1,0:T(8,128)(2,1)S(1)} %get-tuple-element.30.w1, f32[1,384]{1,0:T(1,128)S(1)} %broadcast_in_dim.9.gain_ref, ...), custom_call_target="tpu_custom_call" | custom-call | flops 5750000128 | tf_op jit(solution)/shard_map/mid/pallas_call | solution.py:399
  25.1 1.0 %collective-permute-start.6 = (bf16[96,256]{1,0:T(8,128)(2,1)S(1)}, bf16[96,256]{1,0:T(8,128)(2,1)S(1)}, u32[]{:S(2)}, u32[]{:S(2)}) collective-permute-start(bf16[96,256]{1,0:T(8,128)(2,1)S(1)} %get-tuple-element.40), channel_id=1, source_target_pairs={{0,8},{2,10},{4,12},{6,14},{8,16},{10,18},{12,20},{14,22},{16,24},... | collective-permute-start | bytes 147464 | tf_op jit(solution)/shard_map/ppermute | solution.py:657
  26.1 1.9 %collective-permute-start.7 = (bf16[96,256]{1,0:T(8,128)(2,1)S(1)}, bf16[96,256]{1,0:T(8,128)(2,1)S(1)}, u32[]{:S(2)}, u32[]{:S(2)}) collective-permute-start(bf16[96,256]{1,0:T(8,128)(2,1)S(1)} %get-tuple-element.41), channel_id=1, source_target_pairs={{0,16},{2,18},{4,20},{6,22},{8,24},{10,26},{12,28},{14,30},{16,0},... | collective-permute-start | bytes 147464 | tf_op jit(solution)/shard_map/ppermute | solution.py:657
  28.0 0.0 collective-permute-done.12.refs_1_
  28.0 1.7 %collective-permute-start.8 = (bf16[96,256]{1,0:T(8,128)(2,1)S(1)}, bf16[96,256]{1,0:T(8,128)(2,1)S(1)}, u32[]{:S(2)}, u32[]{:S(2)}) collective-permute-start(bf16[96,256]{1,0:T(8,128)(2,1)S(1)} %get-tuple-element.42), channel_id=1, source_target_pairs={{0,24},{2,26},{4,28},{6,30},{8,0},{10,2},{12,4},{14,6},{16,8},{18,... | collective-permute-start | bytes 147464 | tf_op jit(solution)/shard_map/ppermute | solution.py:657
  29.8 0.0 collective-permute-done.13.refs_2_
  29.8 0.0 collective-permute-done.14.refs_3_
  29.8 1.0 %prep.1 = (bf16[288,896]{1,0:T(8,128)(2,1)S(1)}, bf16[192,192]{1,0:T(8,128)(2,1)S(1)}, bf16[3,256,256]{2,1,0:T(8,128)(2,1)S(1)}, f32[192,128]{1,0:T(8,128)S(1)},...) custom-call(s32[16]{0:T(128)} %frames_hbm.3, s32[16]{0:T(128)} %assign_hbm.3, f32[1,192]{1,0:T(1,128)} %bitcast.12, ...), custom_call_target="tpu_custom_call" | custom-call | flops 11500000 | tf_op jit(solution)/shard_map/prep/pallas_call | solution.py:474
  30.7 0.1 collective-permute-start.15
  30.8 0.3 collective-permute-done.6.refs_1_
  31.1 1.5 %collective-permute-done.7.refs_2_ = bf16[96,256]{1,0:T(8,128)(2,1)S(1)} collective-permute-done((bf16[96,256]{1,0:T(8,128)(2,1)S(1)}, bf16[96,256]{1,0:T(8,128)(2,1)S(1)}, u32[]{:S(2)}, u32[]{:S(2)}) %collective-permute-start.7) | collective-permute-done | bytes 49184 | tf_op jit(solution)/shard_map/ppermute | solution.py:657
  32.7 0.0 collective-permute-done.8.refs_3_
  32.7 0.1 collective-permute-start.9
  32.8 0.0 collective-permute-done.15.other
  32.8 1.2 %wide.1.w_all = bf16[576,1152]{1,0:T(8,128)(2,1)S(1)} custom-call(bf16[288,896]{1,0:T(8,128)(2,1)S(1)} %get-tuple-element.47.own, bf16[288,896]{1,0:T(8,128)(2,1)S(1)} %collective-permute-done.15.other, bf16[192,192]{1,0:T(8,128)(2,1)S(1)} %get-tuple-element.48.order), custom_call_target="tpu_custom_call" | custom-call | flops 11500000 | tf_op jit(solution)/shard_map/wide/pallas_call | solution.py:516
  33.9 0.2 collective-permute-done.9.other
  34.2 3.4 %finish.1 = bf16[1,4,8,6144]{3,2,1,0:T(8,128)(2,1)} custom-call(bf16[384,256]{1,0:T(8,128)(2,1)S(1)} %stack.1.own, bf16[384,256]{1,0:T(8,128)(2,1)S(1)} %collective-permute-done.9.other, bf16[576,1152]{1,0:T(8,128)(2,1)S(1)} %wide.1.w_all, bf16[3,256,256]{2,1,0:T(8,128)(2,1)S(1)} %get-tuple-element.49.pick, f32[192,128]{1,0:T(8,128)S(1)} %get-tuple-element.50.gmid_ref, ...), custom_call_target="tpu_custom_call" | custom-call | flops 5520000000 | tf_op jit(solution)/shard_map/finish/pallas_call | solution.py:638
  (7 shorter events, 0.2 us)
Async XLA Ops:
  0.0 7.7 %copy-start = (bf16[12,27,96]{2,1,0:T(8,128)(2,1)S(1)}, bf16[12,27,96]{2,1,0:T(8,128)(2,1)}, u32[]{:S(2)}) copy-start(bf16[12,27,96]{2,1,0:T(8,128)(2,1)} %param.16) | copy-start | bytes 186628
  0.0 11.2 %copy-start.1 = (f32[384]{0:T(512)S(1)}, f32[384]{0:T(512)}, u32[]{:S(2)}) copy-start(f32[384]{0:T(512)} %param.17) | copy-start | bytes 4612
  1.6 9.6 %collective-permute-start = (bf16[80,256]{1,0:T(8,128)(2,1)S(1)}, bf16[80,256]{1,0:T(8,128)(2,1)S(1)}, u32[]{:S(2)}, u32[]{:S(2)}) collective-permute-start(bf16[80,256]{1,0:T(8,128)(2,1)S(1)} %get-tuple-element.32), channel_id=1, source_target_pairs={{0,8},{2,10},{4,12},{6,14},{8,16},{10,18},{12,20},{14,22},{16,24},... | collective-permute-start | bytes 122888 | tf_op jit(solution)/shard_map/ppermute | solution.py:657
  4.7 6.5 %collective-permute-start.1 = (bf16[80,256]{1,0:T(8,128)(2,1)S(1)}, bf16[80,256]{1,0:T(8,128)(2,1)S(1)}, u32[]{:S(2)}, u32[]{:S(2)}) collective-permute-start(bf16[80,256]{1,0:T(8,128)(2,1)S(1)} %get-tuple-element.33), channel_id=1, source_target_pairs={{0,24},{2,26},{4,28},{6,30},{8,0},{10,2},{12,4},{14,6},{16,8},{18,... | collective-permute-start | bytes 122888 | tf_op jit(solution)/shard_map/ppermute | solution.py:657
  6.8 4.9 %collective-permute-start.2 = (bf16[80,256]{1,0:T(8,128)(2,1)S(1)}, bf16[80,256]{1,0:T(8,128)(2,1)S(1)}, u32[]{:S(2)}, u32[]{:S(2)}) collective-permute-start(bf16[80,256]{1,0:T(8,128)(2,1)S(1)} %get-tuple-element.34), channel_id=1, source_target_pairs={{0,16},{2,18},{4,20},{6,22},{8,24},{10,26},{12,28},{14,30},{16,0},... | collective-permute-start | bytes 122888 | tf_op jit(solution)/shard_map/ppermute | solution.py:657
  8.0 7.5 %collective-permute-start.11 = (bf16[24,896]{1,0:T(8,128)(2,1)S(1)}, bf16[24,896]{1,0:T(8,128)(2,1)S(1)}, u32[]{:S(2)}, u32[]{:S(2)}) collective-permute-start(bf16[24,896]{1,0:T(8,128)(2,1)S(1)} %pad_bitcast_fusion.half), channel_id=1, source_target_pairs={{0,6},{2,4},{4,2},{6,0},{8,14},{10,12},{12,10},{14,8},{16,22},{18,... | collective-permute-start | bytes 129032 | tf_op jit(solution)/shard_map/ppermute | solution.py:661
  10.6 5.3 %collective-permute-start.10 = (bf16[48,896]{1,0:T(8,128)(2,1)S(1)}, bf16[48,896]{1,0:T(8,128)(2,1)S(1)}, u32[]{:S(2)}, u32[]{:S(2)}) collective-permute-start(bf16[48,896]{1,0:T(8,128)(2,1)S(1)} %bitcast.11), channel_id=1, source_target_pairs={{0,2},{1,5},{2,0},{3,7},{4,6},{5,1},{6,4},{7,3},{8,10},{9,13},{10,... | collective-permute-start | bytes 258056 | tf_op jit(solution)/shard_map/ppermute | solution.py:666
  12.0 7.0 %collective-permute-start.3 = (bf16[288,256]{1,0:T(8,128)(2,1)S(1)}, bf16[288,256]{1,0:T(8,128)(2,1)S(1)}, u32[]{:S(2)}, u32[]{:S(2)}) collective-permute-start(bf16[288,256]{1,0:T(8,128)(2,1)S(1)} %get-tuple-element.36), channel_id=1, source_target_pairs={{0,2},{2,0},{4,6},{6,4},{8,10},{10,8},{12,14},{14,12},{16,18},{18,... | collective-permute-start | bytes 442376 | tf_op jit(solution)/shard_map/ppermute | solution.py:661
  13.7 8.0 %collective-permute-start.4 = (bf16[288,256]{1,0:T(8,128)(2,1)S(1)}, bf16[288,256]{1,0:T(8,128)(2,1)S(1)}, u32[]{:S(2)}, u32[]{:S(2)}) collective-permute-start(bf16[288,256]{1,0:T(8,128)(2,1)S(1)} %get-tuple-element.37), channel_id=1, source_target_pairs={{0,4},{2,6},{4,0},{6,2},{8,12},{10,14},{12,8},{14,10},{16,20},{18,... | collective-permute-start | bytes 442376 | tf_op jit(solution)/shard_map/ppermute | solution.py:661
  15.2 6.5 %collective-permute-start.5 = (bf16[288,256]{1,0:T(8,128)(2,1)S(1)}, bf16[288,256]{1,0:T(8,128)(2,1)S(1)}, u32[]{:S(2)}, u32[]{:S(2)}) collective-permute-start(bf16[288,256]{1,0:T(8,128)(2,1)S(1)} %get-tuple-element.38), channel_id=1, source_target_pairs={{0,6},{2,4},{4,2},{6,0},{8,14},{10,12},{12,10},{14,8},{16,22},{18,... | collective-permute-start | bytes 442376 | tf_op jit(solution)/shard_map/ppermute | solution.py:661
  15.9 12.1 %collective-permute-start.12 = (bf16[72,896]{1,0:T(8,128)(2,1)S(1)}, bf16[72,896]{1,0:T(8,128)(2,1)S(1)}, u32[]{:S(2)}, u32[]{:S(2)}) collective-permute-start(bf16[72,896]{1,0:T(8,128)(2,1)S(1)} %regroup.1.refs_0_), channel_id=1, source_target_pairs={{0,8},{2,10},{4,12},{6,14},{8,16},{10,18},{12,20},{14,22},{16,24},... | collective-permute-start | bytes 387080 | tf_op jit(solution)/shard_map/ppermute | solution.py:657
  17.8 12.0 %collective-permute-start.13 = (bf16[72,896]{1,0:T(8,128)(2,1)S(1)}, bf16[72,896]{1,0:T(8,128)(2,1)S(1)}, u32[]{:S(2)}, u32[]{:S(2)}) collective-permute-start(bf16[72,896]{1,0:T(8,128)(2,1)S(1)} %regroup.1.refs_0_), channel_id=1, source_target_pairs={{0,16},{2,18},{4,20},{6,22},{8,24},{10,26},{12,28},{14,30},{16,0},... | collective-permute-start | bytes 387080 | tf_op jit(solution)/shard_map/ppermute | solution.py:657
  19.0 10.7 %collective-permute-start.14 = (bf16[72,896]{1,0:T(8,128)(2,1)S(1)}, bf16[72,896]{1,0:T(8,128)(2,1)S(1)}, u32[]{:S(2)}, u32[]{:S(2)}) collective-permute-start(bf16[72,896]{1,0:T(8,128)(2,1)S(1)} %regroup.1.refs_0_), channel_id=1, source_target_pairs={{0,24},{2,26},{4,28},{6,30},{8,0},{10,2},{12,4},{14,6},{16,8},{18,... | collective-permute-start | bytes 387080 | tf_op jit(solution)/shard_map/ppermute | solution.py:657
  25.1 6.0 %collective-permute-start.6 = (bf16[96,256]{1,0:T(8,128)(2,1)S(1)}, bf16[96,256]{1,0:T(8,128)(2,1)S(1)}, u32[]{:S(2)}, u32[]{:S(2)}) collective-permute-start(bf16[96,256]{1,0:T(8,128)(2,1)S(1)} %get-tuple-element.40), channel_id=1, source_target_pairs={{0,8},{2,10},{4,12},{6,14},{8,16},{10,18},{12,20},{14,22},{16,24},... | collective-permute-start | bytes 147464 | tf_op jit(solution)/shard_map/ppermute | solution.py:657
  26.1 6.5 %collective-permute-start.7 = (bf16[96,256]{1,0:T(8,128)(2,1)S(1)}, bf16[96,256]{1,0:T(8,128)(2,1)S(1)}, u32[]{:S(2)}, u32[]{:S(2)}) collective-permute-start(bf16[96,256]{1,0:T(8,128)(2,1)S(1)} %get-tuple-element.41), channel_id=1, source_target_pairs={{0,16},{2,18},{4,20},{6,22},{8,24},{10,26},{12,28},{14,30},{16,0},... | collective-permute-start | bytes 147464 | tf_op jit(solution)/shard_map/ppermute | solution.py:657
  28.0 4.6 %collective-permute-start.8 = (bf16[96,256]{1,0:T(8,128)(2,1)S(1)}, bf16[96,256]{1,0:T(8,128)(2,1)S(1)}, u32[]{:S(2)}, u32[]{:S(2)}) collective-permute-start(bf16[96,256]{1,0:T(8,128)(2,1)S(1)} %get-tuple-element.42), channel_id=1, source_target_pairs={{0,24},{2,26},{4,28},{6,30},{8,0},{10,2},{12,4},{14,6},{16,8},{18,... | collective-permute-start | bytes 147464 | tf_op jit(solution)/shard_map/ppermute | solution.py:657
  30.7 2.0 %collective-permute-start.15 = (bf16[288,896]{1,0:T(8,128)(2,1)S(1)}, bf16[288,896]{1,0:T(8,128)(2,1)S(1)}, u32[]{:S(2)}, u32[]{:S(2)}) collective-permute-start(bf16[288,896]{1,0:T(8,128)(2,1)S(1)} %get-tuple-element.47.own), channel_id=1, source_target_pairs={{0,1},{1,0},{2,3},{3,2},{4,5},{5,4},{6,7},{7,6},{8,9},{9,8},{10,11... | collective-permute-start | bytes 1548296 | tf_op jit(solution)/shard_map/ppermute | solution.py:670
  32.7 1.5 %collective-permute-start.9 = (bf16[384,256]{1,0:T(8,128)(2,1)S(1)}, bf16[384,256]{1,0:T(8,128)(2,1)S(1)}, u32[]{:S(2)}, u32[]{:S(2)}) collective-permute-start(bf16[384,256]{1,0:T(8,128)(2,1)S(1)} %stack.1.own), channel_id=1, source_target_pairs={{0,1},{1,0},{2,3},{3,2},{4,5},{5,4},{6,7},{7,6},{8,9},{9,8},{10,11... | collective-permute-start | bytes 589832 | tf_op jit(solution)/shard_map/ppermute | solution.py:670
